TPU v7x, 32 devices: a whole 2x2x4 slice. The times are simulated.
32 devices in a mesh: groups: 2 (over y), tok: 4 (over x, core), hid: 4 (over z).
Axes of the slice: x: 2, y: 2, z: 4, core: 2. Of those that a mesh axis runs over, the one named last changes fastest.
Arguments:
- states: bfloat16 [8192, 5376], P(('groups', 'tok'), 'hid'), parts along dimension 0, may hold values from -6 to 6
- w_qkv: bfloat16 [5376, 8, 512], P('tok', 'hid'), may hold values from -0.078125 to 0.078125
- w_out: bfloat16 [2048, 5376], P('tok', 'hid'), may hold values from -0.125 to 0.125
- q_gain: float32 [128], replicated, may hold values from 0.5 to 14, as said below
- k_gain: float32 [128], replicated, may hold values from 0.5 to 14, as said below
Outputs:
- attended: bfloat16 [8192, 5376], P(('groups', 'tok'), 'hid'), parts along dimension 0
There are 2 independent parts, one for each index of `groups`. A program takes and returns all parts, laid end to end along the dimension named above; an argument that names none is the same for every part. Nothing has to cross between parts.
Inputs may be any that keep to these rules, and one draw needn't show every extreme that they name: `q_gain`: entries are positive. `k_gain`: entries are positive.
All inputs are finite; a program needn't handle non-finite values.
Results may differ from a plain program's by a relative error of at most 0.017.
The roundings to bfloat16 on the way count: a program that leaves them out, or rounds other values in their place, can miss the bound.
Values may be sent and summed in bfloat16 or wider, within the bound.
A program may use at most 128 MiB of HBM per device.

v0:
```python
import math

import jax
import jax.numpy as jnp
from jax import lax
from jax.sharding import PartitionSpec as P

HD = 128
GROUP = 2
WINDOW = 1024


EPS = 1e-06
SCALE = 168.0 ** (-0.5)
ROPE_BASE = 10000.0


def from_behind(value, axis, steps):
    count = lax.axis_size(axis)
    first, last = (max(0, -steps), min(count, count - steps))
    return lax.ppermute(value, axis, [(source, source + steps) for source in range(first, last)])


def head_norm(values, gain):
    meansq = jnp.mean(values * values, axis=-1, keepdims=True)
    return values * lax.rsqrt(meansq + EPS) * gain


def rotate(values, pos):
    half = values.shape[-1] // 2
    inverse = jnp.exp(
        jnp.arange(half, dtype=jnp.float32) * (-2.0 * math.log(ROPE_BASE) / values.shape[-1])
    )
    angle = pos.astype(jnp.float32)[:, None] * inverse[None, :]
    shape = (angle.shape[0],) + (1,) * (values.ndim - 2) + (half,)
    cosine = jnp.cos(angle).reshape(shape)
    sine = jnp.sin(angle).reshape(shape)
    first = values[..., :half]
    second = values[..., half:]
    return jnp.concatenate(
        [first * cosine - second * sine, second * cosine + first * sine], axis=-1
    )


def attend(query, keys, values, q_first, k_first):
    scores = jnp.einsum("qhgd,khd->hgqk", query, keys, preferred_element_type=jnp.float32) * SCALE
    q_index = q_first + jnp.arange(query.shape[0], dtype=jnp.int32)
    k_index = k_first + jnp.arange(keys.shape[0], dtype=jnp.int32)
    keep = (
        (k_index[None, :] <= q_index[:, None])
        & (q_index[:, None] - k_index[None, :] < WINDOW)
        & (k_index[None, :] >= 0)
    )
    masked = jnp.where(keep, scores, jnp.float32(-1e30))
    top = jnp.max(masked, axis=-1, keepdims=True)
    expo = jnp.where(keep, jnp.exp(masked - top), jnp.float32(0.0))
    total = jnp.sum(expo, axis=-1, keepdims=True)
    weights = (expo / total).astype(jnp.bfloat16)
    result = jnp.einsum("hgqk,khd->qhgd", weights, values, preferred_element_type=jnp.float32)
    return result.astype(jnp.bfloat16)


def on_device(states, w_qkv, w_out, q_gain, k_gain):
    rows = states.shape[0]
    kv_local = w_qkv.shape[1]
    columns = kv_local * (GROUP + 2) * HD
    weight_whole = lax.all_gather(w_qkv, "tok", axis=0, tiled=True).reshape(-1, columns)
    weight_part = weight_whole
    qkv = jnp.dot(
        lax.all_gather(states, "hid", axis=1, tiled=True),
        weight_part,
        preferred_element_type=jnp.float32,
    )
    qkv = qkv.reshape(rows, kv_local, GROUP + 2, HD)
    base = lax.axis_index("tok") * rows
    pos = base + jnp.arange(rows, dtype=jnp.int32)
    query = rotate(head_norm(qkv[:, :, :GROUP], q_gain), pos).astype(jnp.bfloat16)
    keys = rotate(head_norm(qkv[:, :, GROUP], k_gain), pos).astype(jnp.bfloat16)
    values = qkv[:, :, GROUP + 1].astype(jnp.bfloat16)
    paired = jnp.stack([keys, values], axis=1).reshape(rows, 2 * kv_local * HD)
    hops = max(1, WINDOW // rows)
    reach = min(WINDOW, rows)
    pieces = []
    current = paired
    current = from_behind(current, "tok", 1)
    pieces.insert(0, current)
    combined = jnp.concatenate(pieces + [paired], axis=0).reshape(-1, 2, kv_local, HD)
    reach_back = hops * reach
    block = 512
    outputs = []
    for index in range(rows // block):
        q_block = query[index * block : (index + 1) * block]
        kv_block = combined[index * block : index * block + block + reach_back]
        outputs.append(
            attend(
                q_block,
                kv_block[:, 0],
                kv_block[:, 1],
                base + index * block,
                base + index * block - reach_back,
            )
        )
    heads_out = jnp.concatenate(outputs, axis=0)
    heads_out = heads_out.reshape(rows, kv_local * GROUP * HD)
    out_whole = lax.all_gather(w_out, "tok", axis=0, tiled=True)
    weight_part = out_whole
    summed = jnp.dot(
        lax.all_gather(heads_out, "hid", axis=1, tiled=True),
        weight_part,
        preferred_element_type=jnp.float32,
    )
    return summed.astype(jnp.bfloat16)


def solution(mesh):
    return jax.shard_map(
        on_device,
        mesh=mesh,
        in_specs=(P(("groups", "tok"), "hid"), P("tok", "hid", None), P("tok", "hid"), P(), P()),
        out_specs=P(("groups", "tok"), "hid"),
        check_vma=False,
    )
```

profile of v0, /device:TPU:1, one launch (start us, length us, event | category | flops | bytes accessed | tf_op | source)
XLA Modules:
  0.0 458.3 jit_solution(5258725831197770475)
XLA Ops:
  6.5 0.0 all-gather.7.cloned.1.call-start
  6.5 0.7 all-gather.7.cloned.1.call-update
  7.3 0.0 all-gather.5.cloned.1.call-start
  7.3 0.7 all-gather.5.cloned.1.call-update
  8.0 0.0 all-gather.11.cloned.1.call-start
  8.1 0.7 all-gather.11.cloned.1.call-update
  8.7 0.0 all-gather.9.cloned.1.call-start
  8.9 1.0 multiply_cosine_fusion
  9.9 1.9 fusion.15
  11.8 1.9 fusion.17
  13.7 70.9 %all-gather.7.cloned.1.call-done = bf16[5376,2,512]{2,1,0:T(2,128)(2,1)} async-done(((bf16[1344,2,512]{2,1,0:T(2,128)(2,1)}), bf16[5376,2,512]{2,1,0:T(2,128)(2,1)}) %all-gather.7.cloned.1.call-update) | async-done | bytes 11010064 | tf_op jit(solution)/shard_map/all_gather | solution.py:67
  84.6 27.7 %copy.39 = bf16[5376,2,512]{0,2,1:T(8,128)(2,1)} copy(bf16[5376,2,512]{2,1,0:T(2,128)(2,1)} %all-gather.7.cloned.1.call-done) | data formatting | bytes 22020096 | tf_op jit(solution)/shard_map/reshape | solution.py:67
  112.3 166.2 %all-gather.5.cloned.1.call-done = bf16[1024,5376]{0,1:T(8,128)(2,1)} async-done(((bf16[1024,1344]{0,1:T(8,128)(2,1)}), bf16[1024,5376]{0,1:T(8,128)(2,1)}) %all-gather.5.cloned.1.call-update) | async-done | bytes 11010064 | tf_op jit(solution)/shard_map/all_gather | solution.py:70
  278.5 0.0 copy-start
  278.5 16.0 %fusion.2 = f32[1024,2,4,128]{0,3,2,1:T(8,128)S(1)} fusion(bf16[2,4,128,5376]{3,2,1,0:T(8,128)(2,1)} %bitcast.101, bf16[1024,5376]{0,1:T(8,128)(2,1)} %all-gather.5.cloned.1.call-done), kind=kOutput, calls=%fused_computation.8 | convolution fusion | flops 11274289152 | bytes 26214400 | tf_op jit(solution)/shard_map/dot_general | solution.py:69
  294.5 0.1 multiply_reduce_fusion.1
  294.6 0.1 fusion.30
  294.7 0.0 copy-done
  294.7 0.0 copy-start.1
  294.7 0.2 multiply_multiply_fusion.1
  294.9 0.2 fusion.31
  295.1 0.1 pad_maximum_fusion.1
  295.2 3.6 collective-permute-start
  298.8 0.2 multiply_reduce_fusion
  299.1 0.0 copy-done.1
  299.1 0.4 multiply_multiply_fusion
  299.5 1.4 subtract_convert_fusion
  300.9 26.8 %collective-permute-done = bf16[1024,512]{0,1:T(8,128)(2,1)S(1)} collective-permute-done((bf16[1024,512]{0,1:T(8,128)(2,1)S(1)}, bf16[1024,512]{0,1:T(8,128)(2,1)S(1)}, u32[]{:S(2)}, u32[]{:S(2)}) %collective-permute-start) | collective-permute-done | bytes 1048608 | tf_op jit(solution)/shard_map/ppermute | solution.py:21
  327.7 0.2 fusion.18
  327.9 10.3 %fusion.45 = (f32[2,2,512]{2,1,0:T(2,128)S(1)}, f32[2,2,512,1536]{2,3,1,0:T(8,128)}) fusion(pred[512,1536]{0,1:T(8,128)(4,1)} %fusion.17, bf16[1536,2,2,128]{0,3,2,1:T(8,128)(2,1)S(1)} %bitcast.105, bf16[1024,2,2,64]{0,3,2,1:T(8,128)(2,1)} %get-tuple-element.6, bf16[1024,2,2,64]{0,3,2,1:T(8,128)(2,1)} %get-tuple-element.5), kind=kOutput, calls=%fused_computation.80 | convolution fusion | flops 822085120 | bytes 15998976 | tf_op jit(solution)/shard_map/sub | solution.py:56
  338.3 10.2 %fusion.46 = (f32[2,2,512]{2,1,0:T(2,128)S(1)}, f32[2,2,512,1536]{2,3,1,0:T(8,128)}) fusion(pred[512,1536]{0,1:T(8,128)(4,1)} %fusion.15, bf16[1536,2,2,128]{0,3,2,1:T(8,128)(2,1)S(1)} %bitcast.107, bf16[1024,2,2,64]{0,3,2,1:T(8,128)(2,1)} %get-tuple-element.5, bf16[1024,2,2,64]{0,3,2,1:T(8,128)(2,1)} %get-tuple-element.6), kind=kOutput, calls=%fused_computation.81 | convolution fusion | flops 822085120 | bytes 15998976 | tf_op jit(solution)/shard_map/sub | solution.py:56
  348.5 0.0 copy-start.2
  348.5 5.7 %fusion.25 = bf16[512,2,2,128]{0,3,2,1:T(8,128)(2,1)S(1)} fusion(f32[2,2,512,1536]{2,3,1,0:T(8,128)} %get-tuple-element.16, f32[2,2,512]{2,1,0:T(2,128)S(1)} %get-tuple-element.15, bf16[1536,2,2,128]{0,3,2,1:T(8,128)(2,1)S(1)} %bitcast.108), kind=kOutput, calls=%fused_computation.37 | convolution fusion | flops 811859968 | bytes 13901824 | tf_op jit(solution)/shard_map/hgqk,khd->qhgd/dot_general | solution.py:59
  354.3 2.4 copy-done.2
  356.7 1.0 fusion.26
  357.7 1.1 pad_maximum_fusion.2
  358.8 0.0 all-gather.9.cloned.1.call-update
  358.8 0.0 all-gather.11.cloned.1.call-done
  358.9 82.8 %all-gather.9.cloned.1.call-done = bf16[1024,2048]{0,1:T(8,128)(2,1)} async-done(((bf16[1024,512]{0,1:T(8,128)(2,1)}), bf16[1024,2048]{0,1:T(8,128)(2,1)}) %all-gather.9.cloned.1.call-update) | async-done | bytes 4194320 | tf_op jit(solution)/shard_map/all_gather | solution.py:108
  441.6 10.1 %convolution_convert_fusion = bf16[1024,1344]{0,1:T(8,128)(2,1)} fusion(bf16[2048,1344]{0,1:T(8,128)(2,1)} %all-gather.11.cloned.1.call-done, bf16[1024,2048]{0,1:T(8,128)(2,1)} %all-gather.9.cloned.1.call-done), kind=kOutput, calls=%fused_computation.20 | convolution fusion | flops 5638520832 | bytes 12451840 | tf_op jit(solution)/shard_map/dot_general | solution.py:107
  (10 shorter events, 0.1 us)
Async XLA Ops:
  6.5 78.1 %all-gather.7.cloned.1.call-start = ((), (), s32[]{:S(2)}) async-start(), calls=%async_computation.1 | async-start | bytes 13762560 | tf_op jit(solution)/shard_map/all_gather | solution.py:67
  7.3 271.3 %all-gather.5.cloned.1.call-start = ((), (), s32[]{:S(2)}) async-start(), calls=%async_computation | async-start | bytes 13762560 | tf_op jit(solution)/shard_map/all_gather | solution.py:70
  8.0 350.8 %all-gather.11.cloned.1.call-start = ((), (), s32[]{:S(2)}) async-start(), calls=%async_computation.3 | async-start | bytes 6881280 | tf_op jit(solution)/shard_map/all_gather | solution.py:105
  8.7 432.9 %all-gather.9.cloned.1.call-start = ((), (), s32[]{:S(2)}) async-start(), calls=%async_computation.2 | async-start | bytes 5242880 | tf_op jit(solution)/shard_map/all_gather | solution.py:108
  278.5 16.2 %copy-start = (f32[128]{0:T(128)S(1)}, f32[128]{0:T(128)}, u32[]{:S(2)}) copy-start(f32[128]{0:T(128)} %param.9) | copy-start | bytes 1540
  294.7 4.4 copy-start.1
  295.2 32.5 %collective-permute-start = (bf16[1024,512]{0,1:T(8,128)(2,1)S(1)}, bf16[1024,512]{0,1:T(8,128)(2,1)S(1)}, u32[]{:S(2)}, u32[]{:S(2)}) collective-permute-start(bf16[1024,512]{0,1:T(8,128)(2,1)S(1)} %bitcast.102), channel_id=1, source_target_pairs={{0,4},{4,8},{8,12},{1,5},{5,9},{9,13},{2,6},{6,10},{10,14},{3,7},{... | collective-permute-start | bytes 3145736 | tf_op jit(solution)/shard_map/ppermute | solution.py:21
  348.5 8.2 %copy-start.2 = (f32[2,2,512,1536]{2,3,1,0:T(8,128)S(1)}, f32[2,2,512,1536]{2,3,1,0:T(8,128)}, u32[]{:S(2)}) copy-start(f32[2,2,512,1536]{2,3,1,0:T(8,128)} %get-tuple-element.14) | copy-start | bytes 37748740
Sparse Core Ops, SparseCore 0:
  8.9 75.6 all-gather.6
  86.2 192.2 all-gather.4
  280.1 44.9 all-gather.10
  358.9 82.6 all-gather.8
where the time goes:
time: 460 us; the launch traced here: 458 us
  waiting for transfers between devices  349 us (76%)
  matrix products  53.4 us (12%)
  local copies, waits for them, and re-layouts  30.2 us (7%)
  between operations  13.3 us (3%)
  other arithmetic  8.82 us (2%)
    all_gather x1, waiting for transfers between devices, on_device(): lax.all_gather(states, 'hid', axis=1, tiled=True)  166 us
    all_gather x1, waiting for transfers between devices, on_device(): lax.all_gather(heads_out, 'hid', axis=1, tiled=True)  82.8 us
    all_gather x1, waiting for transfers between devices, on_device(): lax.all_gather(w_qkv, 'tok', axis=0, tiled=True).reshape(-1, columns)  70.9 us
    reshape x1, local copies, waits for them, and re-layouts, on_device(): lax.all_gather(w_qkv, 'tok', axis=0, tiled=True).reshape(-1, columns)  27.7 us
    ppermute x1, waiting for transfers between devices, from_behind(): lax.ppermute(value, axis, [(source, source + steps) for source in range(f...  26.8 us
    sub x2, matrix products, attend(): expo = jnp.where(keep, jnp.exp(masked - top), jnp.float32(0.0))  20.6 us
    dot_general x1, matrix products, on_device(): jnp.dot(lax.all_gather(states, 'hid', axis=1, tiled=True), weight_part, p...  16 us
    dot_general x1, matrix products, on_device(): jnp.dot(lax.all_gather(heads_out, 'hid', axis=1, tiled=True), weight_part...  10.1 us
  transfers between devices with their start and end apart: 5, of which 4 were waited for; matrix products, arithmetic and copies ran while one was open for 17% of the time, Pallas kernels for 0%

commit v1 on v0

--- a/solution.py
+++ b/solution.py
@@ -60,17 +60,41 @@
     return result.astype(jnp.bfloat16)
 
 
+def line_gather_dot(blocks, weight, axis):
+    count = lax.axis_size(axis)
+    here = lax.axis_index(axis)
+    depth = blocks[0].shape[1]
+
+    def term(block, owner):
+        rows = lax.dynamic_slice_in_dim(weight, owner * depth, depth, 0)
+        return jnp.dot(block, rows, preferred_element_type=jnp.float32)
+
+    results = []
+    for block in blocks:
+        up = down = block
+        total = term(block, here)
+        for step in range(1, count):
+            up = lax.ppermute(up, axis, [(i, i + 1) for i in range(step - 1, count - 1)])
+            down = lax.ppermute(down, axis, [(i + 1, i) for i in range(count - step)])
+            below = jnp.maximum(here - step, 0)
+            above = jnp.minimum(here + step, count - 1)
+            if 2 * step < count:
+                total = total + term(up, below) + term(down, above)
+            else:
+                from_below = here >= step
+                total = total + term(
+                    jnp.where(from_below, up, down), jnp.where(from_below, below, above)
+                )
+        results.append(total)
+    return results
+
+
 def on_device(states, w_qkv, w_out, q_gain, k_gain):
     rows = states.shape[0]
     kv_local = w_qkv.shape[1]
     columns = kv_local * (GROUP + 2) * HD
-    weight_whole = lax.all_gather(w_qkv, "tok", axis=0, tiled=True).reshape(-1, columns)
-    weight_part = weight_whole
-    qkv = jnp.dot(
-        lax.all_gather(states, "hid", axis=1, tiled=True),
-        weight_part,
-        preferred_element_type=jnp.float32,
-    )
+    weight_whole = lax.all_gather(w_qkv.reshape(-1, columns), "tok", axis=0, tiled=True)
+    (qkv,) = line_gather_dot([states], weight_whole, "hid")
     qkv = qkv.reshape(rows, kv_local, GROUP + 2, HD)
     base = lax.axis_index("tok") * rows
     pos = base + jnp.arange(rows, dtype=jnp.int32)
@@ -98,18 +122,11 @@
                 kv_block[:, 1],
                 base + index * block,
                 base + index * block - reach_back,
-            )
+            ).reshape(block, kv_local * GROUP * HD)
         )
-    heads_out = jnp.concatenate(outputs, axis=0)
-    heads_out = heads_out.reshape(rows, kv_local * GROUP * HD)
     out_whole = lax.all_gather(w_out, "tok", axis=0, tiled=True)
-    weight_part = out_whole
-    summed = jnp.dot(
-        lax.all_gather(heads_out, "hid", axis=1, tiled=True),
-        weight_part,
-        preferred_element_type=jnp.float32,
-    )
-    return summed.astype(jnp.bfloat16)
+    summed = line_gather_dot(outputs, out_whole, "hid")
+    return jnp.concatenate([part.astype(jnp.bfloat16) for part in summed], axis=0)
 
 
 def solution(mesh):

time: 460 us -> 345 us (0.75)
  waiting for transfers between devices: 349 us -> 186 us
  starting transfers between devices: 3.75 us -> 35.7 us
  matrix products: 53.4 us -> 74.8 us
  local copies, waits for them, and re-layouts: 30.2 us -> 16.6 us
  other arithmetic: 8.82 us -> 13.7 us
    all_gather x3 -> x1, waiting for transfers between devices: 320 us -> 0.02 us  [on_device(): lax.all_gather(w_qkv.reshape(-1, columns), 'tok', axis=0, tiled=True)]
    ppermute x0 -> x18, waiting for transfers between devices: none -> 178 us  [the longest x9 122 us: line_gather_dot(): down = lax.ppermute(down, axis, [(i + 1, i) for i in range(count - step)])]
    ppermute x0 -> x18, starting transfers between devices: none -> 29 us  [the longest x9 16.9 us: line_gather_dot(): lax.ppermute(up, axis, [(i, i + 1) for i in range(step - 1, count - 1)])]
    reshape x1 -> x0, local copies, waits for them, and re-layouts: 27.7 us -> none  [on_device(): lax.all_gather(w_qkv, 'tok', axis=0, tiled=True).reshape(-1, columns)]
    ppermute x1, waiting for transfers between devices: 26.8 us -> 8.02 us  [from_behind(): lax.ppermute(value, axis, [(source, source + steps) for source in range(f...]
    dot_general x2 -> x15, matrix products: 26.1 us -> 42.2 us  [term(): return jnp.dot(block, rows, preferred_element_type=jnp.float32)]
    unnamed x6 -> x26, local copies, waits for them, and re-layouts: 2.43 us -> 11.8 us
    dot_general x2, matrix products: 6.72 us -> 12 us  [attend(): jnp.einsum('hgqk,khd->qhgd', weights, values, preferred_element_type=jnp....]
  transfers between devices with their start and end apart: 5 -> 21, of which waited for: 4 -> 10; matrix products, arithmetic and copies ran while one was open for 17% -> 27% of each run, Pallas kernels for 0% -> 0%
where the time goes in v1:
time: 345 us; the launch traced here: 341 us
  waiting for transfers between devices  186 us (54%)
  matrix products  74.8 us (22%)
  starting transfers between devices  35.7 us (10%)
  local copies, waits for them, and re-layouts  16.6 us (5%)
  between operations  14.3 us (4%)
  other arithmetic  13.7 us (4%)
    ppermute x9, waiting for transfers between devices, line_gather_dot(): down = lax.ppermute(down, axis, [(i + 1, i) for i in range(count - step)])  122 us
    ppermute x9, waiting for transfers between devices, line_gather_dot(): lax.ppermute(up, axis, [(i, i + 1) for i in range(step - 1, count - 1)])  55.5 us
    dot_general x15, matrix products, term(): return jnp.dot(block, rows, preferred_element_type=jnp.float32)  42.2 us
    sub x2, matrix products, attend(): expo = jnp.where(keep, jnp.exp(masked - top), jnp.float32(0.0))  20.6 us
    ppermute x9, starting transfers between devices, line_gather_dot(): lax.ppermute(up, axis, [(i, i + 1) for i in range(step - 1, count - 1)])  16.9 us
    ppermute x9, starting transfers between devices, line_gather_dot(): down = lax.ppermute(down, axis, [(i + 1, i) for i in range(count - step)])  12.1 us
    dot_general x2, matrix products, attend(): jnp.einsum('hgqk,khd->qhgd', weights, values, preferred_element_type=jnp....  12 us
    unnamed x26, local copies, waits for them, and re-layouts  11.8 us
  transfers between devices with their start and end apart: 21, of which 10 were waited for; matrix products, arithmetic and copies ran while one was open for 27% of the time, Pallas kernels for 0%

profile of v1, /device:TPU:1, one launch (start us, length us, event | category | flops | bytes accessed | tf_op | source)
XLA Modules:
  0.0 341.0 jit_solution(5018109188759766012)
XLA Ops:
  6.5 4.0 %copy.40 = bf16[168,8,2,512]{3,1,2,0:T(8,128)(2,1)} copy(bf16[168,8,2,512]{3,2,1,0:T(2,128)(2,1)} %bitcast.112) | data formatting | bytes 5505024
  10.7 1.7 copy-done.7
  12.4 5.5 %collective-permute-start = (bf16[1024,1344]{0,1:T(8,128)(2,1)S(1)}, bf16[1024,1344]{0,1:T(8,128)(2,1)}, u32[]{:S(2)}, u32[]{:S(2)}) collective-permute-start(bf16[1024,1344]{0,1:T(8,128)(2,1)S(1)} %copy-done.7), channel_id=1, source_target_pairs={{0,1},{1,2},{2,3},{4,5},{5,6},{6,7},{8,9},{9,10},{10,11},{12,13},{... | collective-permute-start | bytes 8257544 | tf_op jit(solution)/shard_map/ppermute | solution.py:77
  17.9 1.3 collective-permute-start.1
  19.2 55.5 %collective-permute-done = bf16[1024,1344]{0,1:T(8,128)(2,1)} collective-permute-done((bf16[1024,1344]{0,1:T(8,128)(2,1)S(1)}, bf16[1024,1344]{0,1:T(8,128)(2,1)}, u32[]{:S(2)}, u32[]{:S(2)}) %collective-permute-start) | collective-permute-done | bytes 2752544 | tf_op jit(solution)/shard_map/ppermute | solution.py:77
  74.7 2.2 collective-permute-start.2
  76.9 3.2 collective-permute-done.1
  80.1 1.3 collective-permute-start.3
  81.5 1.0 multiply_cosine_fusion
  82.5 1.0 copy.25
  83.5 1.0 copy.26
  84.5 1.9 fusion.14
  86.5 1.9 fusion.16
  88.4 0.8 collective-permute-start.4
  89.2 52.8 %collective-permute-done.3 = bf16[1024,1344]{0,1:T(8,128)(2,1)} collective-permute-done((bf16[1024,1344]{0,1:T(8,128)(2,1)}, bf16[1024,1344]{0,1:T(8,128)(2,1)}, u32[]{:S(2)}, u32[]{:S(2)}) %collective-permute-start.3) | collective-permute-done | bytes 2752544 | tf_op jit(solution)/shard_map/ppermute | solution.py:78
  142.0 1.8 collective-permute-start.5
  143.9 6.3 %fusion.25 = f32[1024,1024]{1,0:T(8,128)S(1)} fusion(bf16[1024,1344]{0,1:T(8,128)(2,1)} %collective-permute-done.1, bf16[5376,1024]{1,0:T(8,128)(2,1)} %all-gather.3.cloned.1.call-done, s32[]{:T(128)S(6)} %select_n.97), kind=kOutput, calls=%fused_computation.43 | convolution fusion | flops 2818572288 | bytes 9699332 | tf_op jit(solution)/shard_map/dot_general | solution.py:70
  150.2 6.3 %fusion.27 = f32[1024,1024]{1,0:T(8,128)S(1)} fusion(bf16[1024,1344]{0,1:T(8,128)(2,1)} %collective-permute-done, bf16[5376,1024]{1,0:T(8,128)(2,1)} %all-gather.3.cloned.1.call-done, s32[]{:T(128)S(6)} %select_n.96), kind=kOutput, calls=%fused_computation.45 | convolution fusion | flops 2818572288 | bytes 9699332 | tf_op jit(solution)/shard_map/dot_general | solution.py:70
  156.6 3.6 %fusion.29 = f32[1024,1024]{1,0:T(8,128)S(1)} fusion(bf16[1024,1344]{0,1:T(8,128)(2,1)S(1)} %copy-done.8, bf16[5376,1024]{1,0:T(8,128)(2,1)S(1)} %bitcast.118, s32[]{:T(128)S(6)} %select_n.95), kind=kOutput, calls=%fused_computation.47 | convolution fusion | flops 2818572288 | bytes 9699332 | tf_op jit(solution)/shard_map/dot_general | solution.py:70
  160.2 7.1 %fusion.22 = f32[1024,1024]{0,1:T(8,128)} fusion(bf16[5376,1024]{1,0:T(8,128)(2,1)S(1)} %bitcast.118, s32[]{:T(128)S(6)} %select_n.101, bf16[1024,1344]{0,1:T(8,128)(2,1)} %collective-permute-done.2, bf16[1024,1344]{0,1:T(8,128)(2,1)} %collective-permute-done.3, pred[]{:T(512)S(6)} %ge.26), kind=kOutput, calls=%fused_computation.40 | convolution fusion | flops 2819948544 | bytes 12451845 | tf_op jit(solution)/shard_map/dot_general | solution.py:70
  167.3 1.5 copy-done.2
  168.8 34.0 %collective-permute-done.5 = bf16[1024,1344]{0,1:T(8,128)(2,1)} collective-permute-done((bf16[1024,1344]{0,1:T(8,128)(2,1)}, bf16[1024,1344]{0,1:T(8,128)(2,1)}, u32[]{:S(2)}, u32[]{:S(2)}) %collective-permute-start.5) | collective-permute-done | bytes 2752544 | tf_op jit(solution)/shard_map/ppermute | solution.py:78
  202.8 8.3 %fusion.12 = f32[1024,1024]{0,1:T(8,128)S(1)} fusion(f32[1024,1024]{0,1:T(8,128)} %fusion.22, f32[1024,1024]{1,0:T(8,128)S(1)} %fusion.25, f32[1024,1024]{1,0:T(8,128)S(1)} %fusion.29, f32[1024,1024]{1,0:T(8,128)S(1)} %fusion.27, bf16[5376,1024]{1,0:T(8,128)(2,1)} %all-gather.3.cloned.1.call-done, s32[]{:T(128)S(6)} %select_n.105, ...), kind=kOutput, calls=%fused_computation.19 | convolution fusion | flops 2824142848 | bytes 29229060 | tf_op jit(solution)/shard_map/dot_general | solution.py:70
  211.1 1.9 copy-done
  213.0 1.5 slice.77
  214.5 1.9 copy.38
  216.4 1.3 multiply_reduce_fusion.1
  217.8 1.3 fusion.59
  219.1 1.4 multiply_multiply_fusion.1
  220.8 6.6 %collective-permute-start.6 = (bf16[1024,512]{0,1:T(8,128)(2,1)S(1)}, bf16[1024,512]{0,1:T(8,128)(2,1)S(1)}, u32[]{:S(2)}, u32[]{:S(2)}) collective-permute-start(bf16[1024,512]{0,1:T(8,128)(2,1)S(1)} %bitcast.110), channel_id=1, source_target_pairs={{0,4},{4,8},{8,12},{1,5},{5,9},{9,13},{2,6},{6,10},{10,14},{3,7},{... | collective-permute-start | bytes 3145736 | tf_op jit(solution)/shard_map/ppermute | solution.py:21
  228.1 0.9 multiply_multiply_fusion
  229.0 2.1 subtract_convert_fusion
  231.1 8.0 %collective-permute-done.6 = bf16[1024,512]{0,1:T(8,128)(2,1)S(1)} collective-permute-done((bf16[1024,512]{0,1:T(8,128)(2,1)S(1)}, bf16[1024,512]{0,1:T(8,128)(2,1)S(1)}, u32[]{:S(2)}, u32[]{:S(2)}) %collective-permute-start.6) | collective-permute-done | bytes 1048608 | tf_op jit(solution)/shard_map/ppermute | solution.py:21
  239.4 10.3 %fusion.94 = (f32[2,2,512]{2,1,0:T(2,128)S(1)}, f32[2,2,512,1536]{2,3,1,0:T(8,128)}) fusion(pred[512,1536]{0,1:T(8,128)(4,1)} %fusion.14, bf16[1536,2,2,128]{0,3,2,1:T(8,128)(2,1)S(1)} %bitcast.115, bf16[1024,2,2,64]{3,0,2,1:T(8,128)(2,1)} %get-tuple-element.5, bf16[1024,2,2,64]{3,0,2,1:T(8,128)(2,1)} %get-tuple-element.6), kind=kOutput, calls=%fused_computation.135 | convolution fusion | flops 822085120 | bytes 17047552 | tf_op jit(solution)/shard_map/sub | solution.py:56
  249.7 6.4 %fusion.43 = bf16[2,128,2,512]{3,1,2,0:T(8,128)(2,1)} fusion(f32[2,2,512,1536]{2,3,1,0:T(8,128)} %get-tuple-element.16, f32[2,2,512]{2,1,0:T(2,128)S(1)} %get-tuple-element.15, bf16[1536,2,2,128]{0,3,2,1:T(8,128)(2,1)S(1)} %bitcast.116), kind=kOutput, calls=%fused_computation.62 | convolution fusion | flops 811859968 | bytes 13901824 | tf_op jit(solution)/shard_map/hgqk,khd->qhgd/dot_general | solution.py:59
  256.0 1.3 collective-permute-start.7
  257.4 1.3 collective-permute-start.8
  258.7 10.4 %fusion.93 = (f32[2,2,512]{2,1,0:T(2,128)S(1)}, f32[2,2,512,1536]{2,3,1,0:T(8,128)}) fusion(pred[512,1536]{0,1:T(8,128)(4,1)} %fusion.16, bf16[1536,2,2,128]{0,3,2,1:T(8,128)(2,1)S(1)} %bitcast.113, bf16[1024,2,2,64]{3,0,2,1:T(8,128)(2,1)} %get-tuple-element.6, bf16[1024,2,2,64]{3,0,2,1:T(8,128)(2,1)} %get-tuple-element.5), kind=kOutput, calls=%fused_computation.134 | convolution fusion | flops 822085120 | bytes 17047552 | tf_op jit(solution)/shard_map/sub | solution.py:56
  269.0 5.6 %fusion.42 = bf16[2,128,2,512]{3,1,2,0:T(8,128)(2,1)S(1)} fusion(f32[2,2,512,1536]{2,3,1,0:T(8,128)} %get-tuple-element.14, f32[2,2,512]{2,1,0:T(2,128)S(1)} %get-tuple-element.13, bf16[1536,2,2,128]{0,3,2,1:T(8,128)(2,1)S(1)} %bitcast.114), kind=kOutput, calls=%fused_computation.61 | convolution fusion | flops 811859968 | bytes 13901824 | tf_op jit(solution)/shard_map/hgqk,khd->qhgd/dot_general | solution.py:59
  274.6 4.0 %collective-permute-start.13 = (bf16[512,512]{0,1:T(8,128)(2,1)S(1)}, bf16[512,512]{0,1:T(8,128)(2,1)S(1)}, u32[]{:S(2)}, u32[]{:S(2)}) collective-permute-start(bf16[512,512]{0,1:T(8,128)(2,1)S(1)} %bitcast.119), channel_id=1, source_target_pairs={{0,1},{1,2},{2,3},{4,5},{5,6},{6,7},{8,9},{9,10},{10,11},{12,13},{... | collective-permute-start | bytes 1572872 | tf_op jit(solution)/shard_map/ppermute | solution.py:77
  278.6 1.3 collective-permute-start.14
  280.0 2.5 fusion.52
  283.1 0.9 fusion.54
  284.0 1.3 collective-permute-start.10
  285.3 0.7 collective-permute-start.9
  286.0 0.9 collective-permute-start.15
  287.0 0.9 convolution_add_fusion.7
  287.9 0.9 convolution_add_fusion.3
  288.8 4.3 %collective-permute-done.14 = bf16[512,512]{0,1:T(8,128)(2,1)S(1)} collective-permute-done((bf16[512,512]{0,1:T(8,128)(2,1)S(1)}, bf16[512,512]{0,1:T(8,128)(2,1)S(1)}, u32[]{:S(2)}, u32[]{:S(2)}) %collective-permute-start.14) | collective-permute-done | bytes 524320 | tf_op jit(solution)/shard_map/ppermute | solution.py:78
  293.1 1.3 collective-permute-start.16
  294.4 0.9 convolution_add_fusion.6
  295.3 0.9 convolution_add_fusion.2
  296.2 0.7 collective-permute-start.11
  296.9 7.4 %collective-permute-done.10 = bf16[512,512]{0,1:T(8,128)(2,1)S(1)} collective-permute-done((bf16[512,512]{0,1:T(8,128)(2,1)S(1)}, bf16[512,512]{0,1:T(8,128)(2,1)S(1)}, u32[]{:S(2)}, u32[]{:S(2)}) %collective-permute-start.10) | collective-permute-done | bytes 524320 | tf_op jit(solution)/shard_map/ppermute | solution.py:78
  304.4 1.3 collective-permute-start.12
  306.4 9.2 %collective-permute-done.16 = bf16[512,512]{0,1:T(8,128)(2,1)S(1)} collective-permute-done((bf16[512,512]{0,1:T(8,128)(2,1)S(1)}, bf16[512,512]{0,1:T(8,128)(2,1)S(1)}, u32[]{:S(2)}, u32[]{:S(2)}) %collective-permute-start.16) | collective-permute-done | bytes 524320 | tf_op jit(solution)/shard_map/ppermute | solution.py:78
  315.6 1.3 collective-permute-start.18
  316.9 0.9 convolution_add_fusion.5
  317.8 0.9 convolution_add_fusion.1
  318.7 6.7 %collective-permute-done.12 = bf16[512,512]{0,1:T(8,128)(2,1)S(1)} collective-permute-done((bf16[512,512]{0,1:T(8,128)(2,1)S(1)}, bf16[512,512]{0,1:T(8,128)(2,1)S(1)}, u32[]{:S(2)}, u32[]{:S(2)}) %collective-permute-start.12) | collective-permute-done | bytes 524320 | tf_op jit(solution)/shard_map/ppermute | solution.py:78
  325.4 0.9 fusion.17
  326.3 4.7 %collective-permute-done.18 = bf16[512,512]{0,1:T(8,128)(2,1)S(1)} collective-permute-done((bf16[512,512]{0,1:T(8,128)(2,1)S(1)}, bf16[512,512]{0,1:T(8,128)(2,1)S(1)}, u32[]{:S(2)}, u32[]{:S(2)}) %collective-permute-start.18) | collective-permute-done | bytes 524320 | tf_op jit(solution)/shard_map/ppermute | solution.py:78
  331.0 0.9 fusion.18
  331.9 2.0 pad_maximum_fusion
  (52 shorter events, 2.7 us)
Async XLA Ops:
  6.5 137.3 %all-gather.3.cloned.1.call-start = ((), (), s32[]{:S(2)}) async-start(), calls=%async_computation | async-start | bytes 13762560 | tf_op jit(solution)/shard_map/all_gather | solution.py:96
  10.6 1.8 copy-start.7
  10.6 269.3 %all-gather.5.cloned.1.call-start = ((), (), s32[]{:S(2)}) async-start(), calls=%async_computation.1 | async-start | bytes 6881280 | tf_op jit(solution)/shard_map/all_gather | solution.py:127
  12.4 62.4 %collective-permute-start = (bf16[1024,1344]{0,1:T(8,128)(2,1)S(1)}, bf16[1024,1344]{0,1:T(8,128)(2,1)}, u32[]{:S(2)}, u32[]{:S(2)}) collective-permute-start(bf16[1024,1344]{0,1:T(8,128)(2,1)S(1)} %copy-done.7), channel_id=1, source_target_pairs={{0,1},{1,2},{2,3},{4,5},{5,6},{6,7},{8,9},{9,10},{10,11},{12,13},{... | collective-permute-start | bytes 8257544 | tf_op jit(solution)/shard_map/ppermute | solution.py:77
  17.9 62.2 %collective-permute-start.1 = (bf16[1024,1344]{0,1:T(8,128)(2,1)S(1)}, bf16[1024,1344]{0,1:T(8,128)(2,1)}, u32[]{:S(2)}, u32[]{:S(2)}) collective-permute-start(bf16[1024,1344]{0,1:T(8,128)(2,1)S(1)} %copy-done.7), channel_id=1, source_target_pairs={{1,0},{2,1},{3,2},{5,4},{6,5},{7,6},{9,8},{10,9},{11,10},{13,12},{... | collective-permute-start | bytes 8257544 | tf_op jit(solution)/shard_map/ppermute | solution.py:78
  74.7 13.7 %collective-permute-start.2 = (bf16[1024,1344]{0,1:T(8,128)(2,1)}, bf16[1024,1344]{0,1:T(8,128)(2,1)}, u32[]{:S(2)}, u32[]{:S(2)}) collective-permute-start(bf16[1024,1344]{0,1:T(8,128)(2,1)} %collective-permute-done), channel_id=1, source_target_pairs={{1,2},{2,3},{5,6},{6,7},{9,10},{10,11},{13,14},{14,15},{17,18},{18... | collective-permute-start | bytes 8257544 | tf_op jit(solution)/shard_map/ppermute | solution.py:77
  80.1 61.9 %collective-permute-start.3 = (bf16[1024,1344]{0,1:T(8,128)(2,1)}, bf16[1024,1344]{0,1:T(8,128)(2,1)}, u32[]{:S(2)}, u32[]{:S(2)}) collective-permute-start(bf16[1024,1344]{0,1:T(8,128)(2,1)} %collective-permute-done.1), channel_id=1, source_target_pairs={{1,0},{2,1},{5,4},{6,5},{9,8},{10,9},{13,12},{14,13},{17,16},{18,1... | collective-permute-start | bytes 8257544 | tf_op jit(solution)/shard_map/ppermute | solution.py:78
  88.4 78.9 %collective-permute-start.4 = (bf16[1024,1344]{0,1:T(8,128)(2,1)}, bf16[1024,1344]{0,1:T(8,128)(2,1)S(1)}, u32[]{:S(2)}, u32[]{:S(2)}) collective-permute-start(bf16[1024,1344]{0,1:T(8,128)(2,1)} %collective-permute-done.2), channel_id=1, source_target_pairs={{2,3},{6,7},{10,11},{14,15},{18,19},{22,23},{26,27},{30,31}} | collective-permute-start | bytes 8257544 | tf_op jit(solution)/shard_map/ppermute | solution.py:77
  142.0 60.8 %collective-permute-start.5 = (bf16[1024,1344]{0,1:T(8,128)(2,1)}, bf16[1024,1344]{0,1:T(8,128)(2,1)}, u32[]{:S(2)}, u32[]{:S(2)}) collective-permute-start(bf16[1024,1344]{0,1:T(8,128)(2,1)} %collective-permute-done.3), channel_id=1, source_target_pairs={{1,0},{5,4},{9,8},{13,12},{17,16},{21,20},{25,24},{29,28}} | collective-permute-start | bytes 8257544 | tf_op jit(solution)/shard_map/ppermute | solution.py:78
  143.9 12.7 %slice-start = ((s8[11010048]{0:T(1024)(128)(4,1)}), s8[4194304]{0:T(1024)(128)(4,1)S(1)}, s32[]{:S(2)}) async-start(s8[11010048]{0:T(1024)(128)(4,1)} %bitcast.117), calls=%async_computation.2 | async-start | bytes 8388608
  143.9 12.7 %slice-start.1 = ((s8[11010048]{0:T(1024)(128)(4,1)}), s8[4194304]{0:T(1024)(128)(4,1)S(1)}, s32[]{:S(2)}) async-start(s8[11010048]{0:T(1024)(128)(4,1)} %bitcast.117), calls=%async_computation.3 | async-start | bytes 8388608
  150.2 6.4 %slice-start.2 = ((s8[11010048]{0:T(1024)(128)(4,1)}), s8[2621440]{0:T(1024)(128)(4,1)S(1)}, s32[]{:S(2)}) async-start(s8[11010048]{0:T(1024)(128)(4,1)} %bitcast.117), calls=%async_computation.4 | async-start | bytes 5242880
  150.2 6.4 %copy-start.8 = (bf16[1024,1344]{0,1:T(8,128)(2,1)S(1)}, bf16[1024,1344]{0,1:T(8,128)(2,1)}, u32[]{:S(2)}) copy-start(bf16[1024,1344]{0,1:T(8,128)(2,1)} %param.5) | copy-start | bytes 8257540
  167.3 1.5 copy-start.2
  211.1 1.9 copy-start
  214.5 4.6 %copy-start.5 = (f32[128]{0:T(128)S(1)}, f32[128]{0:T(128)}, u32[]{:S(2)}) copy-start(f32[128]{0:T(128)} %param.9) | copy-start | bytes 1540
  220.5 7.6 %copy-start.6 = (f32[128]{0:T(128)S(1)}, f32[128]{0:T(128)}, u32[]{:S(2)}) copy-start(f32[128]{0:T(128)} %param.8) | copy-start | bytes 1540
  220.8 8.2 %copy-start.3 = (f32[1024,64]{1,0:T(8,128)S(1)}, f32[1024,64]{1,0:T(8,128)}, u32[]{:S(2)}) copy-start(f32[1024,64]{1,0:T(8,128)} %copy.25) | copy-start | bytes 786436
  220.8 8.2 %copy-start.4 = (f32[1024,64]{1,0:T(8,128)S(1)}, f32[1024,64]{1,0:T(8,128)}, u32[]{:S(2)}) copy-start(f32[1024,64]{1,0:T(8,128)} %copy.26) | copy-start | bytes 786436
  220.8 18.4 %collective-permute-start.6 = (bf16[1024,512]{0,1:T(8,128)(2,1)S(1)}, bf16[1024,512]{0,1:T(8,128)(2,1)S(1)}, u32[]{:S(2)}, u32[]{:S(2)}) collective-permute-start(bf16[1024,512]{0,1:T(8,128)(2,1)S(1)} %bitcast.110), channel_id=1, source_target_pairs={{0,4},{4,8},{8,12},{1,5},{5,9},{9,13},{2,6},{6,10},{10,14},{3,7},{... | collective-permute-start | bytes 3145736 | tf_op jit(solution)/shard_map/ppermute | solution.py:21
  256.0 29.2 %collective-permute-start.7 = (bf16[512,512]{0,1:T(8,128)(2,1)}, bf16[512,512]{0,1:T(8,128)(2,1)S(1)}, u32[]{:S(2)}, u32[]{:S(2)}) collective-permute-start(bf16[512,512]{0,1:T(8,128)(2,1)} %bitcast.16), channel_id=1, source_target_pairs={{0,1},{1,2},{2,3},{4,5},{5,6},{6,7},{8,9},{9,10},{10,11},{12,13},{... | collective-permute-start | bytes 1572872 | tf_op jit(solution)/shard_map/ppermute | solution.py:77
  257.4 26.6 %collective-permute-start.8 = (bf16[512,512]{0,1:T(8,128)(2,1)}, bf16[512,512]{0,1:T(8,128)(2,1)S(1)}, u32[]{:S(2)}, u32[]{:S(2)}) collective-permute-start(bf16[512,512]{0,1:T(8,128)(2,1)} %bitcast.16), channel_id=1, source_target_pairs={{1,0},{2,1},{3,2},{5,4},{6,5},{7,6},{9,8},{10,9},{11,10},{13,12},{... | collective-permute-start | bytes 1572872 | tf_op jit(solution)/shard_map/ppermute | solution.py:78
  274.6 11.4 %collective-permute-start.13 = (bf16[512,512]{0,1:T(8,128)(2,1)S(1)}, bf16[512,512]{0,1:T(8,128)(2,1)S(1)}, u32[]{:S(2)}, u32[]{:S(2)}) collective-permute-start(bf16[512,512]{0,1:T(8,128)(2,1)S(1)} %bitcast.119), channel_id=1, source_target_pairs={{0,1},{1,2},{2,3},{4,5},{5,6},{6,7},{8,9},{9,10},{10,11},{12,13},{... | collective-permute-start | bytes 1572872 | tf_op jit(solution)/shard_map/ppermute | solution.py:77
  278.6 14.5 %collective-permute-start.14 = (bf16[512,512]{0,1:T(8,128)(2,1)S(1)}, bf16[512,512]{0,1:T(8,128)(2,1)S(1)}, u32[]{:S(2)}, u32[]{:S(2)}) collective-permute-start(bf16[512,512]{0,1:T(8,128)(2,1)S(1)} %bitcast.120), channel_id=1, source_target_pairs={{1,0},{2,1},{3,2},{5,4},{6,5},{7,6},{9,8},{10,9},{11,10},{13,12},{... | collective-permute-start | bytes 1572872 | tf_op jit(solution)/shard_map/ppermute | solution.py:78
  279.9 3.1 copy-start.1
  284.0 20.4 %collective-permute-start.10 = (bf16[512,512]{0,1:T(8,128)(2,1)S(1)}, bf16[512,512]{0,1:T(8,128)(2,1)S(1)}, u32[]{:S(2)}, u32[]{:S(2)}) collective-permute-start(bf16[512,512]{0,1:T(8,128)(2,1)S(1)} %collective-permute-done.8), channel_id=1, source_target_pairs={{1,0},{2,1},{5,4},{6,5},{9,8},{10,9},{13,12},{14,13},{17,16},{18,1... | collective-permute-start | bytes 1572872 | tf_op jit(solution)/shard_map/ppermute | solution.py:78
  285.3 10.9 %collective-permute-start.9 = (bf16[512,512]{0,1:T(8,128)(2,1)S(1)}, bf16[512,512]{0,1:T(8,128)(2,1)S(1)}, u32[]{:S(2)}, u32[]{:S(2)}) collective-permute-start(bf16[512,512]{0,1:T(8,128)(2,1)S(1)} %collective-permute-done.7), channel_id=1, source_target_pairs={{1,2},{2,3},{5,6},{6,7},{9,10},{10,11},{13,14},{14,15},{17,18},{18... | collective-permute-start | bytes 1572872 | tf_op jit(solution)/shard_map/ppermute | solution.py:77
  286.0 19.7 %collective-permute-start.15 = (bf16[512,512]{0,1:T(8,128)(2,1)S(1)}, bf16[512,512]{0,1:T(8,128)(2,1)S(1)}, u32[]{:S(2)}, u32[]{:S(2)}) collective-permute-start(bf16[512,512]{0,1:T(8,128)(2,1)S(1)} %collective-permute-done.13), channel_id=1, source_target_pairs={{1,2},{2,3},{5,6},{6,7},{9,10},{10,11},{13,14},{14,15},{17,18},{18... | collective-permute-start | bytes 1572872 | tf_op jit(solution)/shard_map/ppermute | solution.py:77
  293.1 22.5 %collective-permute-start.16 = (bf16[512,512]{0,1:T(8,128)(2,1)S(1)}, bf16[512,512]{0,1:T(8,128)(2,1)S(1)}, u32[]{:S(2)}, u32[]{:S(2)}) collective-permute-start(bf16[512,512]{0,1:T(8,128)(2,1)S(1)} %collective-permute-done.14), channel_id=1, source_target_pairs={{1,0},{2,1},{5,4},{6,5},{9,8},{10,9},{13,12},{14,13},{17,16},{18,1... | collective-permute-start | bytes 1572872 | tf_op jit(solution)/shard_map/ppermute | solution.py:78
  296.2 22.4 %collective-permute-start.11 = (bf16[512,512]{0,1:T(8,128)(2,1)S(1)}, bf16[512,512]{0,1:T(8,128)(2,1)S(1)}, u32[]{:S(2)}, u32[]{:S(2)}) collective-permute-start(bf16[512,512]{0,1:T(8,128)(2,1)S(1)} %collective-permute-done.9), channel_id=1, source_target_pairs={{2,3},{6,7},{10,11},{14,15},{18,19},{22,23},{26,27},{30,31}} | collective-permute-start | bytes 1572872 | tf_op jit(solution)/shard_map/ppermute | solution.py:77
  304.4 21.0 %collective-permute-start.12 = (bf16[512,512]{0,1:T(8,128)(2,1)S(1)}, bf16[512,512]{0,1:T(8,128)(2,1)S(1)}, u32[]{:S(2)}, u32[]{:S(2)}) collective-permute-start(bf16[512,512]{0,1:T(8,128)(2,1)S(1)} %collective-permute-done.10), channel_id=1, source_target_pairs={{1,0},{5,4},{9,8},{13,12},{17,16},{21,20},{25,24},{29,28}} | collective-permute-start | bytes 1572872 | tf_op jit(solution)/shard_map/ppermute | solution.py:78
  305.7 20.6 %collective-permute-start.17 = (bf16[512,512]{0,1:T(8,128)(2,1)S(1)}, bf16[512,512]{0,1:T(8,128)(2,1)S(1)}, u32[]{:S(2)}, u32[]{:S(2)}) collective-permute-start(bf16[512,512]{0,1:T(8,128)(2,1)S(1)} %collective-permute-done.15), channel_id=1, source_target_pairs={{2,3},{6,7},{10,11},{14,15},{18,19},{22,23},{26,27},{30,31}} | collective-permute-start | bytes 1572872 | tf_op jit(solution)/shard_map/ppermute | solution.py:77
  315.6 15.4 %collective-permute-start.18 = (bf16[512,512]{0,1:T(8,128)(2,1)S(1)}, bf16[512,512]{0,1:T(8,128)(2,1)S(1)}, u32[]{:S(2)}, u32[]{:S(2)}) collective-permute-start(bf16[512,512]{0,1:T(8,128)(2,1)S(1)} %collective-permute-done.16), channel_id=1, source_target_pairs={{1,0},{5,4},{9,8},{13,12},{17,16},{21,20},{25,24},{29,28}} | collective-permute-start | bytes 1572872 | tf_op jit(solution)/shard_map/ppermute | solution.py:78
Sparse Core Ops, SparseCore 0:
  10.7 75.6 all-gather.2
  88.0 41.9 all-gather.4

commit v2 on v1

v2 whole, which is shorter than its diff:
```python
import functools
import math

import jax
import jax.numpy as jnp
from jax import lax
from jax.experimental import pallas as pl
from jax.experimental.pallas import tpu as pltpu
from jax.sharding import PartitionSpec as P

HD = 128
GROUP = 2
WINDOW = 1024


EPS = 1e-06
SCALE = 168.0 ** (-0.5)
ROPE_BASE = 10000.0
PIECES = 2
CHUNKS = 2


def from_behind(value, axis, steps):
    count = lax.axis_size(axis)
    first, last = (max(0, -steps), min(count, count - steps))
    return lax.ppermute(value, axis, [(source, source + steps) for source in range(first, last)])


def rope_tables(rows, base):
    half = HD // 2
    inverse = jnp.exp(
        jnp.arange(half, dtype=jnp.float32) * (-2.0 * math.log(ROPE_BASE) / HD)
    )
    pos = base + jnp.arange(rows, dtype=jnp.int32)
    angle = pos.astype(jnp.float32)[:, None] * inverse[None, :]
    cosine, sine = jnp.cos(angle), jnp.sin(angle)
    return (
        jnp.concatenate([cosine, cosine], axis=1),
        jnp.concatenate([-sine, sine], axis=1),
    )


def norm_rope_kernel(rotated, total, x_ref, gain_ref, cos_ref, sin_ref, o_ref):
    gain = gain_ref[...]
    cosine, sine = cos_ref[...], sin_ref[...]
    for head in range(x_ref.shape[1] // HD):
        columns = slice(head * HD, (head + 1) * HD)
        values = x_ref[:, columns]
        if head % total < rotated:
            meansq = jnp.mean(values * values, axis=-1, keepdims=True)
            values = values * lax.rsqrt(meansq + EPS) * gain
            values = values * cosine + pltpu.roll(values, HD // 2, 1) * sine
        o_ref[:, columns] = values.astype(o_ref.dtype)


def norm_rope(values, gain, cosine, sine, rotated, total):
    rows, columns = values.shape
    tile = 256
    row = lambda i: (i, 0)
    return pl.pallas_call(
        functools.partial(norm_rope_kernel, rotated, total),
        out_shape=jax.ShapeDtypeStruct((rows, columns), jnp.bfloat16),
        grid=(rows // tile,),
        in_specs=[
            pl.BlockSpec((tile, columns), row),
            pl.BlockSpec((1, HD), lambda i: (0, 0)),
            pl.BlockSpec((tile, HD), row),
            pl.BlockSpec((tile, HD), row),
        ],
        out_specs=pl.BlockSpec((tile, columns), row),
        cost_estimate=pl.CostEstimate(
            flops=20 * rows * columns, bytes_accessed=6 * rows * columns, transcendentals=0
        ),
    )(values, gain.reshape(1, HD), cosine, sine)


def attend_kernel(q_tile, row0, base_ref, q_ref, k_ref, v_ref, o_ref):
    first = row0 + pl.program_id(1) * q_tile
    span = q_tile + WINDOW
    keys = k_ref[pl.ds(pl.multiple_of(first, q_tile), span), :]
    values = v_ref[pl.ds(pl.multiple_of(first, q_tile), span), :]
    row = lax.broadcasted_iota(jnp.int32, (q_tile, span), 0)
    column = lax.broadcasted_iota(jnp.int32, (q_tile, span), 1)
    least = jnp.maximum(row, WINDOW - 1 - (base_ref[0] + first))
    keep = (column > least) & (column <= row + WINDOW)
    for member in range(GROUP):
        columns = slice(member * HD, (member + 1) * HD)
        scores = lax.dot_general(
            q_ref[:, columns], keys, (((1,), (1,)), ((), ())), preferred_element_type=jnp.float32
        )
        masked = jnp.where(keep, scores, jnp.float32(-1e30))
        top = jnp.max(masked, axis=-1, keepdims=True)
        expo = jnp.exp2((masked - top) * jnp.float32(SCALE * math.log2(math.e)))
        total = jnp.sum(expo, axis=-1, keepdims=True)
        weights = (expo * (1.0 / total)).astype(jnp.bfloat16)
        result = jnp.dot(weights, values, preferred_element_type=jnp.float32)
        o_ref[:, columns] = result.astype(o_ref.dtype)


def attend(query, paired, base, row0, count):
    kv_local = query.shape[1] // (GROUP * HD)
    q_tile = 256
    from_tile = row0 // q_tile
    whole = paired.shape[0]
    return pl.pallas_call(
        functools.partial(attend_kernel, q_tile, row0),
        out_shape=jax.ShapeDtypeStruct((count, query.shape[1]), jnp.bfloat16),
        grid=(kv_local, count // q_tile),
        in_specs=[
            pl.BlockSpec(memory_space=pltpu.SMEM),
            pl.BlockSpec((q_tile, GROUP * HD), lambda h, i: (from_tile + i, h)),
            pl.BlockSpec((whole, HD), lambda h, i: (0, 2 * h)),
            pl.BlockSpec((whole, HD), lambda h, i: (0, 2 * h + 1)),
        ],
        out_specs=pl.BlockSpec((q_tile, GROUP * HD), lambda h, i: (i, h)),
        compiler_params=pltpu.CompilerParams(vmem_limit_bytes=32 * 1024 * 1024),
        cost_estimate=pl.CostEstimate(
            flops=4 * count * query.shape[1] * (WINDOW + q_tile),
            bytes_accessed=4 * (whole + count) * query.shape[1],
            transcendentals=count * query.shape[1] // HD * (WINDOW + q_tile),
        ),
    )(base.reshape(1), query, paired, paired)


def line_gather_dot(pieces, weight, axis, depth, column_ranges):
    count = lax.axis_size(axis)
    here = lax.axis_index(axis)

    def terms(totals, piece, owner, first):
        out = []
        for total, (start, width) in zip(totals, column_ranges):
            rows = lax.dynamic_slice(
                weight, (owner * depth + first, start), (piece.shape[1], width)
            )
            term = jnp.dot(piece, rows, preferred_element_type=jnp.float32)
            out.append(term if total is None else total + term)
        return out

    totals = [None] * len(column_ranges)
    ups = [piece for piece, _ in pieces]
    downs = list(ups)
    for piece, first in pieces:
        totals = terms(totals, piece, here, first)
    for step in range(1, count):
        for at, (_, first) in enumerate(pieces):
            up = lax.ppermute(ups[at], axis, [(i, i + 1) for i in range(step - 1, count - 1)])
            down = lax.ppermute(downs[at], axis, [(i + 1, i) for i in range(count - step)])
            ups[at], downs[at] = up, down
            if step == count - 1 and len(totals) > 1:
                totals, up, down = lax.optimization_barrier((totals, up, down))
            below = jnp.maximum(here - step, 0)
            above = jnp.minimum(here + step, count - 1)
            if 2 * step < count:
                totals = terms(totals, up, below, first)
                totals = terms(totals, down, above, first)
            else:
                from_below = here >= step
                totals = terms(
                    totals,
                    jnp.where(from_below, up, down),
                    jnp.where(from_below, below, above),
                    first,
                )
    return totals


def on_device(states, w_qkv, w_out, q_gain, k_gain):
    rows, depth = states.shape
    kv_local = w_qkv.shape[1]
    q_columns = kv_local * GROUP * HD
    kv_columns = kv_local * 2 * HD
    arranged = jnp.concatenate(
        [
            w_qkv[:, :, : GROUP * HD].reshape(-1, q_columns),
            w_qkv[:, :, GROUP * HD :].reshape(-1, kv_columns),
        ],
        axis=1,
    )
    weight_whole = lax.all_gather(arranged, "tok", axis=0, tiled=True)
    part = depth // PIECES
    kv, query = line_gather_dot(
        [(states[:, i * part : (i + 1) * part], i * part) for i in range(PIECES)],
        weight_whole,
        "hid",
        depth,
        [(q_columns, kv_columns), (0, q_columns)],
    )
    base = lax.axis_index("tok") * rows
    cosine, sine = rope_tables(rows, base)
    paired = norm_rope(kv, k_gain, cosine, sine, 1, 2)
    behind = from_behind(paired[rows - WINDOW :], "tok", 1)
    query = norm_rope(query, q_gain, cosine, sine, 1, 1)
    combined = jnp.concatenate([behind, paired], axis=0)
    block = rows // CHUNKS
    out_whole = lax.all_gather(w_out, "tok", axis=0, tiled=True)
    results = []
    for index in range(CHUNKS):
        heads = attend(query, combined, base, index * block, block)
        (summed,) = line_gather_dot(
            [(heads, 0)], out_whole, "hid", heads.shape[1], [(0, w_out.shape[1])]
        )
        results.append(summed.astype(jnp.bfloat16))
    return jnp.concatenate(results, axis=0)


def solution(mesh):
    return jax.shard_map(
        on_device,
        mesh=mesh,
        in_specs=(P(("groups", "tok"), "hid"), P("tok", "hid", None), P("tok", "hid"), P(), P()),
        out_specs=P(("groups", "tok"), "hid"),
        check_vma=False,
    )
```

time: 345 us -> 326 us (0.945)
  waiting for transfers between devices: 186 us -> 155 us
  Pallas kernels: 0 us -> 25.5 us
  matrix products: 74.8 us -> 60.7 us
  local copies, waits for them, and re-layouts: 16.6 us -> 6.19 us
  starting transfers between devices: 35.7 us -> 45.7 us
    ppermute x18 -> x24, waiting for transfers between devices: 178 us -> 152 us  [the longest x12 103 us: line_gather_dot(): lax.ppermute(downs[at], axis, [(i + 1, i) for i in range(count - step)])]
    pallas_call x0 -> x4, Pallas kernels: none -> 25.5 us  [the longest x2 16.2 us: attend(): pl.pallas_call(functools.partial(attend_kernel, q_tile, row0), out_shape=...]
    sub x2 -> x0, matrix products: 20.6 us -> none  [attend(): expo = jnp.where(keep, jnp.exp(masked - top), jnp.float32(0.0))]
    ppermute x18 -> x24, starting transfers between devices: 29 us -> 40.8 us  [the longest x12 25 us: line_gather_dot(): lax.ppermute(ups[at], axis, [(i, i + 1) for i in range(step - 1, count -...]
    unnamed x26 -> x14, local copies, waits for them, and re-layouts: 11.8 us -> 2.34 us
    dot_general x17 -> x30, matrix products: 54.1 us -> 60.7 us  [terms(): term = jnp.dot(piece, rows, preferred_element_type=jnp.float32)]
    ppermute x1, waiting for transfers between devices: 8.02 us -> 2.66 us  [from_behind(): lax.ppermute(value, axis, [(source, source + steps) for source in range(f...]
    add x4, other arithmetic: 0.03 us -> 4.55 us  [terms(): out.append(term if total is None else total + term)]
  transfers between devices with their start and end apart: 21 -> 27, of which waited for: 10 -> 14; matrix products, arithmetic and copies ran while one was open for 27% -> 22% of each run, Pallas kernels for 0% -> 8%
where the time goes in v2:
time: 326 us; the launch traced here: 320 us
  waiting for transfers between devices  155 us (48%)
  matrix products  60.7 us (19%)
  starting transfers between devices  45.7 us (14%)
  Pallas kernels  25.5 us (8%)
  between operations  14.4 us (4%)
  other arithmetic  12.9 us (4%)
  local copies, waits for them, and re-layouts  6.19 us (2%)
    ppermute x12, waiting for transfers between devices, line_gather_dot(): lax.ppermute(downs[at], axis, [(i + 1, i) for i in range(count - step)])  103 us
    dot_general x30, matrix products, terms(): term = jnp.dot(piece, rows, preferred_element_type=jnp.float32)  60.7 us
    ppermute x12, waiting for transfers between devices, line_gather_dot(): lax.ppermute(ups[at], axis, [(i, i + 1) for i in range(step - 1, count -...  48.5 us
    ppermute x12, starting transfers between devices, line_gather_dot(): lax.ppermute(ups[at], axis, [(i, i + 1) for i in range(step - 1, count -...  25 us
    pallas_call x2, Pallas kernels, attend(): pl.pallas_call(functools.partial(attend_kernel, q_tile, row0), out_shape=...  16.2 us
    ppermute x12, starting transfers between devices, line_gather_dot(): lax.ppermute(downs[at], axis, [(i + 1, i) for i in range(count - step)])  15.8 us
    pallas_call x2, Pallas kernels, norm_rope(): pl.pallas_call(functools.partial(norm_rope_kernel, rotated, total), out_s...  9.37 us
  transfers between devices with their start and end apart: 27, of which 14 were waited for; matrix products, arithmetic and copies ran while one was open for 22% of the time, Pallas kernels for 8%

profile of v2, /device:TPU:1, one launch (start us, length us, event | category | flops | bytes accessed | tf_op | source)
XLA Modules:
  0.0 320.1 jit_solution(12893195613020119635)
XLA Ops:
  6.5 3.6 %fusion.108 = (bf16[1344,2,256]{2,1,0:T(2,128)(2,1)S(1)}, bf16[1344,2,256]{2,1,0:T(2,128)(2,1)S(1)}) fusion(bf16[1344,2,512]{2,1,0:T(2,128)(2,1)} %param.6), kind=kLoop, calls=%fused_computation.125 | loop fusion | bytes 5505024 | tf_op jit(solution)/shard_map/slice | solution.py:174
  10.8 1.9 pad_maximum_fusion
  12.7 1.7 copy-done.3
  14.7 5.1 %collective-permute-start = (bf16[1024,672]{0,1:T(8,128)(2,1)S(1)}, bf16[1024,672]{0,1:T(8,128)(2,1)}, u32[]{:S(2)}, u32[]{:S(2)}) collective-permute-start(bf16[1024,672]{0,1:T(8,128)(2,1)S(1)} %get-tuple-element.22), channel_id=1, source_target_pairs={{0,1},{1,2},{2,3},{4,5},{5,6},{6,7},{8,9},{9,10},{10,11},{12,13},{... | collective-permute-start | bytes 4128776 | tf_op jit(solution)/shard_map/ppermute | solution.py:146
  19.8 1.3 collective-permute-start.1
  21.1 5.1 %collective-permute-start.2 = (bf16[1024,672]{0,1:T(8,128)(2,1)S(1)}, bf16[1024,672]{0,1:T(8,128)(2,1)}, u32[]{:S(2)}, u32[]{:S(2)}) collective-permute-start(bf16[1024,672]{0,1:T(8,128)(2,1)S(1)} %get-tuple-element.21), channel_id=1, source_target_pairs={{0,1},{1,2},{2,3},{4,5},{5,6},{6,7},{8,9},{9,10},{10,11},{12,13},{... | collective-permute-start | bytes 4128776 | tf_op jit(solution)/shard_map/ppermute | solution.py:146
  26.2 1.3 collective-permute-start.3
  27.5 20.0 %collective-permute-done = bf16[1024,672]{0,1:T(8,128)(2,1)} collective-permute-done((bf16[1024,672]{0,1:T(8,128)(2,1)S(1)}, bf16[1024,672]{0,1:T(8,128)(2,1)}, u32[]{:S(2)}, u32[]{:S(2)}) %collective-permute-start) | collective-permute-done | bytes 1376288 | tf_op jit(solution)/shard_map/ppermute | solution.py:146
  48.3 4.2 %collective-permute-done.1 = bf16[1024,672]{0,1:T(8,128)(2,1)} collective-permute-done((bf16[1024,672]{0,1:T(8,128)(2,1)S(1)}, bf16[1024,672]{0,1:T(8,128)(2,1)}, u32[]{:S(2)}, u32[]{:S(2)}) %collective-permute-start.1) | collective-permute-done | bytes 1376288 | tf_op jit(solution)/shard_map/ppermute | solution.py:147
  52.5 1.3 collective-permute-start.5
  53.8 23.2 %collective-permute-done.2 = bf16[1024,672]{0,1:T(8,128)(2,1)} collective-permute-done((bf16[1024,672]{0,1:T(8,128)(2,1)S(1)}, bf16[1024,672]{0,1:T(8,128)(2,1)}, u32[]{:S(2)}, u32[]{:S(2)}) %collective-permute-start.2) | collective-permute-done | bytes 1376288 | tf_op jit(solution)/shard_map/ppermute | solution.py:146
  77.8 4.2 %collective-permute-done.3 = bf16[1024,672]{0,1:T(8,128)(2,1)} collective-permute-done((bf16[1024,672]{0,1:T(8,128)(2,1)S(1)}, bf16[1024,672]{0,1:T(8,128)(2,1)}, u32[]{:S(2)}, u32[]{:S(2)}) %collective-permute-start.3) | collective-permute-done | bytes 1376288 | tf_op jit(solution)/shard_map/ppermute | solution.py:147
  82.0 1.3 collective-permute-start.7
  83.4 1.9 fusion.72
  85.3 1.3 pad_maximum_fusion.3
  86.7 1.8 collective-permute-start.8
  88.4 23.1 %collective-permute-done.5 = bf16[1024,672]{0,1:T(8,128)(2,1)} collective-permute-done((bf16[1024,672]{0,1:T(8,128)(2,1)}, bf16[1024,672]{0,1:T(8,128)(2,1)}, u32[]{:S(2)}, u32[]{:S(2)}) %collective-permute-start.5) | collective-permute-done | bytes 1376288 | tf_op jit(solution)/shard_map/ppermute | solution.py:147
  111.5 1.3 collective-permute-start.9
  112.8 1.8 collective-permute-start.10
  114.6 26.4 %collective-permute-done.7 = bf16[1024,672]{0,1:T(8,128)(2,1)} collective-permute-done((bf16[1024,672]{0,1:T(8,128)(2,1)}, bf16[1024,672]{0,1:T(8,128)(2,1)}, u32[]{:S(2)}, u32[]{:S(2)}) %collective-permute-start.7) | collective-permute-done | bytes 1376288 | tf_op jit(solution)/shard_map/ppermute | solution.py:147
  141.0 1.5 collective-permute-start.11
  142.5 2.7 fusion.34
  145.3 3.2 %fusion.52 = f32[512,1024]{0,1:T(8,128)S(1)} fusion(bf16[1024,672]{0,1:T(8,128)(2,1)} %collective-permute-done.3, bf16[5376,1024]{1,0:T(8,128)(2,1)} %all-gather.3.cloned.1.call-done, s32[]{:T(128)S(6)} %select_n.122), kind=kOutput, calls=%fused_computation.65 | convolution fusion | flops 704643072 | bytes 4161540 | tf_op jit(solution)/shard_map/dot_general | solution.py:135
  148.5 2.6 fusion.36
  151.1 2.4 fusion.54
  153.5 2.4 fusion.38
  155.9 2.4 fusion.56
  158.3 2.4 fusion.40
  160.7 2.5 fusion.58
  166.4 2.4 fusion.32
  168.8 3.2 fusion.4
  171.9 2.1 fusion.62
  174.1 2.6 fusion.50
  176.6 3.0 fusion.5
  179.6 2.6 fusion.24
  182.7 2.6 fusion.26
  185.8 14.2 %collective-permute-done.11 = bf16[1024,672]{0,1:T(8,128)(2,1)} collective-permute-done((bf16[1024,672]{0,1:T(8,128)(2,1)}, bf16[1024,672]{0,1:T(8,128)(2,1)}, u32[]{:S(2)}, u32[]{:S(2)}) %collective-permute-start.11) | collective-permute-done | bytes 1376288 | tf_op jit(solution)/shard_map/ppermute | solution.py:147
  200.0 2.5 fusion.20
  202.6 1.8 add.250.x_ref
  204.4 4.4 %shard_map.56 = bf16[1024,512]{1,0:T(8,128)(2,1)} custom-call(f32[1024,512]{1,0:T(8,128)} %add.250.x_ref, f32[1,128]{1,0:T(1,128)} %bitcast.33, f32[1024,128]{1,0:T(8,128)} %get-tuple-element.28.cos_ref, f32[1024,128]{1,0:T(8,128)} %get-tuple-element.29.sin_ref), custom_call_target="tpu_custom_call" | custom-call | flops 10485760 | bytes 3145728 | tf_op jit(solution)/shard_map/pallas_call | solution.py:60
  208.7 4.9 %collective-permute-start.12 = (bf16[1024,512]{1,0:T(8,128)(2,1)}, bf16[1024,512]{1,0:T(8,128)(2,1)}, u32[]{:S(2)}, u32[]{:S(2)}) collective-permute-start(bf16[1024,512]{1,0:T(8,128)(2,1)} %shard_map.56), channel_id=1, source_target_pairs={{0,4},{4,8},{8,12},{1,5},{5,9},{9,13},{2,6},{6,10},{10,14},{3,7},{... | collective-permute-start | bytes 3145736 | tf_op jit(solution)/shard_map/ppermute | solution.py:26
  213.6 2.6 fusion.22
  216.2 1.8 add.247.x_ref
  218.0 5.0 %shard_map.55.q_ref = bf16[1024,512]{1,0:T(8,128)(2,1)} custom-call(f32[1024,512]{1,0:T(8,128)} %add.247.x_ref, f32[1,128]{1,0:T(1,128)} %bitcast.34, f32[1024,128]{1,0:T(8,128)} %get-tuple-element.28.cos_ref, f32[1024,128]{1,0:T(8,128)} %get-tuple-element.29.sin_ref), custom_call_target="tpu_custom_call" | custom-call | flops 10485760 | bytes 3145728 | tf_op jit(solution)/shard_map/pallas_call | solution.py:60
  223.0 2.7 collective-permute-done.12
  225.6 1.4 pad_maximum_fusion.2.k_ref.v_ref
  227.0 8.1 %shard_map.57 = bf16[512,512]{1,0:T(8,128)(2,1)S(1)} custom-call(s32[1]{0:T(128)} %bitcast.base_ref, bf16[1024,512]{1,0:T(8,128)(2,1)S(1)} %copy-done, bf16[2048,512]{1,0:T(8,128)(2,1)S(1)} %pad_maximum_fusion.2.k_ref.v_ref, bf16[2048,512]{1,0:T(8,128)(2,1)S(1)} %pad_maximum_fusion.2.k_ref.v_ref), custom_call_target="tpu_custom_call" | custom-call | flops 1342177280 | bytes 5242880 | tf_op jit(solution)/shard_map/pallas_call | solution.py:105
  235.1 2.1 collective-permute-start.13
  237.2 1.5 collective-permute-start.14
  238.7 8.1 %shard_map.58 = bf16[512,512]{1,0:T(8,128)(2,1)S(1)} custom-call(s32[1]{0:T(128)} %bitcast.base_ref, bf16[1024,512]{1,0:T(8,128)(2,1)S(1)} %copy-done, bf16[2048,512]{1,0:T(8,128)(2,1)S(1)} %pad_maximum_fusion.2.k_ref.v_ref, bf16[2048,512]{1,0:T(8,128)(2,1)S(1)} %pad_maximum_fusion.2.k_ref.v_ref), custom_call_target="tpu_custom_call" | custom-call | flops 1342177280 | bytes 5242880 | tf_op jit(solution)/shard_map/pallas_call | solution.py:105
  246.8 4.8 %collective-permute-start.19 = (bf16[512,512]{1,0:T(8,128)(2,1)S(1)}, bf16[512,512]{1,0:T(8,128)(2,1)}, u32[]{:S(2)}, u32[]{:S(2)}) collective-permute-start(bf16[512,512]{1,0:T(8,128)(2,1)S(1)} %shard_map.58), channel_id=1, source_target_pairs={{0,1},{1,2},{2,3},{4,5},{5,6},{6,7},{8,9},{9,10},{10,11},{12,13},{... | collective-permute-start | bytes 1572872 | tf_op jit(solution)/shard_map/ppermute | solution.py:146
  253.6 1.3 collective-permute-start.16
  254.9 5.2 %collective-permute-done.19 = bf16[512,512]{1,0:T(8,128)(2,1)} collective-permute-done((bf16[512,512]{1,0:T(8,128)(2,1)S(1)}, bf16[512,512]{1,0:T(8,128)(2,1)}, u32[]{:S(2)}, u32[]{:S(2)}) %collective-permute-start.19) | collective-permute-done | bytes 524320 | tf_op jit(solution)/shard_map/ppermute | solution.py:146
  260.9 2.6 fusion.16
  263.5 2.4 fusion.14
  267.5 1.3 collective-permute-start.22
  269.7 2.0 fusion.10
  273.3 5.4 %collective-permute-done.16 = bf16[512,512]{1,0:T(8,128)(2,1)S(1)} collective-permute-done((bf16[512,512]{1,0:T(8,128)(2,1)S(1)}, bf16[512,512]{1,0:T(8,128)(2,1)S(1)}, u32[]{:S(2)}, u32[]{:S(2)}) %collective-permute-start.16) | collective-permute-done | bytes 524320 | tf_op jit(solution)/shard_map/ppermute | solution.py:147
  278.7 1.3 collective-permute-start.18
  280.7 9.2 %collective-permute-done.22 = bf16[512,512]{1,0:T(8,128)(2,1)S(1)} collective-permute-done((bf16[512,512]{1,0:T(8,128)(2,1)}, bf16[512,512]{1,0:T(8,128)(2,1)S(1)}, u32[]{:S(2)}, u32[]{:S(2)}) %collective-permute-start.22) | collective-permute-done | bytes 524320 | tf_op jit(solution)/shard_map/ppermute | solution.py:147
  290.0 1.3 collective-permute-start.24
  293.1 8.1 %collective-permute-done.18 = bf16[512,512]{1,0:T(8,128)(2,1)S(1)} collective-permute-done((bf16[512,512]{1,0:T(8,128)(2,1)S(1)}, bf16[512,512]{1,0:T(8,128)(2,1)S(1)}, u32[]{:S(2)}, u32[]{:S(2)}) %collective-permute-start.18) | collective-permute-done | bytes 524320 | tf_op jit(solution)/shard_map/ppermute | solution.py:147
  302.2 7.8 %collective-permute-done.24 = bf16[512,512]{1,0:T(8,128)(2,1)S(1)} collective-permute-done((bf16[512,512]{1,0:T(8,128)(2,1)S(1)}, bf16[512,512]{1,0:T(8,128)(2,1)S(1)}, u32[]{:S(2)}, u32[]{:S(2)}) %collective-permute-start.24) | collective-permute-done | bytes 524320 | tf_op jit(solution)/shard_map/ppermute | solution.py:147
  310.9 1.9 pad_maximum_fusion.1
  (53 shorter events, 17.8 us)
Async XLA Ops:
  6.5 136.0 %all-gather.3.cloned.1.call-start = ((), (), s32[]{:S(2)}) async-start(), calls=%async_computation | async-start | bytes 13762560 | tf_op jit(solution)/shard_map/all_gather | solution.py:179
  12.6 1.8 copy-start.3
  12.7 248.2 %all-gather.5.cloned.1.call-start = ((), (), s32[]{:S(2)}) async-start(), calls=%async_computation.1 | async-start | bytes 6881280 | tf_op jit(solution)/shard_map/all_gather | solution.py:195
  14.7 32.9 %collective-permute-start = (bf16[1024,672]{0,1:T(8,128)(2,1)S(1)}, bf16[1024,672]{0,1:T(8,128)(2,1)}, u32[]{:S(2)}, u32[]{:S(2)}) collective-permute-start(bf16[1024,672]{0,1:T(8,128)(2,1)S(1)} %get-tuple-element.22), channel_id=1, source_target_pairs={{0,1},{1,2},{2,3},{4,5},{5,6},{6,7},{8,9},{9,10},{10,11},{12,13},{... | collective-permute-start | bytes 4128776 | tf_op jit(solution)/shard_map/ppermute | solution.py:146
  19.8 32.7 %collective-permute-start.1 = (bf16[1024,672]{0,1:T(8,128)(2,1)S(1)}, bf16[1024,672]{0,1:T(8,128)(2,1)}, u32[]{:S(2)}, u32[]{:S(2)}) collective-permute-start(bf16[1024,672]{0,1:T(8,128)(2,1)S(1)} %get-tuple-element.22), channel_id=1, source_target_pairs={{1,0},{2,1},{3,2},{5,4},{6,5},{7,6},{9,8},{10,9},{11,10},{13,12},{... | collective-permute-start | bytes 4128776 | tf_op jit(solution)/shard_map/ppermute | solution.py:147
  21.1 55.9 %collective-permute-start.2 = (bf16[1024,672]{0,1:T(8,128)(2,1)S(1)}, bf16[1024,672]{0,1:T(8,128)(2,1)}, u32[]{:S(2)}, u32[]{:S(2)}) collective-permute-start(bf16[1024,672]{0,1:T(8,128)(2,1)S(1)} %get-tuple-element.21), channel_id=1, source_target_pairs={{0,1},{1,2},{2,3},{4,5},{5,6},{6,7},{8,9},{9,10},{10,11},{12,13},{... | collective-permute-start | bytes 4128776 | tf_op jit(solution)/shard_map/ppermute | solution.py:146
  26.2 55.8 %collective-permute-start.3 = (bf16[1024,672]{0,1:T(8,128)(2,1)S(1)}, bf16[1024,672]{0,1:T(8,128)(2,1)}, u32[]{:S(2)}, u32[]{:S(2)}) collective-permute-start(bf16[1024,672]{0,1:T(8,128)(2,1)S(1)} %get-tuple-element.21), channel_id=1, source_target_pairs={{1,0},{2,1},{3,2},{5,4},{6,5},{7,6},{9,8},{10,9},{11,10},{13,12},{... | collective-permute-start | bytes 4128776 | tf_op jit(solution)/shard_map/ppermute | solution.py:147
  47.6 39.1 %collective-permute-start.4 = (bf16[1024,672]{0,1:T(8,128)(2,1)}, bf16[1024,672]{0,1:T(8,128)(2,1)S(1)}, u32[]{:S(2)}, u32[]{:S(2)}) collective-permute-start(bf16[1024,672]{0,1:T(8,128)(2,1)} %collective-permute-done), channel_id=1, source_target_pairs={{1,2},{2,3},{5,6},{6,7},{9,10},{10,11},{13,14},{14,15},{17,18},{18... | collective-permute-start | bytes 4128776 | tf_op jit(solution)/shard_map/ppermute | solution.py:146
  52.5 59.0 %collective-permute-start.5 = (bf16[1024,672]{0,1:T(8,128)(2,1)}, bf16[1024,672]{0,1:T(8,128)(2,1)}, u32[]{:S(2)}, u32[]{:S(2)}) collective-permute-start(bf16[1024,672]{0,1:T(8,128)(2,1)} %collective-permute-done.1), channel_id=1, source_target_pairs={{1,0},{2,1},{5,4},{6,5},{9,8},{10,9},{13,12},{14,13},{17,16},{18,1... | collective-permute-start | bytes 4128776 | tf_op jit(solution)/shard_map/ppermute | solution.py:147
  77.0 35.8 %collective-permute-start.6 = (bf16[1024,672]{0,1:T(8,128)(2,1)}, bf16[1024,672]{0,1:T(8,128)(2,1)S(1)}, u32[]{:S(2)}, u32[]{:S(2)}) collective-permute-start(bf16[1024,672]{0,1:T(8,128)(2,1)} %collective-permute-done.2), channel_id=1, source_target_pairs={{1,2},{2,3},{5,6},{6,7},{9,10},{10,11},{13,14},{14,15},{17,18},{18... | collective-permute-start | bytes 4128776 | tf_op jit(solution)/shard_map/ppermute | solution.py:146
  82.0 59.0 %collective-permute-start.7 = (bf16[1024,672]{0,1:T(8,128)(2,1)}, bf16[1024,672]{0,1:T(8,128)(2,1)}, u32[]{:S(2)}, u32[]{:S(2)}) collective-permute-start(bf16[1024,672]{0,1:T(8,128)(2,1)} %collective-permute-done.3), channel_id=1, source_target_pairs={{1,0},{2,1},{5,4},{6,5},{9,8},{10,9},{13,12},{14,13},{17,16},{18,1... | collective-permute-start | bytes 4128776 | tf_op jit(solution)/shard_map/ppermute | solution.py:147
  86.7 93.0 %collective-permute-start.8 = (bf16[1024,672]{0,1:T(8,128)(2,1)S(1)}, bf16[1024,672]{0,1:T(8,128)(2,1)}, u32[]{:S(2)}, u32[]{:S(2)}) collective-permute-start(bf16[1024,672]{0,1:T(8,128)(2,1)S(1)} %collective-permute-done.4), channel_id=1, source_target_pairs={{2,3},{6,7},{10,11},{14,15},{18,19},{22,23},{26,27},{30,31}} | collective-permute-start | bytes 4128776 | tf_op jit(solution)/shard_map/ppermute | solution.py:146
  111.5 68.1 %collective-permute-start.9 = (bf16[1024,672]{0,1:T(8,128)(2,1)}, bf16[1024,672]{0,1:T(8,128)(2,1)}, u32[]{:S(2)}, u32[]{:S(2)}) collective-permute-start(bf16[1024,672]{0,1:T(8,128)(2,1)} %collective-permute-done.5), channel_id=1, source_target_pairs={{1,0},{5,4},{9,8},{13,12},{17,16},{21,20},{25,24},{29,28}} | collective-permute-start | bytes 4128776 | tf_op jit(solution)/shard_map/ppermute | solution.py:147
  112.8 72.9 %collective-permute-start.10 = (bf16[1024,672]{0,1:T(8,128)(2,1)S(1)}, bf16[1024,672]{0,1:T(8,128)(2,1)}, u32[]{:S(2)}, u32[]{:S(2)}) collective-permute-start(bf16[1024,672]{0,1:T(8,128)(2,1)S(1)} %collective-permute-done.6), channel_id=1, source_target_pairs={{2,3},{6,7},{10,11},{14,15},{18,19},{22,23},{26,27},{30,31}} | collective-permute-start | bytes 4128776 | tf_op jit(solution)/shard_map/ppermute | solution.py:146
  141.0 59.0 %collective-permute-start.11 = (bf16[1024,672]{0,1:T(8,128)(2,1)}, bf16[1024,672]{0,1:T(8,128)(2,1)}, u32[]{:S(2)}, u32[]{:S(2)}) collective-permute-start(bf16[1024,672]{0,1:T(8,128)(2,1)} %collective-permute-done.7), channel_id=1, source_target_pairs={{1,0},{5,4},{9,8},{13,12},{17,16},{21,20},{25,24},{29,28}} | collective-permute-start | bytes 4128776 | tf_op jit(solution)/shard_map/ppermute | solution.py:147
  142.5 8.6 %copy-start.5 = (bf16[5376,1024]{1,0:T(8,128)(2,1)S(1)}, bf16[5376,1024]{1,0:T(8,128)(2,1)}, u32[]{:S(2)}) copy-start(bf16[5376,1024]{1,0:T(8,128)(2,1)} %all-gather.3.cloned.1.call-done) | copy-start | bytes 33030148
  160.7 2.6 copy-start.4
  208.7 16.9 %collective-permute-start.12 = (bf16[1024,512]{1,0:T(8,128)(2,1)}, bf16[1024,512]{1,0:T(8,128)(2,1)}, u32[]{:S(2)}, u32[]{:S(2)}) collective-permute-start(bf16[1024,512]{1,0:T(8,128)(2,1)} %shard_map.56), channel_id=1, source_target_pairs={{0,4},{4,8},{8,12},{1,5},{5,9},{9,13},{2,6},{6,10},{10,14},{3,7},{... | collective-permute-start | bytes 3145736 | tf_op jit(solution)/shard_map/ppermute | solution.py:26
  218.0 7.7 %copy-start.2 = (bf16[1024,512]{1,0:T(8,128)(2,1)S(1)}, bf16[1024,512]{1,0:T(8,128)(2,1)}, u32[]{:S(2)}) copy-start(bf16[1024,512]{1,0:T(8,128)(2,1)} %shard_map.56) | copy-start | bytes 3145732
  223.0 4.0 %copy-start = (bf16[1024,512]{1,0:T(8,128)(2,1)S(1)}, bf16[1024,512]{1,0:T(8,128)(2,1)}, u32[]{:S(2)}) copy-start(bf16[1024,512]{1,0:T(8,128)(2,1)} %shard_map.55.q_ref) | copy-start | bytes 3145732
  235.1 17.8 %collective-permute-start.13 = (bf16[512,512]{1,0:T(8,128)(2,1)S(1)}, bf16[512,512]{1,0:T(8,128)(2,1)}, u32[]{:S(2)}, u32[]{:S(2)}) collective-permute-start(bf16[512,512]{1,0:T(8,128)(2,1)S(1)} %shard_map.57), channel_id=1, source_target_pairs={{0,1},{1,2},{2,3},{4,5},{5,6},{6,7},{8,9},{9,10},{10,11},{12,13},{... | collective-permute-start | bytes 1572872 | tf_op jit(solution)/shard_map/ppermute | solution.py:146
  237.2 16.4 %collective-permute-start.14 = (bf16[512,512]{1,0:T(8,128)(2,1)S(1)}, bf16[512,512]{1,0:T(8,128)(2,1)S(1)}, u32[]{:S(2)}, u32[]{:S(2)}) collective-permute-start(bf16[512,512]{1,0:T(8,128)(2,1)S(1)} %shard_map.57), channel_id=1, source_target_pairs={{1,0},{2,1},{3,2},{5,4},{6,5},{7,6},{9,8},{10,9},{11,10},{13,12},{... | collective-permute-start | bytes 1572872 | tf_op jit(solution)/shard_map/ppermute | solution.py:147
  246.8 13.3 %collective-permute-start.19 = (bf16[512,512]{1,0:T(8,128)(2,1)S(1)}, bf16[512,512]{1,0:T(8,128)(2,1)}, u32[]{:S(2)}, u32[]{:S(2)}) collective-permute-start(bf16[512,512]{1,0:T(8,128)(2,1)S(1)} %shard_map.58), channel_id=1, source_target_pairs={{0,1},{1,2},{2,3},{4,5},{5,6},{6,7},{8,9},{9,10},{10,11},{12,13},{... | collective-permute-start | bytes 1572872 | tf_op jit(solution)/shard_map/ppermute | solution.py:146
  251.6 15.9 %collective-permute-start.20 = (bf16[512,512]{1,0:T(8,128)(2,1)S(1)}, bf16[512,512]{1,0:T(8,128)(2,1)}, u32[]{:S(2)}, u32[]{:S(2)}) collective-permute-start(bf16[512,512]{1,0:T(8,128)(2,1)S(1)} %shard_map.58), channel_id=1, source_target_pairs={{1,0},{2,1},{3,2},{5,4},{6,5},{7,6},{9,8},{10,9},{11,10},{13,12},{... | collective-permute-start | bytes 1572872 | tf_op jit(solution)/shard_map/ppermute | solution.py:147
  252.9 19.7 %collective-permute-start.15 = (bf16[512,512]{1,0:T(8,128)(2,1)}, bf16[512,512]{1,0:T(8,128)(2,1)S(1)}, u32[]{:S(2)}, u32[]{:S(2)}) collective-permute-start(bf16[512,512]{1,0:T(8,128)(2,1)} %collective-permute-done.13), channel_id=1, source_target_pairs={{1,2},{2,3},{5,6},{6,7},{9,10},{10,11},{13,14},{14,15},{17,18},{18... | collective-permute-start | bytes 1572872 | tf_op jit(solution)/shard_map/ppermute | solution.py:146
  253.6 25.1 %collective-permute-start.16 = (bf16[512,512]{1,0:T(8,128)(2,1)S(1)}, bf16[512,512]{1,0:T(8,128)(2,1)S(1)}, u32[]{:S(2)}, u32[]{:S(2)}) collective-permute-start(bf16[512,512]{1,0:T(8,128)(2,1)S(1)} %collective-permute-done.14), channel_id=1, source_target_pairs={{1,0},{2,1},{5,4},{6,5},{9,8},{10,9},{13,12},{14,13},{17,16},{18,1... | collective-permute-start | bytes 1572872 | tf_op jit(solution)/shard_map/ppermute | solution.py:147
  260.2 19.9 %collective-permute-start.21 = (bf16[512,512]{1,0:T(8,128)(2,1)}, bf16[512,512]{1,0:T(8,128)(2,1)S(1)}, u32[]{:S(2)}, u32[]{:S(2)}) collective-permute-start(bf16[512,512]{1,0:T(8,128)(2,1)} %collective-permute-done.19), channel_id=1, source_target_pairs={{1,2},{2,3},{5,6},{6,7},{9,10},{10,11},{13,14},{14,15},{17,18},{18... | collective-permute-start | bytes 1572872 | tf_op jit(solution)/shard_map/ppermute | solution.py:146
  260.9 5.0 %copy-start.1 = (bf16[2048,1344]{0,1:T(8,128)(2,1)S(1)}, bf16[2048,1344]{0,1:T(8,128)(2,1)}, u32[]{:S(2)}) copy-start(bf16[2048,1344]{0,1:T(8,128)(2,1)} %all-gather.5.cloned.1.call-done) | copy-start | bytes 16515076
  267.5 22.5 %collective-permute-start.22 = (bf16[512,512]{1,0:T(8,128)(2,1)}, bf16[512,512]{1,0:T(8,128)(2,1)S(1)}, u32[]{:S(2)}, u32[]{:S(2)}) collective-permute-start(bf16[512,512]{1,0:T(8,128)(2,1)} %collective-permute-done.20), channel_id=1, source_target_pairs={{1,0},{2,1},{5,4},{6,5},{9,8},{10,9},{13,12},{14,13},{17,16},{18,1... | collective-permute-start | bytes 1572872 | tf_op jit(solution)/shard_map/ppermute | solution.py:147
  272.6 20.5 %collective-permute-start.17 = (bf16[512,512]{1,0:T(8,128)(2,1)S(1)}, bf16[512,512]{1,0:T(8,128)(2,1)S(1)}, u32[]{:S(2)}, u32[]{:S(2)}) collective-permute-start(bf16[512,512]{1,0:T(8,128)(2,1)S(1)} %collective-permute-done.15), channel_id=1, source_target_pairs={{2,3},{6,7},{10,11},{14,15},{18,19},{22,23},{26,27},{30,31}} | collective-permute-start | bytes 1572872 | tf_op jit(solution)/shard_map/ppermute | solution.py:146
  278.7 22.5 %collective-permute-start.18 = (bf16[512,512]{1,0:T(8,128)(2,1)S(1)}, bf16[512,512]{1,0:T(8,128)(2,1)S(1)}, u32[]{:S(2)}, u32[]{:S(2)}) collective-permute-start(bf16[512,512]{1,0:T(8,128)(2,1)S(1)} %collective-permute-done.16), channel_id=1, source_target_pairs={{1,0},{5,4},{9,8},{13,12},{17,16},{21,20},{25,24},{29,28}} | collective-permute-start | bytes 1572872 | tf_op jit(solution)/shard_map/ppermute | solution.py:147
  280.0 22.1 %collective-permute-start.23 = (bf16[512,512]{1,0:T(8,128)(2,1)S(1)}, bf16[512,512]{1,0:T(8,128)(2,1)S(1)}, u32[]{:S(2)}, u32[]{:S(2)}) collective-permute-start(bf16[512,512]{1,0:T(8,128)(2,1)S(1)} %collective-permute-done.21), channel_id=1, source_target_pairs={{2,3},{6,7},{10,11},{14,15},{18,19},{22,23},{26,27},{30,31}} | collective-permute-start | bytes 1572872 | tf_op jit(solution)/shard_map/ppermute | solution.py:146
  290.0 20.0 %collective-permute-start.24 = (bf16[512,512]{1,0:T(8,128)(2,1)S(1)}, bf16[512,512]{1,0:T(8,128)(2,1)S(1)}, u32[]{:S(2)}, u32[]{:S(2)}) collective-permute-start(bf16[512,512]{1,0:T(8,128)(2,1)S(1)} %collective-permute-done.22), channel_id=1, source_target_pairs={{1,0},{5,4},{9,8},{13,12},{17,16},{21,20},{25,24},{29,28}} | collective-permute-start | bytes 1572872 | tf_op jit(solution)/shard_map/ppermute | solution.py:147
Sparse Core Ops, SparseCore 0:
  12.8 75.6 all-gather.2
  90.1 41.9 all-gather.4

commit v3 on v2

--- a/solution.py
+++ b/solution.py
@@ -17,7 +17,6 @@
 SCALE = 168.0 ** (-0.5)
 ROPE_BASE = 10000.0
 PIECES = 2
-CHUNKS = 2
 
 
 def from_behind(value, axis, steps):
@@ -74,30 +73,55 @@
     )(values, gain.reshape(1, HD), cosine, sine)
 
 
-def attend_kernel(q_tile, row0, base_ref, q_ref, k_ref, v_ref, o_ref):
+def attend_kernel(q_tile, row0, base_ref, q_ref, gain_ref, cos_ref, sin_ref, k_ref, v_ref, o_ref):
     first = row0 + pl.program_id(1) * q_tile
-    span = q_tile + WINDOW
-    keys = k_ref[pl.ds(pl.multiple_of(first, q_tile), span), :]
-    values = v_ref[pl.ds(pl.multiple_of(first, q_tile), span), :]
-    row = lax.broadcasted_iota(jnp.int32, (q_tile, span), 0)
-    column = lax.broadcasted_iota(jnp.int32, (q_tile, span), 1)
-    least = jnp.maximum(row, WINDOW - 1 - (base_ref[0] + first))
-    keep = (column > least) & (column <= row + WINDOW)
+    parts = ((0, q_tile), (q_tile, WINDOW - q_tile), (WINDOW, q_tile))
+    slices = [pl.ds(pl.multiple_of(first + start, q_tile), width) for start, width in parts]
+    row = lax.broadcasted_iota(jnp.int32, (q_tile, q_tile), 0)
+    column = lax.broadcasted_iota(jnp.int32, (q_tile, q_tile), 1)
+    before = WINDOW - 1 - (base_ref[0] + first)
+    low_keep = column > jnp.maximum(row, before)
+    high_keep = column <= row
+    middle = lax.broadcasted_iota(jnp.int32, (1, parts[1][1]), 1) + q_tile
+    middle_bias = jnp.where(middle > before, jnp.float32(0.0), jnp.float32(-1e30))
+    gain, cosine, sine = gain_ref[...], cos_ref[...], sin_ref[...]
     for member in range(GROUP):
         columns = slice(member * HD, (member + 1) * HD)
-        scores = lax.dot_general(
-            q_ref[:, columns], keys, (((1,), (1,)), ((), ())), preferred_element_type=jnp.float32
-        )
-        masked = jnp.where(keep, scores, jnp.float32(-1e30))
-        top = jnp.max(masked, axis=-1, keepdims=True)
-        expo = jnp.exp2((masked - top) * jnp.float32(SCALE * math.log2(math.e)))
-        total = jnp.sum(expo, axis=-1, keepdims=True)
-        weights = (expo * (1.0 / total)).astype(jnp.bfloat16)
-        result = jnp.dot(weights, values, preferred_element_type=jnp.float32)
+        vectors = q_ref[:, columns]
+        meansq = jnp.mean(vectors * vectors, axis=-1, keepdims=True)
+        vectors = vectors * lax.rsqrt(meansq + EPS) * gain
+        vectors = vectors * cosine + pltpu.roll(vectors, HD // 2, 1) * sine
+        query = vectors.astype(jnp.bfloat16)
+        low, mid, high = [
+            lax.dot_general(
+                query, k_ref[at, :], (((1,), (1,)), ((), ())), preferred_element_type=jnp.float32
+            )
+            for at in slices
+        ]
+        masked = [
+            jnp.where(low_keep, low, jnp.float32(-1e30)),
+            mid + middle_bias,
+            jnp.where(high_keep, high, jnp.float32(-1e30)),
+        ]
+        tops = [jnp.max(part, axis=-1, keepdims=True) for part in masked]
+        top = jnp.maximum(jnp.maximum(tops[0], tops[1]), tops[2])
+        expo = [
+            jnp.exp2((part - top) * jnp.float32(SCALE * math.log2(math.e))) for part in masked
+        ]
+        sums = [jnp.sum(part, axis=-1, keepdims=True) for part in expo]
+        inverse = 1.0 / (sums[0] + sums[1] + sums[2])
+        result = None
+        for part, at in zip(expo, slices):
+            term = jnp.dot(
+                (part * inverse).astype(jnp.bfloat16),
+                v_ref[at, :],
+                preferred_element_type=jnp.float32,
+            )
+            result = term if result is None else result + term
         o_ref[:, columns] = result.astype(o_ref.dtype)
 
 
-def attend(query, paired, base, row0, count):
+def attend(query, gain, cosine, sine, paired, base, row0, count):
     kv_local = query.shape[1] // (GROUP * HD)
     q_tile = 256
     from_tile = row0 // q_tile
@@ -109,6 +133,9 @@
         in_specs=[
             pl.BlockSpec(memory_space=pltpu.SMEM),
             pl.BlockSpec((q_tile, GROUP * HD), lambda h, i: (from_tile + i, h)),
+            pl.BlockSpec((1, HD), lambda h, i: (0, 0)),
+            pl.BlockSpec((q_tile, HD), lambda h, i: (from_tile + i, 0)),
+            pl.BlockSpec((q_tile, HD), lambda h, i: (from_tile + i, 0)),
             pl.BlockSpec((whole, HD), lambda h, i: (0, 2 * h)),
             pl.BlockSpec((whole, HD), lambda h, i: (0, 2 * h + 1)),
         ],
@@ -119,10 +146,23 @@
             bytes_accessed=4 * (whole + count) * query.shape[1],
             transcendentals=count * query.shape[1] // HD * (WINDOW + q_tile),
         ),
-    )(base.reshape(1), query, paired, paired)
-
-
-def line_gather_dot(pieces, weight, axis, depth, column_ranges):
+    )(base.reshape(1), query, gain.reshape(1, HD), cosine, sine, paired, paired)
+
+
+def line_hops(pieces, axis):
+    count = lax.axis_size(axis)
+    hops = []
+    ups = downs = [piece for piece, _ in pieces]
+    for step in range(1, count):
+        upward = [(i, i + 1) for i in range(step - 1, count - 1)]
+        downward = [(i + 1, i) for i in range(count - step)]
+        ups = [lax.ppermute(up, axis, upward) for up in ups]
+        downs = [lax.ppermute(down, axis, downward) for down in downs]
+        hops.append(list(zip(ups, downs)))
+    return hops
+
+
+def line_gather_dot(pieces, hops, weight, axis, depth, column_ranges):
     count = lax.axis_size(axis)
     here = lax.axis_index(axis)
 
@@ -137,19 +177,14 @@
         return out
 
     totals = [None] * len(column_ranges)
-    ups = [piece for piece, _ in pieces]
-    downs = list(ups)
     for piece, first in pieces:
         totals = terms(totals, piece, here, first)
     for step in range(1, count):
-        for at, (_, first) in enumerate(pieces):
-            up = lax.ppermute(ups[at], axis, [(i, i + 1) for i in range(step - 1, count - 1)])
-            down = lax.ppermute(downs[at], axis, [(i + 1, i) for i in range(count - step)])
-            ups[at], downs[at] = up, down
+        below = jnp.maximum(here - step, 0)
+        above = jnp.minimum(here + step, count - 1)
+        for (up, down), (_, first) in zip(hops[step - 1], pieces):
             if step == count - 1 and len(totals) > 1:
                 totals, up, down = lax.optimization_barrier((totals, up, down))
-            below = jnp.maximum(here - step, 0)
-            above = jnp.minimum(here + step, count - 1)
             if 2 * step < count:
                 totals = terms(totals, up, below, first)
                 totals = terms(totals, down, above, first)
@@ -169,6 +204,10 @@
     kv_local = w_qkv.shape[1]
     q_columns = kv_local * GROUP * HD
     kv_columns = kv_local * 2 * HD
+    part = depth // PIECES
+    pieces = [(states[:, i * part : (i + 1) * part], i * part) for i in range(PIECES)]
+    hops = line_hops(pieces, "hid")
+    out_whole = lax.all_gather(w_out, "tok", axis=0, tiled=True)
     arranged = jnp.concatenate(
         [
             w_qkv[:, :, : GROUP * HD].reshape(-1, q_columns),
@@ -177,9 +216,9 @@
         axis=1,
     )
     weight_whole = lax.all_gather(arranged, "tok", axis=0, tiled=True)
-    part = depth // PIECES
     kv, query = line_gather_dot(
-        [(states[:, i * part : (i + 1) * part], i * part) for i in range(PIECES)],
+        pieces,
+        hops,
         weight_whole,
         "hid",
         depth,
@@ -189,15 +228,18 @@
     cosine, sine = rope_tables(rows, base)
     paired = norm_rope(kv, k_gain, cosine, sine, 1, 2)
     behind = from_behind(paired[rows - WINDOW :], "tok", 1)
-    query = norm_rope(query, q_gain, cosine, sine, 1, 1)
     combined = jnp.concatenate([behind, paired], axis=0)
-    block = rows // CHUNKS
-    out_whole = lax.all_gather(w_out, "tok", axis=0, tiled=True)
     results = []
-    for index in range(CHUNKS):
-        heads = attend(query, combined, base, index * block, block)
+    quarter = rows // 4
+    for row0, count in ((0, quarter), (quarter, quarter), (2 * quarter, rows - 2 * quarter)):
+        heads = attend(query, q_gain, cosine, sine, combined, base, row0, count)
         (summed,) = line_gather_dot(
-            [(heads, 0)], out_whole, "hid", heads.shape[1], [(0, w_out.shape[1])]
+            [(heads, 0)],
+            line_hops([(heads, 0)], "hid"),
+            out_whole,
+            "hid",
+            heads.shape[1],
+            [(0, w_out.shape[1])],
         )
         results.append(summed.astype(jnp.bfloat16))
     return jnp.concatenate(results, axis=0)

time: 326 us -> 334 us (1.025)
  starting transfers between devices: 45.7 us -> 54.6 us
  matrix products: 60.7 us -> 64.5 us
    ppermute x24 -> x30, starting transfers between devices: 40.8 us -> 49.7 us  [the longest x15 30.1 us: line_hops(): ups = [lax.ppermute(up, axis, upward) for up in ups]]
    ppermute x24 -> x30, waiting for transfers between devices: 152 us -> 145 us  [the longest x15 102 us: line_hops(): downs = [lax.ppermute(down, axis, downward) for down in downs]]
    ppermute x1, waiting for transfers between devices: 2.66 us -> 8.92 us  [from_behind(): lax.ppermute(value, axis, [(source, source + steps) for source in range(f...]
    pallas_call x2 -> x1, Pallas kernels: 9.37 us -> 4.33 us  [norm_rope(): pl.pallas_call(functools.partial(norm_rope_kernel, rotated, total), out_s...]
    dot_general x30 -> x35, matrix products: 60.7 us -> 64.5 us  [terms(): term = jnp.dot(piece, rows, preferred_element_type=jnp.float32)]
    pallas_call x2 -> x3, Pallas kernels: 16.2 us -> 17.9 us  [attend(): pl.pallas_call(functools.partial(attend_kernel, q_tile, row0), out_shape=...]
  transfers between devices with their start and end apart: 27 -> 33, of which waited for: 14 -> 13; matrix products, arithmetic and copies ran while one was open for 22% -> 21% of each run, Pallas kernels for 8% -> 7%
where the time goes in v3:
time: 334 us; the launch traced here: 328 us
  waiting for transfers between devices  154 us (46%)
  matrix products  64.5 us (19%)
  starting transfers between devices  54.6 us (16%)
  Pallas kernels  22.2 us (7%)
  between operations  14.4 us (4%)
  other arithmetic  10.4 us (3%)
  local copies, waits for them, and re-layouts  7.8 us (2%)
    ppermute x15, waiting for transfers between devices, line_hops(): downs = [lax.ppermute(down, axis, downward) for down in downs]  102 us
    dot_general x35, matrix products, terms(): term = jnp.dot(piece, rows, preferred_element_type=jnp.float32)  64.5 us
    ppermute x15, waiting for transfers between devices, line_hops(): ups = [lax.ppermute(up, axis, upward) for up in ups]  43.3 us
    ppermute x15, starting transfers between devices, line_hops(): ups = [lax.ppermute(up, axis, upward) for up in ups]  30.1 us
    ppermute x15, starting transfers between devices, line_hops(): downs = [lax.ppermute(down, axis, downward) for down in downs]  19.6 us
    pallas_call x3, Pallas kernels, attend(): pl.pallas_call(functools.partial(attend_kernel, q_tile, row0), out_shape=...  17.9 us
    ppermute x1, waiting for transfers between devices, from_behind(): lax.ppermute(value, axis, [(source, source + steps) for source in range(f...  8.92 us
  transfers between devices with their start and end apart: 33, of which 13 were waited for; matrix products, arithmetic and copies ran while one was open for 21% of the time, Pallas kernels for 7%

profile of v3, /device:TPU:1, one launch (start us, length us, event | category | flops | bytes accessed | tf_op | source)
XLA Modules:
  0.0 328.2 jit_solution(7821909765960589625)
XLA Ops:
  6.5 3.6 %fusion.126 = (bf16[1344,2,256]{2,1,0:T(2,128)(2,1)S(1)}, bf16[1344,2,256]{2,1,0:T(2,128)(2,1)S(1)}) fusion(bf16[1344,2,512]{2,1,0:T(2,128)(2,1)} %param.6), kind=kLoop, calls=%fused_computation.146 | loop fusion | bytes 5505024 | tf_op jit(solution)/shard_map/slice | solution.py:213
  10.8 1.9 pad_maximum_fusion
  12.7 1.7 copy-done.7
  14.7 5.1 %collective-permute-start = (bf16[1024,672]{0,1:T(8,128)(2,1)S(1)}, bf16[1024,672]{0,1:T(8,128)(2,1)}, u32[]{:S(2)}, u32[]{:S(2)}) collective-permute-start(bf16[1024,672]{0,1:T(8,128)(2,1)S(1)} %get-tuple-element.22), channel_id=1, source_target_pairs={{0,1},{1,2},{2,3},{4,5},{5,6},{6,7},{8,9},{9,10},{10,11},{12,13},{... | collective-permute-start | bytes 4128776 | tf_op jit(solution)/shard_map/ppermute | solution.py:159
  21.1 5.1 %collective-permute-start.2 = (bf16[1024,672]{0,1:T(8,128)(2,1)S(1)}, bf16[1024,672]{0,1:T(8,128)(2,1)}, u32[]{:S(2)}, u32[]{:S(2)}) collective-permute-start(bf16[1024,672]{0,1:T(8,128)(2,1)S(1)} %get-tuple-element.21), channel_id=1, source_target_pairs={{0,1},{1,2},{2,3},{4,5},{5,6},{6,7},{8,9},{9,10},{10,11},{12,13},{... | collective-permute-start | bytes 4128776 | tf_op jit(solution)/shard_map/ppermute | solution.py:159
  27.5 20.1 %collective-permute-done = bf16[1024,672]{0,1:T(8,128)(2,1)} collective-permute-done((bf16[1024,672]{0,1:T(8,128)(2,1)S(1)}, bf16[1024,672]{0,1:T(8,128)(2,1)}, u32[]{:S(2)}, u32[]{:S(2)}) %collective-permute-start) | collective-permute-done | bytes 1376288 | tf_op jit(solution)/shard_map/ppermute | solution.py:159
  48.3 4.2 %collective-permute-done.1 = bf16[1024,672]{0,1:T(8,128)(2,1)} collective-permute-done((bf16[1024,672]{0,1:T(8,128)(2,1)S(1)}, bf16[1024,672]{0,1:T(8,128)(2,1)}, u32[]{:S(2)}, u32[]{:S(2)}) %collective-permute-start.1) | collective-permute-done | bytes 1376288 | tf_op jit(solution)/shard_map/ppermute | solution.py:160
  53.8 23.2 %collective-permute-done.2 = bf16[1024,672]{0,1:T(8,128)(2,1)} collective-permute-done((bf16[1024,672]{0,1:T(8,128)(2,1)S(1)}, bf16[1024,672]{0,1:T(8,128)(2,1)}, u32[]{:S(2)}, u32[]{:S(2)}) %collective-permute-start.2) | collective-permute-done | bytes 1376288 | tf_op jit(solution)/shard_map/ppermute | solution.py:159
  77.8 4.2 %collective-permute-done.3 = bf16[1024,672]{0,1:T(8,128)(2,1)} collective-permute-done((bf16[1024,672]{0,1:T(8,128)(2,1)S(1)}, bf16[1024,672]{0,1:T(8,128)(2,1)}, u32[]{:S(2)}, u32[]{:S(2)}) %collective-permute-start.3) | collective-permute-done | bytes 1376288 | tf_op jit(solution)/shard_map/ppermute | solution.py:160
  83.4 1.9 fusion.85
  85.3 1.3 pad_maximum_fusion.3
  86.7 1.8 collective-permute-start.8
  88.4 23.1 %collective-permute-done.5 = bf16[1024,672]{0,1:T(8,128)(2,1)} collective-permute-done((bf16[1024,672]{0,1:T(8,128)(2,1)}, bf16[1024,672]{0,1:T(8,128)(2,1)}, u32[]{:S(2)}, u32[]{:S(2)}) %collective-permute-start.5) | collective-permute-done | bytes 1376288 | tf_op jit(solution)/shard_map/ppermute | solution.py:160
  112.8 1.9 collective-permute-start.10
  114.7 26.3 %collective-permute-done.7 = bf16[1024,672]{0,1:T(8,128)(2,1)} collective-permute-done((bf16[1024,672]{0,1:T(8,128)(2,1)}, bf16[1024,672]{0,1:T(8,128)(2,1)}, u32[]{:S(2)}, u32[]{:S(2)}) %collective-permute-start.7) | collective-permute-done | bytes 1376288 | tf_op jit(solution)/shard_map/ppermute | solution.py:160
  141.0 1.5 collective-permute-start.11
  142.5 2.7 fusion.43
  145.2 3.2 fusion.61
  148.5 2.6 fusion.45
  151.1 2.4 fusion.63
  153.5 2.4 fusion.47
  155.9 2.4 fusion.65
  158.2 2.4 fusion.49
  160.7 2.5 fusion.67
  166.3 2.4 fusion.41
  168.7 3.4 %fusion.6 = f32[1024,512]{1,0:T(8,128)S(1)} fusion(f32[1024,512]{1,0:T(8,128)S(1)} %fusion.41, f32[512,1024]{0,1:T(8,128)S(1)} %fusion.43, f32[512,1024]{0,1:T(8,128)S(1)} %fusion.45, f32[512,1024]{0,1:T(8,128)S(1)} %fusion.47, f32[512,1024]{0,1:T(8,128)S(1)} %fusion.49, f32[512,1024]{0,1:T(8,128)S(1)} %fusion.53, f32[512,1024]{0,1:T(8,128)S(1)} %fusion.51, ...), kind=kOutput, calls=%fused_computation.19 | convolution fusion | flops 709001216 | bytes 20217860 | tf_op jit(solution)/shard_map/dot_general | solution.py:175
  172.1 2.1 fusion.71
  174.3 2.6 fusion.59
  176.8 3.0 fusion.7
  179.8 2.6 fusion.33
  182.9 2.6 fusion.35
  185.9 14.1 %collective-permute-done.11 = bf16[1024,672]{0,1:T(8,128)(2,1)} collective-permute-done((bf16[1024,672]{0,1:T(8,128)(2,1)}, bf16[1024,672]{0,1:T(8,128)(2,1)}, u32[]{:S(2)}, u32[]{:S(2)}) %collective-permute-start.11) | collective-permute-done | bytes 1376288 | tf_op jit(solution)/shard_map/ppermute | solution.py:160
  200.0 2.5 fusion.29
  202.5 1.8 add.267.x_ref
  204.3 4.3 %shard_map.55 = bf16[1024,512]{1,0:T(8,128)(2,1)} custom-call(f32[1024,512]{1,0:T(8,128)} %add.267.x_ref, f32[1,128]{1,0:T(1,128)} %bitcast.39, f32[1024,128]{1,0:T(8,128)} %get-tuple-element.28.cos_ref, f32[1024,128]{1,0:T(8,128)} %get-tuple-element.29.sin_ref), custom_call_target="tpu_custom_call" | custom-call | flops 10485760 | bytes 3145728 | tf_op jit(solution)/shard_map/pallas_call | solution.py:59
  208.7 4.9 %collective-permute-start.12 = (bf16[1024,512]{1,0:T(8,128)(2,1)}, bf16[1024,512]{1,0:T(8,128)(2,1)S(1)}, u32[]{:S(2)}, u32[]{:S(2)}) collective-permute-start(bf16[1024,512]{1,0:T(8,128)(2,1)} %shard_map.55), channel_id=1, source_target_pairs={{0,4},{4,8},{8,12},{1,5},{5,9},{9,13},{2,6},{6,10},{10,14},{3,7},{... | collective-permute-start | bytes 3145736 | tf_op jit(solution)/shard_map/ppermute | solution.py:25
  213.5 2.6 fusion.31
  216.7 8.9 %collective-permute-done.12 = bf16[1024,512]{1,0:T(8,128)(2,1)S(1)} collective-permute-done((bf16[1024,512]{1,0:T(8,128)(2,1)}, bf16[1024,512]{1,0:T(8,128)(2,1)S(1)}, u32[]{:S(2)}, u32[]{:S(2)}) %collective-permute-start.12) | collective-permute-done | bytes 1048608 | tf_op jit(solution)/shard_map/ppermute | solution.py:25
  225.8 4.3 %shard_map.56 = bf16[256,512]{1,0:T(8,128)(2,1)S(1)} custom-call(s32[1]{0:T(128)} %bitcast.base_ref, f32[1024,512]{1,0:T(8,128)S(1)} %add.264.q_ref, f32[1,128]{1,0:T(1,128)S(1)} %bitcast.32, f32[1024,128]{1,0:T(8,128)S(1)} %copy-done.2, f32[1024,128]{1,0:T(8,128)S(1)} %copy-done.3, bf16[2048,512]{1,0:T(8,128)(2,1)S(1)} %pad_maximum_fusion.2.k_ref.v_ref, ...), custom_call_target="tpu_custom_call" | custom-call | flops 671088640 | bytes 4718592 | tf_op jit(solution)/shard_map/pallas_call | solution.py:129
  230.0 2.0 collective-permute-start.13
  232.0 1.5 collective-permute-start.14
  233.5 1.6 copy-done.1
  235.1 4.9 %shard_map.57 = bf16[256,512]{1,0:T(8,128)(2,1)} custom-call(s32[1]{0:T(128)} %bitcast.base_ref, f32[1024,512]{1,0:T(8,128)S(1)} %copy-done.1, f32[1,128]{1,0:T(1,128)S(1)} %bitcast.33, f32[1024,128]{1,0:T(8,128)S(1)} %copy-done.2, f32[1024,128]{1,0:T(8,128)S(1)} %copy-done.3, bf16[2048,512]{1,0:T(8,128)(2,1)S(1)} %pad_maximum_fusion.2.k_ref.v_ref, ...), custom_call_target="tpu_custom_call" | custom-call | flops 671088640 | bytes 4718592 | tf_op jit(solution)/shard_map/pallas_call | solution.py:129
  240.0 4.7 %collective-permute-start.19 = (bf16[256,512]{1,0:T(8,128)(2,1)}, bf16[256,512]{1,0:T(8,128)(2,1)}, u32[]{:S(2)}, u32[]{:S(2)}) collective-permute-start(bf16[256,512]{1,0:T(8,128)(2,1)} %shard_map.57), channel_id=1, source_target_pairs={{0,1},{1,2},{2,3},{4,5},{5,6},{6,7},{8,9},{9,10},{10,11},{12,13},{... | collective-permute-start | bytes 786440 | tf_op jit(solution)/shard_map/ppermute | solution.py:159
  245.9 8.7 %shard_map.58 = bf16[512,512]{1,0:T(8,128)(2,1)} custom-call(s32[1]{0:T(128)} %bitcast.base_ref, f32[1024,512]{1,0:T(8,128)S(1)} %copy-done.1, f32[1,128]{1,0:T(1,128)S(1)} %bitcast.34, f32[1024,128]{1,0:T(8,128)S(1)} %copy-done.2, f32[1024,128]{1,0:T(8,128)S(1)} %copy-done.3, bf16[2048,512]{1,0:T(8,128)(2,1)S(1)} %pad_maximum_fusion.2.k_ref.v_ref, ...), custom_call_target="tpu_custom_call" | custom-call | flops 1342177280 | bytes 5242880 | tf_op jit(solution)/shard_map/pallas_call | solution.py:129
  254.6 4.0 %collective-permute-start.25 = (bf16[512,512]{1,0:T(8,128)(2,1)}, bf16[512,512]{1,0:T(8,128)(2,1)S(1)}, u32[]{:S(2)}, u32[]{:S(2)}) collective-permute-start(bf16[512,512]{1,0:T(8,128)(2,1)} %shard_map.58), channel_id=1, source_target_pairs={{0,1},{1,2},{2,3},{4,5},{5,6},{6,7},{8,9},{9,10},{10,11},{12,13},{... | collective-permute-start | bytes 1572872 | tf_op jit(solution)/shard_map/ppermute | solution.py:159
  258.7 1.3 collective-permute-start.26
  260.0 2.1 fusion.24
  262.9 2.0 fusion.18
  265.4 1.3 collective-permute-start.16
  266.7 1.5 fusion.22
  268.9 1.5 fusion.16
  270.5 1.5 fusion.2
  272.0 1.3 collective-permute-start.22
  275.6 1.3 collective-permute-start.18
  277.8 2.0 fusion
  280.4 1.3 collective-permute-start.28
  281.7 5.7 %collective-permute-done.22 = bf16[256,512]{1,0:T(8,128)(2,1)S(1)} collective-permute-done((bf16[256,512]{1,0:T(8,128)(2,1)}, bf16[256,512]{1,0:T(8,128)(2,1)S(1)}, u32[]{:S(2)}, u32[]{:S(2)}) %collective-permute-start.22) | collective-permute-done | bytes 262176 | tf_op jit(solution)/shard_map/ppermute | solution.py:160
  288.7 1.3 collective-permute-start.24
  290.0 3.7 %collective-permute-done.18 = bf16[256,512]{1,0:T(8,128)(2,1)S(1)} collective-permute-done((bf16[256,512]{1,0:T(8,128)(2,1)S(1)}, bf16[256,512]{1,0:T(8,128)(2,1)S(1)}, u32[]{:S(2)}, u32[]{:S(2)}) %collective-permute-start.18) | collective-permute-done | bytes 262176 | tf_op jit(solution)/shard_map/ppermute | solution.py:160
  295.0 10.0 %collective-permute-done.28 = bf16[512,512]{1,0:T(8,128)(2,1)S(1)} collective-permute-done((bf16[512,512]{1,0:T(8,128)(2,1)S(1)}, bf16[512,512]{1,0:T(8,128)(2,1)S(1)}, u32[]{:S(2)}, u32[]{:S(2)}) %collective-permute-start.28) | collective-permute-done | bytes 524320 | tf_op jit(solution)/shard_map/ppermute | solution.py:160
  306.2 4.3 %collective-permute-done.24 = bf16[256,512]{1,0:T(8,128)(2,1)S(1)} collective-permute-done((bf16[256,512]{1,0:T(8,128)(2,1)S(1)}, bf16[256,512]{1,0:T(8,128)(2,1)S(1)}, u32[]{:S(2)}, u32[]{:S(2)}) %collective-permute-start.24) | collective-permute-done | bytes 262176 | tf_op jit(solution)/shard_map/ppermute | solution.py:160
  312.0 6.3 %collective-permute-done.30 = bf16[512,512]{1,0:T(8,128)(2,1)S(1)} collective-permute-done((bf16[512,512]{1,0:T(8,128)(2,1)S(1)}, bf16[512,512]{1,0:T(8,128)(2,1)S(1)}, u32[]{:S(2)}, u32[]{:S(2)}) %collective-permute-start.30) | collective-permute-done | bytes 524320 | tf_op jit(solution)/shard_map/ppermute | solution.py:160
  319.3 1.9 pad_maximum_fusion.1
  (78 shorter events, 26.8 us)
Async XLA Ops:
  6.5 136.0 %all-gather.3.cloned.1.call-start = ((), (), s32[]{:S(2)}) async-start(), calls=%async_computation | async-start | bytes 13762560 | tf_op jit(solution)/shard_map/all_gather | solution.py:218
  12.6 1.8 copy-start.7
  12.7 247.3 %all-gather.5.cloned.1.call-start = ((), (), s32[]{:S(2)}) async-start(), calls=%async_computation.1 | async-start | bytes 6881280 | tf_op jit(solution)/shard_map/all_gather | solution.py:210
  14.7 32.9 %collective-permute-start = (bf16[1024,672]{0,1:T(8,128)(2,1)S(1)}, bf16[1024,672]{0,1:T(8,128)(2,1)}, u32[]{:S(2)}, u32[]{:S(2)}) collective-permute-start(bf16[1024,672]{0,1:T(8,128)(2,1)S(1)} %get-tuple-element.22), channel_id=1, source_target_pairs={{0,1},{1,2},{2,3},{4,5},{5,6},{6,7},{8,9},{9,10},{10,11},{12,13},{... | collective-permute-start | bytes 4128776 | tf_op jit(solution)/shard_map/ppermute | solution.py:159
  19.8 32.7 %collective-permute-start.1 = (bf16[1024,672]{0,1:T(8,128)(2,1)S(1)}, bf16[1024,672]{0,1:T(8,128)(2,1)}, u32[]{:S(2)}, u32[]{:S(2)}) collective-permute-start(bf16[1024,672]{0,1:T(8,128)(2,1)S(1)} %get-tuple-element.22), channel_id=1, source_target_pairs={{1,0},{2,1},{3,2},{5,4},{6,5},{7,6},{9,8},{10,9},{11,10},{13,12},{... | collective-permute-start | bytes 4128776 | tf_op jit(solution)/shard_map/ppermute | solution.py:160
  21.1 55.9 %collective-permute-start.2 = (bf16[1024,672]{0,1:T(8,128)(2,1)S(1)}, bf16[1024,672]{0,1:T(8,128)(2,1)}, u32[]{:S(2)}, u32[]{:S(2)}) collective-permute-start(bf16[1024,672]{0,1:T(8,128)(2,1)S(1)} %get-tuple-element.21), channel_id=1, source_target_pairs={{0,1},{1,2},{2,3},{4,5},{5,6},{6,7},{8,9},{9,10},{10,11},{12,13},{... | collective-permute-start | bytes 4128776 | tf_op jit(solution)/shard_map/ppermute | solution.py:159
  26.2 55.8 %collective-permute-start.3 = (bf16[1024,672]{0,1:T(8,128)(2,1)S(1)}, bf16[1024,672]{0,1:T(8,128)(2,1)}, u32[]{:S(2)}, u32[]{:S(2)}) collective-permute-start(bf16[1024,672]{0,1:T(8,128)(2,1)S(1)} %get-tuple-element.21), channel_id=1, source_target_pairs={{1,0},{2,1},{3,2},{5,4},{6,5},{7,6},{9,8},{10,9},{11,10},{13,12},{... | collective-permute-start | bytes 4128776 | tf_op jit(solution)/shard_map/ppermute | solution.py:160
  47.6 39.1 %collective-permute-start.4 = (bf16[1024,672]{0,1:T(8,128)(2,1)}, bf16[1024,672]{0,1:T(8,128)(2,1)S(1)}, u32[]{:S(2)}, u32[]{:S(2)}) collective-permute-start(bf16[1024,672]{0,1:T(8,128)(2,1)} %collective-permute-done), channel_id=1, source_target_pairs={{1,2},{2,3},{5,6},{6,7},{9,10},{10,11},{13,14},{14,15},{17,18},{18... | collective-permute-start | bytes 4128776 | tf_op jit(solution)/shard_map/ppermute | solution.py:159
  52.5 59.0 %collective-permute-start.5 = (bf16[1024,672]{0,1:T(8,128)(2,1)}, bf16[1024,672]{0,1:T(8,128)(2,1)}, u32[]{:S(2)}, u32[]{:S(2)}) collective-permute-start(bf16[1024,672]{0,1:T(8,128)(2,1)} %collective-permute-done.1), channel_id=1, source_target_pairs={{1,0},{2,1},{5,4},{6,5},{9,8},{10,9},{13,12},{14,13},{17,16},{18,1... | collective-permute-start | bytes 4128776 | tf_op jit(solution)/shard_map/ppermute | solution.py:160
  77.0 35.8 %collective-permute-start.6 = (bf16[1024,672]{0,1:T(8,128)(2,1)}, bf16[1024,672]{0,1:T(8,128)(2,1)S(1)}, u32[]{:S(2)}, u32[]{:S(2)}) collective-permute-start(bf16[1024,672]{0,1:T(8,128)(2,1)} %collective-permute-done.2), channel_id=1, source_target_pairs={{1,2},{2,3},{5,6},{6,7},{9,10},{10,11},{13,14},{14,15},{17,18},{18... | collective-permute-start | bytes 4128776 | tf_op jit(solution)/shard_map/ppermute | solution.py:159
  82.0 59.0 %collective-permute-start.7 = (bf16[1024,672]{0,1:T(8,128)(2,1)}, bf16[1024,672]{0,1:T(8,128)(2,1)}, u32[]{:S(2)}, u32[]{:S(2)}) collective-permute-start(bf16[1024,672]{0,1:T(8,128)(2,1)} %collective-permute-done.3), channel_id=1, source_target_pairs={{1,0},{2,1},{5,4},{6,5},{9,8},{10,9},{13,12},{14,13},{17,16},{18,1... | collective-permute-start | bytes 4128776 | tf_op jit(solution)/shard_map/ppermute | solution.py:160
  86.7 93.1 %collective-permute-start.8 = (bf16[1024,672]{0,1:T(8,128)(2,1)S(1)}, bf16[1024,672]{0,1:T(8,128)(2,1)}, u32[]{:S(2)}, u32[]{:S(2)}) collective-permute-start(bf16[1024,672]{0,1:T(8,128)(2,1)S(1)} %collective-permute-done.4), channel_id=1, source_target_pairs={{2,3},{6,7},{10,11},{14,15},{18,19},{22,23},{26,27},{30,31}} | collective-permute-start | bytes 4128776 | tf_op jit(solution)/shard_map/ppermute | solution.py:159
  111.5 68.3 %collective-permute-start.9 = (bf16[1024,672]{0,1:T(8,128)(2,1)}, bf16[1024,672]{0,1:T(8,128)(2,1)}, u32[]{:S(2)}, u32[]{:S(2)}) collective-permute-start(bf16[1024,672]{0,1:T(8,128)(2,1)} %collective-permute-done.5), channel_id=1, source_target_pairs={{1,0},{5,4},{9,8},{13,12},{17,16},{21,20},{25,24},{29,28}} | collective-permute-start | bytes 4128776 | tf_op jit(solution)/shard_map/ppermute | solution.py:160
  112.8 73.1 %collective-permute-start.10 = (bf16[1024,672]{0,1:T(8,128)(2,1)S(1)}, bf16[1024,672]{0,1:T(8,128)(2,1)}, u32[]{:S(2)}, u32[]{:S(2)}) collective-permute-start(bf16[1024,672]{0,1:T(8,128)(2,1)S(1)} %collective-permute-done.6), channel_id=1, source_target_pairs={{2,3},{6,7},{10,11},{14,15},{18,19},{22,23},{26,27},{30,31}} | collective-permute-start | bytes 4128776 | tf_op jit(solution)/shard_map/ppermute | solution.py:159
  141.0 59.0 %collective-permute-start.11 = (bf16[1024,672]{0,1:T(8,128)(2,1)}, bf16[1024,672]{0,1:T(8,128)(2,1)}, u32[]{:S(2)}, u32[]{:S(2)}) collective-permute-start(bf16[1024,672]{0,1:T(8,128)(2,1)} %collective-permute-done.7), channel_id=1, source_target_pairs={{1,0},{5,4},{9,8},{13,12},{17,16},{21,20},{25,24},{29,28}} | collective-permute-start | bytes 4128776 | tf_op jit(solution)/shard_map/ppermute | solution.py:160
  142.5 8.6 %copy-start.9 = (bf16[5376,1024]{1,0:T(8,128)(2,1)S(1)}, bf16[5376,1024]{1,0:T(8,128)(2,1)}, u32[]{:S(2)}) copy-start(bf16[5376,1024]{1,0:T(8,128)(2,1)} %all-gather.3.cloned.1.call-done) | copy-start | bytes 33030148
  160.6 2.5 copy-start.8
  208.7 16.9 %collective-permute-start.12 = (bf16[1024,512]{1,0:T(8,128)(2,1)}, bf16[1024,512]{1,0:T(8,128)(2,1)S(1)}, u32[]{:S(2)}, u32[]{:S(2)}) collective-permute-start(bf16[1024,512]{1,0:T(8,128)(2,1)} %shard_map.55), channel_id=1, source_target_pairs={{0,4},{4,8},{8,12},{1,5},{5,9},{9,13},{2,6},{6,10},{10,14},{3,7},{... | collective-permute-start | bytes 3145736 | tf_op jit(solution)/shard_map/ppermute | solution.py:25
  216.1 9.5 %copy-start.6 = (bf16[1024,512]{1,0:T(8,128)(2,1)S(1)}, bf16[1024,512]{1,0:T(8,128)(2,1)}, u32[]{:S(2)}) copy-start(bf16[1024,512]{1,0:T(8,128)(2,1)} %shard_map.55) | copy-start | bytes 3145732
  216.6 9.1 %copy-start = (f32[1024,512]{1,0:T(8,128)}, f32[1024,512]{1,0:T(8,128)S(1)}, u32[]{:S(2)}) copy-start(f32[1024,512]{1,0:T(8,128)S(1)} %add.264.q_ref) | copy-start | bytes 6291460
  216.6 9.1 %copy-start.2 = (f32[1024,128]{1,0:T(8,128)S(1)}, f32[1024,128]{1,0:T(8,128)}, u32[]{:S(2)}) copy-start(f32[1024,128]{1,0:T(8,128)} %get-tuple-element.28.cos_ref) | copy-start | bytes 1572868
  216.6 9.1 %copy-start.3 = (f32[1024,128]{1,0:T(8,128)S(1)}, f32[1024,128]{1,0:T(8,128)}, u32[]{:S(2)}) copy-start(f32[1024,128]{1,0:T(8,128)} %get-tuple-element.29.sin_ref) | copy-start | bytes 1572868
  216.6 9.1 %copy-start.4 = (f32[128]{0:T(128)S(1)}, f32[128]{0:T(128)}, u32[]{:S(2)}) copy-start(f32[128]{0:T(128)} %param.8) | copy-start | bytes 1540
  230.0 28.7 %collective-permute-start.13 = (bf16[256,512]{1,0:T(8,128)(2,1)S(1)}, bf16[256,512]{1,0:T(8,128)(2,1)}, u32[]{:S(2)}, u32[]{:S(2)}) collective-permute-start(bf16[256,512]{1,0:T(8,128)(2,1)S(1)} %shard_map.56), channel_id=1, source_target_pairs={{0,1},{1,2},{2,3},{4,5},{5,6},{6,7},{8,9},{9,10},{10,11},{12,13},{... | collective-permute-start | bytes 786440 | tf_op jit(solution)/shard_map/ppermute | solution.py:159
  232.0 30.1 %collective-permute-start.14 = (bf16[256,512]{1,0:T(8,128)(2,1)S(1)}, bf16[256,512]{1,0:T(8,128)(2,1)}, u32[]{:S(2)}, u32[]{:S(2)}) collective-permute-start(bf16[256,512]{1,0:T(8,128)(2,1)S(1)} %shard_map.56), channel_id=1, source_target_pairs={{1,0},{2,1},{3,2},{5,4},{6,5},{7,6},{9,8},{10,9},{11,10},{13,12},{... | collective-permute-start | bytes 786440 | tf_op jit(solution)/shard_map/ppermute | solution.py:160
  233.5 1.6 copy-start.1
  240.0 25.5 %collective-permute-start.19 = (bf16[256,512]{1,0:T(8,128)(2,1)}, bf16[256,512]{1,0:T(8,128)(2,1)}, u32[]{:S(2)}, u32[]{:S(2)}) collective-permute-start(bf16[256,512]{1,0:T(8,128)(2,1)} %shard_map.57), channel_id=1, source_target_pairs={{0,1},{1,2},{2,3},{4,5},{5,6},{6,7},{8,9},{9,10},{10,11},{12,13},{... | collective-permute-start | bytes 786440 | tf_op jit(solution)/shard_map/ppermute | solution.py:159
  244.6 23.6 %collective-permute-start.20 = (bf16[256,512]{1,0:T(8,128)(2,1)}, bf16[256,512]{1,0:T(8,128)(2,1)}, u32[]{:S(2)}, u32[]{:S(2)}) collective-permute-start(bf16[256,512]{1,0:T(8,128)(2,1)} %shard_map.57), channel_id=1, source_target_pairs={{1,0},{2,1},{3,2},{5,4},{6,5},{7,6},{9,8},{10,9},{11,10},{13,12},{... | collective-permute-start | bytes 786440 | tf_op jit(solution)/shard_map/ppermute | solution.py:160
  254.6 17.3 %collective-permute-start.25 = (bf16[512,512]{1,0:T(8,128)(2,1)}, bf16[512,512]{1,0:T(8,128)(2,1)S(1)}, u32[]{:S(2)}, u32[]{:S(2)}) collective-permute-start(bf16[512,512]{1,0:T(8,128)(2,1)} %shard_map.58), channel_id=1, source_target_pairs={{0,1},{1,2},{2,3},{4,5},{5,6},{6,7},{8,9},{9,10},{10,11},{12,13},{... | collective-permute-start | bytes 1572872 | tf_op jit(solution)/shard_map/ppermute | solution.py:159
  258.7 16.9 %collective-permute-start.26 = (bf16[512,512]{1,0:T(8,128)(2,1)}, bf16[512,512]{1,0:T(8,128)(2,1)S(1)}, u32[]{:S(2)}, u32[]{:S(2)}) collective-permute-start(bf16[512,512]{1,0:T(8,128)(2,1)} %shard_map.58), channel_id=1, source_target_pairs={{1,0},{2,1},{3,2},{5,4},{6,5},{7,6},{9,8},{10,9},{11,10},{13,12},{... | collective-permute-start | bytes 1572872 | tf_op jit(solution)/shard_map/ppermute | solution.py:160
  260.0 4.8 %copy-start.5 = (bf16[2048,1344]{0,1:T(8,128)(2,1)S(1)}, bf16[2048,1344]{0,1:T(8,128)(2,1)}, u32[]{:S(2)}) copy-start(bf16[2048,1344]{0,1:T(8,128)(2,1)} %all-gather.5.cloned.1.call-done) | copy-start | bytes 16515076
  262.2 12.0 %collective-permute-start.15 = (bf16[256,512]{1,0:T(8,128)(2,1)}, bf16[256,512]{1,0:T(8,128)(2,1)S(1)}, u32[]{:S(2)}, u32[]{:S(2)}) collective-permute-start(bf16[256,512]{1,0:T(8,128)(2,1)} %collective-permute-done.13), channel_id=1, source_target_pairs={{1,2},{2,3},{5,6},{6,7},{9,10},{10,11},{13,14},{14,15},{17,18},{18... | collective-permute-start | bytes 786440 | tf_op jit(solution)/shard_map/ppermute | solution.py:159
  265.4 9.5 %collective-permute-start.16 = (bf16[256,512]{1,0:T(8,128)(2,1)}, bf16[256,512]{1,0:T(8,128)(2,1)S(1)}, u32[]{:S(2)}, u32[]{:S(2)}) collective-permute-start(bf16[256,512]{1,0:T(8,128)(2,1)} %collective-permute-done.14), channel_id=1, source_target_pairs={{1,0},{2,1},{5,4},{6,5},{9,8},{10,9},{13,12},{14,13},{17,16},{18,1... | collective-permute-start | bytes 786440 | tf_op jit(solution)/shard_map/ppermute | solution.py:160
  268.3 12.1 %collective-permute-start.21 = (bf16[256,512]{1,0:T(8,128)(2,1)}, bf16[256,512]{1,0:T(8,128)(2,1)S(1)}, u32[]{:S(2)}, u32[]{:S(2)}) collective-permute-start(bf16[256,512]{1,0:T(8,128)(2,1)} %collective-permute-done.19), channel_id=1, source_target_pairs={{1,2},{2,3},{5,6},{6,7},{9,10},{10,11},{13,14},{14,15},{17,18},{18... | collective-permute-start | bytes 786440 | tf_op jit(solution)/shard_map/ppermute | solution.py:159
  272.0 15.5 %collective-permute-start.22 = (bf16[256,512]{1,0:T(8,128)(2,1)}, bf16[256,512]{1,0:T(8,128)(2,1)S(1)}, u32[]{:S(2)}, u32[]{:S(2)}) collective-permute-start(bf16[256,512]{1,0:T(8,128)(2,1)} %collective-permute-done.20), channel_id=1, source_target_pairs={{1,0},{2,1},{5,4},{6,5},{9,8},{10,9},{13,12},{14,13},{17,16},{18,1... | collective-permute-start | bytes 786440 | tf_op jit(solution)/shard_map/ppermute | solution.py:160
  274.2 20.1 %collective-permute-start.27 = (bf16[512,512]{1,0:T(8,128)(2,1)S(1)}, bf16[512,512]{1,0:T(8,128)(2,1)S(1)}, u32[]{:S(2)}, u32[]{:S(2)}) collective-permute-start(bf16[512,512]{1,0:T(8,128)(2,1)S(1)} %collective-permute-done.25), channel_id=1, source_target_pairs={{1,2},{2,3},{5,6},{6,7},{9,10},{10,11},{13,14},{14,15},{17,18},{18... | collective-permute-start | bytes 1572872 | tf_op jit(solution)/shard_map/ppermute | solution.py:159
  274.9 13.8 %collective-permute-start.17 = (bf16[256,512]{1,0:T(8,128)(2,1)S(1)}, bf16[256,512]{1,0:T(8,128)(2,1)S(1)}, u32[]{:S(2)}, u32[]{:S(2)}) collective-permute-start(bf16[256,512]{1,0:T(8,128)(2,1)S(1)} %collective-permute-done.15), channel_id=1, source_target_pairs={{2,3},{6,7},{10,11},{14,15},{18,19},{22,23},{26,27},{30,31}} | collective-permute-start | bytes 786440 | tf_op jit(solution)/shard_map/ppermute | solution.py:159
  275.6 18.1 %collective-permute-start.18 = (bf16[256,512]{1,0:T(8,128)(2,1)S(1)}, bf16[256,512]{1,0:T(8,128)(2,1)S(1)}, u32[]{:S(2)}, u32[]{:S(2)}) collective-permute-start(bf16[256,512]{1,0:T(8,128)(2,1)S(1)} %collective-permute-done.16), channel_id=1, source_target_pairs={{1,0},{5,4},{9,8},{13,12},{17,16},{21,20},{25,24},{29,28}} | collective-permute-start | bytes 786440 | tf_op jit(solution)/shard_map/ppermute | solution.py:160
  280.4 24.5 %collective-permute-start.28 = (bf16[512,512]{1,0:T(8,128)(2,1)S(1)}, bf16[512,512]{1,0:T(8,128)(2,1)S(1)}, u32[]{:S(2)}, u32[]{:S(2)}) collective-permute-start(bf16[512,512]{1,0:T(8,128)(2,1)S(1)} %collective-permute-done.26), channel_id=1, source_target_pairs={{1,0},{2,1},{5,4},{6,5},{9,8},{10,9},{13,12},{14,13},{17,16},{18,1... | collective-permute-start | bytes 1572872 | tf_op jit(solution)/shard_map/ppermute | solution.py:160
  287.4 18.8 %collective-permute-start.23 = (bf16[256,512]{1,0:T(8,128)(2,1)S(1)}, bf16[256,512]{1,0:T(8,128)(2,1)S(1)}, u32[]{:S(2)}, u32[]{:S(2)}) collective-permute-start(bf16[256,512]{1,0:T(8,128)(2,1)S(1)} %collective-permute-done.21), channel_id=1, source_target_pairs={{2,3},{6,7},{10,11},{14,15},{18,19},{22,23},{26,27},{30,31}} | collective-permute-start | bytes 786440 | tf_op jit(solution)/shard_map/ppermute | solution.py:159
  288.7 21.8 %collective-permute-start.24 = (bf16[256,512]{1,0:T(8,128)(2,1)S(1)}, bf16[256,512]{1,0:T(8,128)(2,1)S(1)}, u32[]{:S(2)}, u32[]{:S(2)}) collective-permute-start(bf16[256,512]{1,0:T(8,128)(2,1)S(1)} %collective-permute-done.22), channel_id=1, source_target_pairs={{1,0},{5,4},{9,8},{13,12},{17,16},{21,20},{25,24},{29,28}} | collective-permute-start | bytes 786440 | tf_op jit(solution)/shard_map/ppermute | solution.py:160
  294.3 17.8 %collective-permute-start.29 = (bf16[512,512]{1,0:T(8,128)(2,1)S(1)}, bf16[512,512]{1,0:T(8,128)(2,1)S(1)}, u32[]{:S(2)}, u32[]{:S(2)}) collective-permute-start(bf16[512,512]{1,0:T(8,128)(2,1)S(1)} %collective-permute-done.27), channel_id=1, source_target_pairs={{2,3},{6,7},{10,11},{14,15},{18,19},{22,23},{26,27},{30,31}} | collective-permute-start | bytes 1572872 | tf_op jit(solution)/shard_map/ppermute | solution.py:159
  304.9 13.4 %collective-permute-start.30 = (bf16[512,512]{1,0:T(8,128)(2,1)S(1)}, bf16[512,512]{1,0:T(8,128)(2,1)S(1)}, u32[]{:S(2)}, u32[]{:S(2)}) collective-permute-start(bf16[512,512]{1,0:T(8,128)(2,1)S(1)} %collective-permute-done.28), channel_id=1, source_target_pairs={{1,0},{5,4},{9,8},{13,12},{17,16},{21,20},{25,24},{29,28}} | collective-permute-start | bytes 1572872 | tf_op jit(solution)/shard_map/ppermute | solution.py:160
Sparse Core Ops, SparseCore 0:
  12.8 75.6 all-gather.2
  90.1 41.9 all-gather.4

commit v4 on v3

--- a/solution.py
+++ b/solution.py
@@ -230,9 +230,9 @@
     behind = from_behind(paired[rows - WINDOW :], "tok", 1)
     combined = jnp.concatenate([behind, paired], axis=0)
     results = []
-    quarter = rows // 4
-    for row0, count in ((0, quarter), (quarter, quarter), (2 * quarter, rows - 2 * quarter)):
-        heads = attend(query, q_gain, cosine, sine, combined, base, row0, count)
+    block = rows // 2
+    for row0 in range(0, rows, block):
+        heads = attend(query, q_gain, cosine, sine, combined, base, row0, block)
         (summed,) = line_gather_dot(
             [(heads, 0)],
             line_hops([(heads, 0)], "hid"),

time: 334 us -> 319 us (0.955)
  starting transfers between devices: 54.6 us -> 45.7 us
  matrix products: 64.5 us -> 60.7 us
    ppermute x15 -> x12, starting transfers between devices: 30.1 us -> 25 us  [line_hops(): ups = [lax.ppermute(up, axis, upward) for up in ups]]
    ppermute x15 -> x12, starting transfers between devices: 19.6 us -> 15.8 us  [line_hops(): downs = [lax.ppermute(down, axis, downward) for down in downs]]
    dot_general x35 -> x30, matrix products: 64.5 us -> 60.7 us  [terms(): term = jnp.dot(piece, rows, preferred_element_type=jnp.float32)]
    ppermute x15 -> x12, waiting for transfers between devices: 43.3 us -> 45.3 us  [line_hops(): ups = [lax.ppermute(up, axis, upward) for up in ups]]
    pallas_call x3 -> x2, Pallas kernels: 17.9 us -> 16.2 us  [attend(): pl.pallas_call(functools.partial(attend_kernel, q_tile, row0), out_shape=...]
    ppermute x15 -> x12, waiting for transfers between devices: 102 us -> 100 us  [line_hops(): downs = [lax.ppermute(down, axis, downward) for down in downs]]
  transfers between devices with their start and end apart: 33 -> 27, of which waited for: 13 -> 14; matrix products, arithmetic and copies ran while one was open for 21% -> 21% of each run, Pallas kernels for 7% -> 7%
where the time goes in v4:
time: 319 us; the launch traced here: 313 us
  waiting for transfers between devices  155 us (49%)
  matrix products  60.7 us (19%)
  starting transfers between devices  45.7 us (14%)
  Pallas kernels  20.5 us (6%)
  between operations  14.5 us (5%)
  other arithmetic  10.4 us (3%)
  local copies, waits for them, and re-layouts  6.2 us (2%)
    ppermute x12, waiting for transfers between devices, line_hops(): downs = [lax.ppermute(down, axis, downward) for down in downs]  100 us
    dot_general x30, matrix products, terms(): term = jnp.dot(piece, rows, preferred_element_type=jnp.float32)  60.7 us
    ppermute x12, waiting for transfers between devices, line_hops(): ups = [lax.ppermute(up, axis, upward) for up in ups]  45.3 us
    ppermute x12, starting transfers between devices, line_hops(): ups = [lax.ppermute(up, axis, upward) for up in ups]  25 us
    pallas_call x2, Pallas kernels, attend(): pl.pallas_call(functools.partial(attend_kernel, q_tile, row0), out_shape=...  16.2 us
    ppermute x12, starting transfers between devices, line_hops(): downs = [lax.ppermute(down, axis, downward) for down in downs]  15.8 us
    ppermute x1, waiting for transfers between devices, from_behind(): lax.ppermute(value, axis, [(source, source + steps) for source in range(f...  8.94 us
  transfers between devices with their start and end apart: 27, of which 14 were waited for; matrix products, arithmetic and copies ran while one was open for 21% of the time, Pallas kernels for 7%

profile of v4, /device:TPU:1, one launch (start us, length us, event | category | flops | bytes accessed | tf_op | source)
XLA Modules:
  0.0 312.6 jit_solution(7332800777780924731)
XLA Ops:
  6.5 3.6 %fusion.108 = (bf16[1344,2,256]{2,1,0:T(2,128)(2,1)S(1)}, bf16[1344,2,256]{2,1,0:T(2,128)(2,1)S(1)}) fusion(bf16[1344,2,512]{2,1,0:T(2,128)(2,1)} %param.6), kind=kLoop, calls=%fused_computation.125 | loop fusion | bytes 5505024 | tf_op jit(solution)/shard_map/slice | solution.py:213
  10.8 1.9 pad_maximum_fusion
  12.7 1.7 copy-done.5
  14.7 5.1 %collective-permute-start = (bf16[1024,672]{0,1:T(8,128)(2,1)S(1)}, bf16[1024,672]{0,1:T(8,128)(2,1)}, u32[]{:S(2)}, u32[]{:S(2)}) collective-permute-start(bf16[1024,672]{0,1:T(8,128)(2,1)S(1)} %get-tuple-element.22), channel_id=1, source_target_pairs={{0,1},{1,2},{2,3},{4,5},{5,6},{6,7},{8,9},{9,10},{10,11},{12,13},{... | collective-permute-start | bytes 4128776 | tf_op jit(solution)/shard_map/ppermute | solution.py:159
  19.8 1.3 collective-permute-start.1
  21.1 5.1 %collective-permute-start.2 = (bf16[1024,672]{0,1:T(8,128)(2,1)S(1)}, bf16[1024,672]{0,1:T(8,128)(2,1)}, u32[]{:S(2)}, u32[]{:S(2)}) collective-permute-start(bf16[1024,672]{0,1:T(8,128)(2,1)S(1)} %get-tuple-element.21), channel_id=1, source_target_pairs={{0,1},{1,2},{2,3},{4,5},{5,6},{6,7},{8,9},{9,10},{10,11},{12,13},{... | collective-permute-start | bytes 4128776 | tf_op jit(solution)/shard_map/ppermute | solution.py:159
  26.2 1.3 collective-permute-start.3
  27.5 20.0 %collective-permute-done = bf16[1024,672]{0,1:T(8,128)(2,1)} collective-permute-done((bf16[1024,672]{0,1:T(8,128)(2,1)S(1)}, bf16[1024,672]{0,1:T(8,128)(2,1)}, u32[]{:S(2)}, u32[]{:S(2)}) %collective-permute-start) | collective-permute-done | bytes 1376288 | tf_op jit(solution)/shard_map/ppermute | solution.py:159
  48.3 4.3 %collective-permute-done.1 = bf16[1024,672]{0,1:T(8,128)(2,1)} collective-permute-done((bf16[1024,672]{0,1:T(8,128)(2,1)S(1)}, bf16[1024,672]{0,1:T(8,128)(2,1)}, u32[]{:S(2)}, u32[]{:S(2)}) %collective-permute-start.1) | collective-permute-done | bytes 1376288 | tf_op jit(solution)/shard_map/ppermute | solution.py:160
  52.5 1.3 collective-permute-start.5
  53.8 23.2 %collective-permute-done.2 = bf16[1024,672]{0,1:T(8,128)(2,1)} collective-permute-done((bf16[1024,672]{0,1:T(8,128)(2,1)S(1)}, bf16[1024,672]{0,1:T(8,128)(2,1)}, u32[]{:S(2)}, u32[]{:S(2)}) %collective-permute-start.2) | collective-permute-done | bytes 1376288 | tf_op jit(solution)/shard_map/ppermute | solution.py:159
  77.8 4.3 %collective-permute-done.3 = bf16[1024,672]{0,1:T(8,128)(2,1)} collective-permute-done((bf16[1024,672]{0,1:T(8,128)(2,1)S(1)}, bf16[1024,672]{0,1:T(8,128)(2,1)}, u32[]{:S(2)}, u32[]{:S(2)}) %collective-permute-start.3) | collective-permute-done | bytes 1376288 | tf_op jit(solution)/shard_map/ppermute | solution.py:160
  82.0 1.3 collective-permute-start.7
  83.4 1.9 fusion.72
  85.3 1.3 pad_maximum_fusion.3
  86.7 1.8 collective-permute-start.8
  88.4 23.1 %collective-permute-done.5 = bf16[1024,672]{0,1:T(8,128)(2,1)} collective-permute-done((bf16[1024,672]{0,1:T(8,128)(2,1)}, bf16[1024,672]{0,1:T(8,128)(2,1)}, u32[]{:S(2)}, u32[]{:S(2)}) %collective-permute-start.5) | collective-permute-done | bytes 1376288 | tf_op jit(solution)/shard_map/ppermute | solution.py:160
  111.5 1.3 collective-permute-start.9
  112.8 1.8 collective-permute-start.10
  114.7 26.4 %collective-permute-done.7 = bf16[1024,672]{0,1:T(8,128)(2,1)} collective-permute-done((bf16[1024,672]{0,1:T(8,128)(2,1)}, bf16[1024,672]{0,1:T(8,128)(2,1)}, u32[]{:S(2)}, u32[]{:S(2)}) %collective-permute-start.7) | collective-permute-done | bytes 1376288 | tf_op jit(solution)/shard_map/ppermute | solution.py:160
  141.0 1.5 collective-permute-start.11
  142.5 2.7 fusion.34
  145.3 3.2 %fusion.52 = f32[512,1024]{0,1:T(8,128)S(1)} fusion(bf16[1024,672]{0,1:T(8,128)(2,1)} %collective-permute-done.3, bf16[5376,1024]{1,0:T(8,128)(2,1)} %all-gather.3.cloned.1.call-done, s32[]{:T(128)S(6)} %select_n.122), kind=kOutput, calls=%fused_computation.65 | convolution fusion | flops 704643072 | bytes 4161540 | tf_op jit(solution)/shard_map/dot_general | solution.py:175
  148.5 2.6 fusion.36
  151.1 2.4 fusion.54
  153.5 2.4 fusion.38
  155.9 2.4 fusion.56
  158.3 2.4 fusion.40
  160.7 2.5 fusion.58
  163.2 1.0 fusion.42
  166.4 2.4 fusion.32
  168.8 3.2 %fusion.4 = f32[1024,512]{1,0:T(8,128)S(1)} fusion(f32[1024,512]{1,0:T(8,128)S(1)} %fusion.32, f32[512,1024]{0,1:T(8,128)S(1)} %fusion.34, f32[512,1024]{0,1:T(8,128)S(1)} %fusion.36, f32[512,1024]{0,1:T(8,128)S(1)} %fusion.38, f32[512,1024]{0,1:T(8,128)S(1)} %fusion.40, f32[512,1024]{0,1:T(8,128)S(1)} %fusion.44, f32[512,1024]{0,1:T(8,128)S(1)} %fusion.42, ...), kind=kOutput, calls=%fused_computation.14 | convolution fusion | flops 709001216 | bytes 20217860 | tf_op jit(solution)/shard_map/dot_general | solution.py:175
  171.9 2.1 fusion.62
  174.1 2.6 fusion.50
  176.6 3.0 fusion.5
  179.6 2.6 fusion.24
  182.7 2.6 fusion.26
  185.8 14.2 %collective-permute-done.11 = bf16[1024,672]{0,1:T(8,128)(2,1)} collective-permute-done((bf16[1024,672]{0,1:T(8,128)(2,1)}, bf16[1024,672]{0,1:T(8,128)(2,1)}, u32[]{:S(2)}, u32[]{:S(2)}) %collective-permute-start.11) | collective-permute-done | bytes 1376288 | tf_op jit(solution)/shard_map/ppermute | solution.py:160
  200.0 2.5 fusion.20
  202.6 1.8 add.247.x_ref
  204.4 4.3 %shard_map.55 = bf16[1024,512]{1,0:T(8,128)(2,1)} custom-call(f32[1024,512]{1,0:T(8,128)} %add.247.x_ref, f32[1,128]{1,0:T(1,128)} %bitcast.35, f32[1024,128]{1,0:T(8,128)} %get-tuple-element.28.cos_ref, f32[1024,128]{1,0:T(8,128)} %get-tuple-element.29.sin_ref), custom_call_target="tpu_custom_call" | custom-call | flops 10485760 | bytes 3145728 | tf_op jit(solution)/shard_map/pallas_call | solution.py:59
  208.7 4.9 %collective-permute-start.12 = (bf16[1024,512]{1,0:T(8,128)(2,1)}, bf16[1024,512]{1,0:T(8,128)(2,1)S(1)}, u32[]{:S(2)}, u32[]{:S(2)}) collective-permute-start(bf16[1024,512]{1,0:T(8,128)(2,1)} %shard_map.55), channel_id=1, source_target_pairs={{0,4},{4,8},{8,12},{1,5},{5,9},{9,13},{2,6},{6,10},{10,14},{3,7},{... | collective-permute-start | bytes 3145736 | tf_op jit(solution)/shard_map/ppermute | solution.py:25
  213.6 2.6 fusion.22
  216.7 8.9 %collective-permute-done.12 = bf16[1024,512]{1,0:T(8,128)(2,1)S(1)} collective-permute-done((bf16[1024,512]{1,0:T(8,128)(2,1)}, bf16[1024,512]{1,0:T(8,128)(2,1)S(1)}, u32[]{:S(2)}, u32[]{:S(2)}) %collective-permute-start.12) | collective-permute-done | bytes 1048608 | tf_op jit(solution)/shard_map/ppermute | solution.py:25
  225.8 8.1 %shard_map.56 = bf16[512,512]{1,0:T(8,128)(2,1)S(1)} custom-call(s32[1]{0:T(128)} %bitcast.base_ref, f32[1024,512]{1,0:T(8,128)S(1)} %add.244.q_ref, f32[1,128]{1,0:T(1,128)S(1)} %bitcast.29, f32[1024,128]{1,0:T(8,128)S(1)} %copy-done, f32[1024,128]{1,0:T(8,128)S(1)} %copy-done.1, bf16[2048,512]{1,0:T(8,128)(2,1)S(1)} %pad_maximum_fusion.2.k_ref.v_ref, ...), custom_call_target="tpu_custom_call" | custom-call | flops 1342177280 | bytes 5242880 | tf_op jit(solution)/shard_map/pallas_call | solution.py:129
  233.9 2.1 collective-permute-start.13
  235.9 1.5 collective-permute-start.14
  237.5 8.1 %shard_map.57 = bf16[512,512]{1,0:T(8,128)(2,1)S(1)} custom-call(s32[1]{0:T(128)} %bitcast.base_ref, f32[1024,512]{1,0:T(8,128)S(1)} %add.244.q_ref, f32[1,128]{1,0:T(1,128)S(1)} %bitcast.30, f32[1024,128]{1,0:T(8,128)S(1)} %copy-done, f32[1024,128]{1,0:T(8,128)S(1)} %copy-done.1, bf16[2048,512]{1,0:T(8,128)(2,1)S(1)} %pad_maximum_fusion.2.k_ref.v_ref, ...), custom_call_target="tpu_custom_call" | custom-call | flops 1342177280 | bytes 5242880 | tf_op jit(solution)/shard_map/pallas_call | solution.py:129
  245.6 4.8 %collective-permute-start.19 = (bf16[512,512]{1,0:T(8,128)(2,1)S(1)}, bf16[512,512]{1,0:T(8,128)(2,1)}, u32[]{:S(2)}, u32[]{:S(2)}) collective-permute-start(bf16[512,512]{1,0:T(8,128)(2,1)S(1)} %shard_map.57), channel_id=1, source_target_pairs={{0,1},{1,2},{2,3},{4,5},{5,6},{6,7},{8,9},{9,10},{10,11},{12,13},{... | collective-permute-start | bytes 1572872 | tf_op jit(solution)/shard_map/ppermute | solution.py:159
  250.4 1.3 collective-permute-start.20
  252.4 1.3 collective-permute-start.16
  253.7 2.0 collective-permute-done.19
  256.4 2.6 fusion.16
  259.0 2.4 fusion.14
  262.4 2.5 collective-permute-done.20
  264.9 1.3 collective-permute-start.22
  267.1 2.0 fusion.10
  270.7 5.4 %collective-permute-done.16 = bf16[512,512]{1,0:T(8,128)(2,1)S(1)} collective-permute-done((bf16[512,512]{1,0:T(8,128)(2,1)S(1)}, bf16[512,512]{1,0:T(8,128)(2,1)S(1)}, u32[]{:S(2)}, u32[]{:S(2)}) %collective-permute-start.16) | collective-permute-done | bytes 524320 | tf_op jit(solution)/shard_map/ppermute | solution.py:160
  276.1 1.3 collective-permute-start.18
  278.1 9.2 %collective-permute-done.22 = bf16[512,512]{1,0:T(8,128)(2,1)S(1)} collective-permute-done((bf16[512,512]{1,0:T(8,128)(2,1)}, bf16[512,512]{1,0:T(8,128)(2,1)S(1)}, u32[]{:S(2)}, u32[]{:S(2)}) %collective-permute-start.22) | collective-permute-done | bytes 524320 | tf_op jit(solution)/shard_map/ppermute | solution.py:160
  287.3 1.3 collective-permute-start.24
  290.5 6.4 %collective-permute-done.18 = bf16[512,512]{1,0:T(8,128)(2,1)S(1)} collective-permute-done((bf16[512,512]{1,0:T(8,128)(2,1)S(1)}, bf16[512,512]{1,0:T(8,128)(2,1)S(1)}, u32[]{:S(2)}, u32[]{:S(2)}) %collective-permute-start.18) | collective-permute-done | bytes 524320 | tf_op jit(solution)/shard_map/ppermute | solution.py:160
  297.9 4.6 %collective-permute-done.24 = bf16[512,512]{1,0:T(8,128)(2,1)S(1)} collective-permute-done((bf16[512,512]{1,0:T(8,128)(2,1)S(1)}, bf16[512,512]{1,0:T(8,128)(2,1)S(1)}, u32[]{:S(2)}, u32[]{:S(2)}) %collective-permute-start.24) | collective-permute-done | bytes 524320 | tf_op jit(solution)/shard_map/ppermute | solution.py:160
  303.5 1.9 pad_maximum_fusion.1
  (56 shorter events, 15.5 us)
Async XLA Ops:
  6.5 136.0 %all-gather.3.cloned.1.call-start = ((), (), s32[]{:S(2)}) async-start(), calls=%async_computation | async-start | bytes 13762560 | tf_op jit(solution)/shard_map/all_gather | solution.py:218
  12.6 1.8 copy-start.5
  12.7 243.8 %all-gather.5.cloned.1.call-start = ((), (), s32[]{:S(2)}) async-start(), calls=%async_computation.1 | async-start | bytes 6881280 | tf_op jit(solution)/shard_map/all_gather | solution.py:210
  14.7 32.9 %collective-permute-start = (bf16[1024,672]{0,1:T(8,128)(2,1)S(1)}, bf16[1024,672]{0,1:T(8,128)(2,1)}, u32[]{:S(2)}, u32[]{:S(2)}) collective-permute-start(bf16[1024,672]{0,1:T(8,128)(2,1)S(1)} %get-tuple-element.22), channel_id=1, source_target_pairs={{0,1},{1,2},{2,3},{4,5},{5,6},{6,7},{8,9},{9,10},{10,11},{12,13},{... | collective-permute-start | bytes 4128776 | tf_op jit(solution)/shard_map/ppermute | solution.py:159
  19.8 32.7 %collective-permute-start.1 = (bf16[1024,672]{0,1:T(8,128)(2,1)S(1)}, bf16[1024,672]{0,1:T(8,128)(2,1)}, u32[]{:S(2)}, u32[]{:S(2)}) collective-permute-start(bf16[1024,672]{0,1:T(8,128)(2,1)S(1)} %get-tuple-element.22), channel_id=1, source_target_pairs={{1,0},{2,1},{3,2},{5,4},{6,5},{7,6},{9,8},{10,9},{11,10},{13,12},{... | collective-permute-start | bytes 4128776 | tf_op jit(solution)/shard_map/ppermute | solution.py:160
  21.1 55.9 %collective-permute-start.2 = (bf16[1024,672]{0,1:T(8,128)(2,1)S(1)}, bf16[1024,672]{0,1:T(8,128)(2,1)}, u32[]{:S(2)}, u32[]{:S(2)}) collective-permute-start(bf16[1024,672]{0,1:T(8,128)(2,1)S(1)} %get-tuple-element.21), channel_id=1, source_target_pairs={{0,1},{1,2},{2,3},{4,5},{5,6},{6,7},{8,9},{9,10},{10,11},{12,13},{... | collective-permute-start | bytes 4128776 | tf_op jit(solution)/shard_map/ppermute | solution.py:159
  26.2 55.8 %collective-permute-start.3 = (bf16[1024,672]{0,1:T(8,128)(2,1)S(1)}, bf16[1024,672]{0,1:T(8,128)(2,1)}, u32[]{:S(2)}, u32[]{:S(2)}) collective-permute-start(bf16[1024,672]{0,1:T(8,128)(2,1)S(1)} %get-tuple-element.21), channel_id=1, source_target_pairs={{1,0},{2,1},{3,2},{5,4},{6,5},{7,6},{9,8},{10,9},{11,10},{13,12},{... | collective-permute-start | bytes 4128776 | tf_op jit(solution)/shard_map/ppermute | solution.py:160
  47.6 39.1 %collective-permute-start.4 = (bf16[1024,672]{0,1:T(8,128)(2,1)}, bf16[1024,672]{0,1:T(8,128)(2,1)S(1)}, u32[]{:S(2)}, u32[]{:S(2)}) collective-permute-start(bf16[1024,672]{0,1:T(8,128)(2,1)} %collective-permute-done), channel_id=1, source_target_pairs={{1,2},{2,3},{5,6},{6,7},{9,10},{10,11},{13,14},{14,15},{17,18},{18... | collective-permute-start | bytes 4128776 | tf_op jit(solution)/shard_map/ppermute | solution.py:159
  52.5 59.0 %collective-permute-start.5 = (bf16[1024,672]{0,1:T(8,128)(2,1)}, bf16[1024,672]{0,1:T(8,128)(2,1)}, u32[]{:S(2)}, u32[]{:S(2)}) collective-permute-start(bf16[1024,672]{0,1:T(8,128)(2,1)} %collective-permute-done.1), channel_id=1, source_target_pairs={{1,0},{2,1},{5,4},{6,5},{9,8},{10,9},{13,12},{14,13},{17,16},{18,1... | collective-permute-start | bytes 4128776 | tf_op jit(solution)/shard_map/ppermute | solution.py:160
  77.0 35.8 %collective-permute-start.6 = (bf16[1024,672]{0,1:T(8,128)(2,1)}, bf16[1024,672]{0,1:T(8,128)(2,1)S(1)}, u32[]{:S(2)}, u32[]{:S(2)}) collective-permute-start(bf16[1024,672]{0,1:T(8,128)(2,1)} %collective-permute-done.2), channel_id=1, source_target_pairs={{1,2},{2,3},{5,6},{6,7},{9,10},{10,11},{13,14},{14,15},{17,18},{18... | collective-permute-start | bytes 4128776 | tf_op jit(solution)/shard_map/ppermute | solution.py:159
  82.0 59.0 %collective-permute-start.7 = (bf16[1024,672]{0,1:T(8,128)(2,1)}, bf16[1024,672]{0,1:T(8,128)(2,1)}, u32[]{:S(2)}, u32[]{:S(2)}) collective-permute-start(bf16[1024,672]{0,1:T(8,128)(2,1)} %collective-permute-done.3), channel_id=1, source_target_pairs={{1,0},{2,1},{5,4},{6,5},{9,8},{10,9},{13,12},{14,13},{17,16},{18,1... | collective-permute-start | bytes 4128776 | tf_op jit(solution)/shard_map/ppermute | solution.py:160
  86.7 93.0 %collective-permute-start.8 = (bf16[1024,672]{0,1:T(8,128)(2,1)S(1)}, bf16[1024,672]{0,1:T(8,128)(2,1)}, u32[]{:S(2)}, u32[]{:S(2)}) collective-permute-start(bf16[1024,672]{0,1:T(8,128)(2,1)S(1)} %collective-permute-done.4), channel_id=1, source_target_pairs={{2,3},{6,7},{10,11},{14,15},{18,19},{22,23},{26,27},{30,31}} | collective-permute-start | bytes 4128776 | tf_op jit(solution)/shard_map/ppermute | solution.py:159
  111.5 68.1 %collective-permute-start.9 = (bf16[1024,672]{0,1:T(8,128)(2,1)}, bf16[1024,672]{0,1:T(8,128)(2,1)}, u32[]{:S(2)}, u32[]{:S(2)}) collective-permute-start(bf16[1024,672]{0,1:T(8,128)(2,1)} %collective-permute-done.5), channel_id=1, source_target_pairs={{1,0},{5,4},{9,8},{13,12},{17,16},{21,20},{25,24},{29,28}} | collective-permute-start | bytes 4128776 | tf_op jit(solution)/shard_map/ppermute | solution.py:160
  112.8 72.9 %collective-permute-start.10 = (bf16[1024,672]{0,1:T(8,128)(2,1)S(1)}, bf16[1024,672]{0,1:T(8,128)(2,1)}, u32[]{:S(2)}, u32[]{:S(2)}) collective-permute-start(bf16[1024,672]{0,1:T(8,128)(2,1)S(1)} %collective-permute-done.6), channel_id=1, source_target_pairs={{2,3},{6,7},{10,11},{14,15},{18,19},{22,23},{26,27},{30,31}} | collective-permute-start | bytes 4128776 | tf_op jit(solution)/shard_map/ppermute | solution.py:159
  141.0 59.0 %collective-permute-start.11 = (bf16[1024,672]{0,1:T(8,128)(2,1)}, bf16[1024,672]{0,1:T(8,128)(2,1)}, u32[]{:S(2)}, u32[]{:S(2)}) collective-permute-start(bf16[1024,672]{0,1:T(8,128)(2,1)} %collective-permute-done.7), channel_id=1, source_target_pairs={{1,0},{5,4},{9,8},{13,12},{17,16},{21,20},{25,24},{29,28}} | collective-permute-start | bytes 4128776 | tf_op jit(solution)/shard_map/ppermute | solution.py:160
  142.5 8.6 %copy-start.7 = (bf16[5376,1024]{1,0:T(8,128)(2,1)S(1)}, bf16[5376,1024]{1,0:T(8,128)(2,1)}, u32[]{:S(2)}) copy-start(bf16[5376,1024]{1,0:T(8,128)(2,1)} %all-gather.3.cloned.1.call-done) | copy-start | bytes 33030148
  160.7 2.6 copy-start.6
  208.7 16.9 %collective-permute-start.12 = (bf16[1024,512]{1,0:T(8,128)(2,1)}, bf16[1024,512]{1,0:T(8,128)(2,1)S(1)}, u32[]{:S(2)}, u32[]{:S(2)}) collective-permute-start(bf16[1024,512]{1,0:T(8,128)(2,1)} %shard_map.55), channel_id=1, source_target_pairs={{0,4},{4,8},{8,12},{1,5},{5,9},{9,13},{2,6},{6,10},{10,14},{3,7},{... | collective-permute-start | bytes 3145736 | tf_op jit(solution)/shard_map/ppermute | solution.py:25
  216.1 9.5 %copy-start.4 = (bf16[1024,512]{1,0:T(8,128)(2,1)S(1)}, bf16[1024,512]{1,0:T(8,128)(2,1)}, u32[]{:S(2)}) copy-start(bf16[1024,512]{1,0:T(8,128)(2,1)} %shard_map.55) | copy-start | bytes 3145732
  216.6 9.1 %copy-start = (f32[1024,128]{1,0:T(8,128)S(1)}, f32[1024,128]{1,0:T(8,128)}, u32[]{:S(2)}) copy-start(f32[1024,128]{1,0:T(8,128)} %get-tuple-element.28.cos_ref) | copy-start | bytes 1572868
  216.6 9.1 %copy-start.1 = (f32[1024,128]{1,0:T(8,128)S(1)}, f32[1024,128]{1,0:T(8,128)}, u32[]{:S(2)}) copy-start(f32[1024,128]{1,0:T(8,128)} %get-tuple-element.29.sin_ref) | copy-start | bytes 1572868
  216.6 9.1 %copy-start.2 = (f32[128]{0:T(128)S(1)}, f32[128]{0:T(128)}, u32[]{:S(2)}) copy-start(f32[128]{0:T(128)} %param.8) | copy-start | bytes 1540
  233.9 17.8 %collective-permute-start.13 = (bf16[512,512]{1,0:T(8,128)(2,1)S(1)}, bf16[512,512]{1,0:T(8,128)(2,1)}, u32[]{:S(2)}, u32[]{:S(2)}) collective-permute-start(bf16[512,512]{1,0:T(8,128)(2,1)S(1)} %shard_map.56), channel_id=1, source_target_pairs={{0,1},{1,2},{2,3},{4,5},{5,6},{6,7},{8,9},{9,10},{10,11},{12,13},{... | collective-permute-start | bytes 1572872 | tf_op jit(solution)/shard_map/ppermute | solution.py:159
  235.9 16.5 %collective-permute-start.14 = (bf16[512,512]{1,0:T(8,128)(2,1)S(1)}, bf16[512,512]{1,0:T(8,128)(2,1)S(1)}, u32[]{:S(2)}, u32[]{:S(2)}) collective-permute-start(bf16[512,512]{1,0:T(8,128)(2,1)S(1)} %shard_map.56), channel_id=1, source_target_pairs={{1,0},{2,1},{3,2},{5,4},{6,5},{7,6},{9,8},{10,9},{11,10},{13,12},{... | collective-permute-start | bytes 1572872 | tf_op jit(solution)/shard_map/ppermute | solution.py:160
  245.6 10.1 %collective-permute-start.19 = (bf16[512,512]{1,0:T(8,128)(2,1)S(1)}, bf16[512,512]{1,0:T(8,128)(2,1)}, u32[]{:S(2)}, u32[]{:S(2)}) collective-permute-start(bf16[512,512]{1,0:T(8,128)(2,1)S(1)} %shard_map.57), channel_id=1, source_target_pairs={{0,1},{1,2},{2,3},{4,5},{5,6},{6,7},{8,9},{9,10},{10,11},{12,13},{... | collective-permute-start | bytes 1572872 | tf_op jit(solution)/shard_map/ppermute | solution.py:159
  250.4 14.5 %collective-permute-start.20 = (bf16[512,512]{1,0:T(8,128)(2,1)S(1)}, bf16[512,512]{1,0:T(8,128)(2,1)}, u32[]{:S(2)}, u32[]{:S(2)}) collective-permute-start(bf16[512,512]{1,0:T(8,128)(2,1)S(1)} %shard_map.57), channel_id=1, source_target_pairs={{1,0},{2,1},{3,2},{5,4},{6,5},{7,6},{9,8},{10,9},{11,10},{13,12},{... | collective-permute-start | bytes 1572872 | tf_op jit(solution)/shard_map/ppermute | solution.py:160
  251.7 18.3 %collective-permute-start.15 = (bf16[512,512]{1,0:T(8,128)(2,1)}, bf16[512,512]{1,0:T(8,128)(2,1)S(1)}, u32[]{:S(2)}, u32[]{:S(2)}) collective-permute-start(bf16[512,512]{1,0:T(8,128)(2,1)} %collective-permute-done.13), channel_id=1, source_target_pairs={{1,2},{2,3},{5,6},{6,7},{9,10},{10,11},{13,14},{14,15},{17,18},{18... | collective-permute-start | bytes 1572872 | tf_op jit(solution)/shard_map/ppermute | solution.py:159
  252.4 23.7 %collective-permute-start.16 = (bf16[512,512]{1,0:T(8,128)(2,1)S(1)}, bf16[512,512]{1,0:T(8,128)(2,1)S(1)}, u32[]{:S(2)}, u32[]{:S(2)}) collective-permute-start(bf16[512,512]{1,0:T(8,128)(2,1)S(1)} %collective-permute-done.14), channel_id=1, source_target_pairs={{1,0},{2,1},{5,4},{6,5},{9,8},{10,9},{13,12},{14,13},{17,16},{18,1... | collective-permute-start | bytes 1572872 | tf_op jit(solution)/shard_map/ppermute | solution.py:160
  255.7 21.7 %collective-permute-start.21 = (bf16[512,512]{1,0:T(8,128)(2,1)}, bf16[512,512]{1,0:T(8,128)(2,1)S(1)}, u32[]{:S(2)}, u32[]{:S(2)}) collective-permute-start(bf16[512,512]{1,0:T(8,128)(2,1)} %collective-permute-done.19), channel_id=1, source_target_pairs={{1,2},{2,3},{5,6},{6,7},{9,10},{10,11},{13,14},{14,15},{17,18},{18... | collective-permute-start | bytes 1572872 | tf_op jit(solution)/shard_map/ppermute | solution.py:159
  256.4 5.0 %copy-start.3 = (bf16[2048,1344]{0,1:T(8,128)(2,1)S(1)}, bf16[2048,1344]{0,1:T(8,128)(2,1)}, u32[]{:S(2)}) copy-start(bf16[2048,1344]{0,1:T(8,128)(2,1)} %all-gather.5.cloned.1.call-done) | copy-start | bytes 16515076
  264.9 22.5 %collective-permute-start.22 = (bf16[512,512]{1,0:T(8,128)(2,1)}, bf16[512,512]{1,0:T(8,128)(2,1)S(1)}, u32[]{:S(2)}, u32[]{:S(2)}) collective-permute-start(bf16[512,512]{1,0:T(8,128)(2,1)} %collective-permute-done.20), channel_id=1, source_target_pairs={{1,0},{2,1},{5,4},{6,5},{9,8},{10,9},{13,12},{14,13},{17,16},{18,1... | collective-permute-start | bytes 1572872 | tf_op jit(solution)/shard_map/ppermute | solution.py:160
  270.0 20.5 %collective-permute-start.17 = (bf16[512,512]{1,0:T(8,128)(2,1)S(1)}, bf16[512,512]{1,0:T(8,128)(2,1)S(1)}, u32[]{:S(2)}, u32[]{:S(2)}) collective-permute-start(bf16[512,512]{1,0:T(8,128)(2,1)S(1)} %collective-permute-done.15), channel_id=1, source_target_pairs={{2,3},{6,7},{10,11},{14,15},{18,19},{22,23},{26,27},{30,31}} | collective-permute-start | bytes 1572872 | tf_op jit(solution)/shard_map/ppermute | solution.py:159
  276.1 20.8 %collective-permute-start.18 = (bf16[512,512]{1,0:T(8,128)(2,1)S(1)}, bf16[512,512]{1,0:T(8,128)(2,1)S(1)}, u32[]{:S(2)}, u32[]{:S(2)}) collective-permute-start(bf16[512,512]{1,0:T(8,128)(2,1)S(1)} %collective-permute-done.16), channel_id=1, source_target_pairs={{1,0},{5,4},{9,8},{13,12},{17,16},{21,20},{25,24},{29,28}} | collective-permute-start | bytes 1572872 | tf_op jit(solution)/shard_map/ppermute | solution.py:160
  277.4 20.5 %collective-permute-start.23 = (bf16[512,512]{1,0:T(8,128)(2,1)S(1)}, bf16[512,512]{1,0:T(8,128)(2,1)S(1)}, u32[]{:S(2)}, u32[]{:S(2)}) collective-permute-start(bf16[512,512]{1,0:T(8,128)(2,1)S(1)} %collective-permute-done.21), channel_id=1, source_target_pairs={{2,3},{6,7},{10,11},{14,15},{18,19},{22,23},{26,27},{30,31}} | collective-permute-start | bytes 1572872 | tf_op jit(solution)/shard_map/ppermute | solution.py:159
  287.3 15.2 %collective-permute-start.24 = (bf16[512,512]{1,0:T(8,128)(2,1)S(1)}, bf16[512,512]{1,0:T(8,128)(2,1)S(1)}, u32[]{:S(2)}, u32[]{:S(2)}) collective-permute-start(bf16[512,512]{1,0:T(8,128)(2,1)S(1)} %collective-permute-done.22), channel_id=1, source_target_pairs={{1,0},{5,4},{9,8},{13,12},{17,16},{21,20},{25,24},{29,28}} | collective-permute-start | bytes 1572872 | tf_op jit(solution)/shard_map/ppermute | solution.py:160
Sparse Core Ops, SparseCore 0:
  12.8 75.6 all-gather.2
  90.1 41.8 all-gather.4

commit v5 on v4

--- a/solution.py
+++ b/solution.py
@@ -16,7 +16,7 @@
 EPS = 1e-06
 SCALE = 168.0 ** (-0.5)
 ROPE_BASE = 10000.0
-PIECES = 2
+PIECES = 3
 
 
 def from_behind(value, axis, steps):
@@ -54,7 +54,7 @@
 
 def norm_rope(values, gain, cosine, sine, rotated, total):
     rows, columns = values.shape
-    tile = 256
+    tile = 512
     row = lambda i: (i, 0)
     return pl.pallas_call(
         functools.partial(norm_rope_kernel, rotated, total),

time: 319 us -> 337 us (1.056)
  the two profiles are of different devices: /device:TPU:1 before, /device:TPU:2 now
where the time goes in v5:
time: 337 us; the launch traced here: 331 us
  waiting for transfers between devices  123 us (36%)
  matrix products  98.4 us (29%)
  starting transfers between devices  56.2 us (17%)
  Pallas kernels  19.3 us (6%)
  between operations  14.3 us (4%)
  other arithmetic  11.4 us (3%)
  local copies, waits for them, and re-layouts  8.49 us (3%)
    dot_general x40, matrix products, terms(): term = jnp.dot(piece, rows, preferred_element_type=jnp.float32)  98.4 us
    ppermute x15, waiting for transfers between devices, line_hops(): downs = [lax.ppermute(down, axis, downward) for down in downs]  87.4 us
    ppermute x15, starting transfers between devices, line_hops(): ups = [lax.ppermute(up, axis, upward) for up in ups]  35 us
    ppermute x15, waiting for transfers between devices, line_hops(): ups = [lax.ppermute(up, axis, upward) for up in ups]  23.5 us
    ppermute x15, starting transfers between devices, line_hops(): downs = [lax.ppermute(down, axis, downward) for down in downs]  19.3 us
    pallas_call x2, Pallas kernels, attend(): pl.pallas_call(functools.partial(attend_kernel, q_tile, row0), out_shape=...  16.2 us
    ppermute x1, waiting for transfers between devices, from_behind(): lax.ppermute(value, axis, [(source, source + steps) for source in range(f...  11.8 us
  transfers between devices with their start and end apart: 33, of which 15 were waited for; matrix products, arithmetic and copies ran while one was open for 32% of the time, Pallas kernels for 6%

profile of v5, /device:TPU:2, one launch (start us, length us, event | category | flops | bytes accessed | tf_op | source)
XLA Modules:
  0.0 330.8 jit_solution(1012693104486542307)
XLA Ops:
  6.5 3.6 %fusion.142 = (bf16[1344,2,256]{2,1,0:T(2,128)(2,1)S(1)}, bf16[1344,2,256]{2,1,0:T(2,128)(2,1)S(1)}) fusion(bf16[1344,2,512]{2,1,0:T(2,128)(2,1)} %param.6), kind=kLoop, calls=%fused_computation.161 | loop fusion | bytes 5505024 | tf_op jit(solution)/shard_map/slice | solution.py:213
  10.7 1.9 pad_maximum_fusion
  12.7 1.7 copy-done.4
  16.0 4.4 %collective-permute-start.2 = (bf16[1024,448]{0,1:T(8,128)(2,1)}, bf16[1024,448]{0,1:T(8,128)(2,1)}, u32[]{:S(2)}, u32[]{:S(2)}) collective-permute-start(bf16[1024,448]{0,1:T(8,128)(2,1)} %get-tuple-element.31), channel_id=1, source_target_pairs={{0,1},{1,2},{2,3},{4,5},{5,6},{6,7},{8,9},{9,10},{10,11},{12,13},{... | collective-permute-start | bytes 2752520 | tf_op jit(solution)/shard_map/ppermute | solution.py:159
  21.7 5.5 %collective-permute-start = (bf16[1024,448]{0,1:T(8,128)(2,1)}, bf16[1024,448]{0,1:T(8,128)(2,1)}, u32[]{:S(2)}, u32[]{:S(2)}) collective-permute-start(bf16[1024,448]{0,1:T(8,128)(2,1)} %get-tuple-element.30), channel_id=1, source_target_pairs={{0,1},{1,2},{2,3},{4,5},{5,6},{6,7},{8,9},{9,10},{10,11},{12,13},{... | collective-permute-start | bytes 2752520 | tf_op jit(solution)/shard_map/ppermute | solution.py:159
  29.8 10.8 %collective-permute-done.2 = bf16[1024,448]{0,1:T(8,128)(2,1)} collective-permute-done((bf16[1024,448]{0,1:T(8,128)(2,1)}, bf16[1024,448]{0,1:T(8,128)(2,1)}, u32[]{:S(2)}, u32[]{:S(2)}) %collective-permute-start.2) | collective-permute-done | bytes 917536 | tf_op jit(solution)/shard_map/ppermute | solution.py:159
  40.6 5.3 %collective-permute-start.4 = (bf16[1024,448]{0,1:T(8,128)(2,1)}, bf16[1024,448]{0,1:T(8,128)(2,1)}, u32[]{:S(2)}, u32[]{:S(2)}) collective-permute-start(bf16[1024,448]{0,1:T(8,128)(2,1)} %get-tuple-element.29), channel_id=1, source_target_pairs={{0,1},{1,2},{2,3},{4,5},{5,6},{6,7},{8,9},{9,10},{10,11},{12,13},{... | collective-permute-start | bytes 2752520 | tf_op jit(solution)/shard_map/ppermute | solution.py:159
  46.0 1.9 fusion.94
  50.9 9.3 %collective-permute-done = bf16[1024,448]{0,1:T(8,128)(2,1)} collective-permute-done((bf16[1024,448]{0,1:T(8,128)(2,1)}, bf16[1024,448]{0,1:T(8,128)(2,1)}, u32[]{:S(2)}, u32[]{:S(2)}) %collective-permute-start) | collective-permute-done | bytes 917536 | tf_op jit(solution)/shard_map/ppermute | solution.py:159
  61.5 4.1 %collective-permute-done.1 = bf16[1024,448]{0,1:T(8,128)(2,1)} collective-permute-done((bf16[1024,448]{0,1:T(8,128)(2,1)}, bf16[1024,448]{0,1:T(8,128)(2,1)}, u32[]{:S(2)}, u32[]{:S(2)}) %collective-permute-start.1) | collective-permute-done | bytes 917536 | tf_op jit(solution)/shard_map/ppermute | solution.py:160
  67.2 18.1 %collective-permute-done.5 = bf16[1024,448]{0,1:T(8,128)(2,1)} collective-permute-done((bf16[1024,448]{0,1:T(8,128)(2,1)}, bf16[1024,448]{0,1:T(8,128)(2,1)}, u32[]{:S(2)}, u32[]{:S(2)}) %collective-permute-start.5) | collective-permute-done | bytes 917536 | tf_op jit(solution)/shard_map/ppermute | solution.py:160
  86.5 1.8 collective-permute-start.10
  88.4 3.6 %fusion.50 = f32[512,1024]{0,1:T(8,128)} fusion(bf16[1024,448]{0,1:T(8,128)(2,1)} %collective-permute-done.5, bf16[5376,1024]{1,0:T(8,128)(2,1)} %all-gather.3.cloned.1.call-done, s32[]{:T(128)S(6)} %select_n.155), kind=kOutput, calls=%fused_computation.69 | convolution fusion | flops 469762048 | bytes 3473412 | tf_op jit(solution)/shard_map/dot_general | solution.py:175
  91.9 2.8 fusion.76
  94.7 3.5 %fusion.52 = f32[512,1024]{0,1:T(8,128)} fusion(bf16[1024,448]{0,1:T(8,128)(2,1)} %collective-permute-done.4, bf16[5376,1024]{1,0:T(8,128)(2,1)} %all-gather.3.cloned.1.call-done, s32[]{:T(128)S(6)} %select_n.154), kind=kOutput, calls=%fused_computation.71 | convolution fusion | flops 469762048 | bytes 3473412 | tf_op jit(solution)/shard_map/dot_general | solution.py:175
  98.3 2.4 fusion.78
  100.7 3.3 fusion.54
  104.0 3.3 fusion.80
  107.2 3.3 fusion.56
  110.5 3.3 fusion.82
  113.8 3.3 %fusion.58 = f32[512,1024]{0,1:T(8,128)} fusion(bf16[1024,448]{0,1:T(8,128)(2,1)} %collective-permute-done.1, bf16[5376,1024]{1,0:T(8,128)(2,1)S(1)} %copy-done.5, s32[]{:T(128)S(6)} %select_n.151), kind=kOutput, calls=%fused_computation.77 | convolution fusion | flops 469762048 | bytes 3473412 | tf_op jit(solution)/shard_map/dot_general | solution.py:175
  117.1 3.3 %fusion.84 = f32[512,1024]{0,1:T(8,128)} fusion(bf16[1024,448]{0,1:T(8,128)(2,1)} %collective-permute-done.1, bf16[5376,1024]{1,0:T(8,128)(2,1)S(1)} %copy-done.5, s32[]{:T(128)S(6)} %select_n.151), kind=kOutput, calls=%fused_computation.101 | convolution fusion | flops 469762048 | bytes 3473412 | tf_op jit(solution)/shard_map/dot_general | solution.py:175
  120.4 3.2 fusion.60
  123.7 3.3 %fusion.86 = f32[512,1024]{0,1:T(8,128)} fusion(bf16[1024,448]{0,1:T(8,128)(2,1)} %collective-permute-done, bf16[5376,1024]{1,0:T(8,128)(2,1)S(1)} %copy-done.5, s32[]{:T(128)S(6)} %select_n.150), kind=kOutput, calls=%fused_computation.103 | convolution fusion | flops 469762048 | bytes 3473412 | tf_op jit(solution)/shard_map/dot_general | solution.py:175
  127.0 2.1 fusion.62
  129.1 2.1 fusion.88
  131.2 2.1 fusion.64
  133.4 2.1 fusion.90
  135.5 2.1 fusion.66
  141.8 2.0 collective-permute-start.14
  143.8 2.0 fusion.46
  145.7 2.0 fusion.72
  147.7 2.1 fusion.92
  149.8 1.9 fusion.48
  151.8 2.0 fusion.74
  155.0 11.6 %collective-permute-done.11 = bf16[1024,448]{0,1:T(8,128)(2,1)S(1)} collective-permute-done((bf16[1024,448]{0,1:T(8,128)(2,1)}, bf16[1024,448]{0,1:T(8,128)(2,1)S(1)}, u32[]{:S(2)}, u32[]{:S(2)}) %collective-permute-start.11) | collective-permute-done | bytes 917536 | tf_op jit(solution)/shard_map/ppermute | solution.py:160
  168.4 8.2 %fusion.5 = f32[1024,512]{1,0:T(8,128)S(1)} fusion(f32[1024,512]{1,0:T(8,128)S(1)} %fusion.46, f32[1024,512]{1,0:T(8,128)S(1)} %fusion.48, f32[512,1024]{0,1:T(8,128)} %fusion.50, f32[512,1024]{0,1:T(8,128)} %fusion.52, f32[512,1024]{0,1:T(8,128)} %fusion.54, f32[512,1024]{0,1:T(8,128)} %fusion.56, f32[512,1024]{0,1:T(8,128)} %fusion.58, ...), kind=kOutput, calls=%fused_computation.15 | convolution fusion | flops 475987968 | bytes 27459588 | tf_op jit(solution)/shard_map/dot_general | solution.py:175
  176.6 7.1 %fusion.7 = f32[1024,512]{1,0:T(8,128)S(1)} fusion(f32[1024,512]{1,0:T(8,128)S(1)} %fusion.72, f32[1024,512]{1,0:T(8,128)S(1)} %fusion.74, f32[512,1024]{0,1:T(8,128)S(1)} %fusion.76, f32[512,1024]{0,1:T(8,128)S(1)} %fusion.78, f32[512,1024]{0,1:T(8,128)} %fusion.80, f32[512,1024]{0,1:T(8,128)} %fusion.82, f32[512,1024]{0,1:T(8,128)} %fusion.84, ...), kind=kOutput, calls=%fused_computation.18 | convolution fusion | flops 475987968 | bytes 27459588 | tf_op jit(solution)/shard_map/dot_general | solution.py:175
  186.5 1.9 fusion.38
  188.9 2.0 fusion.40
  191.3 14.8 %collective-permute-done.15 = bf16[1024,448]{0,1:T(8,128)(2,1)} collective-permute-done((bf16[1024,448]{0,1:T(8,128)(2,1)}, bf16[1024,448]{0,1:T(8,128)(2,1)}, u32[]{:S(2)}, u32[]{:S(2)}) %collective-permute-start.15) | collective-permute-done | bytes 917536 | tf_op jit(solution)/shard_map/ppermute | solution.py:160
  206.1 1.9 fusion.34
  208.5 2.0 fusion.36
  211.0 10.2 %collective-permute-done.17 = bf16[1024,448]{0,1:T(8,128)(2,1)S(1)} collective-permute-done((bf16[1024,448]{0,1:T(8,128)(2,1)S(1)}, bf16[1024,448]{0,1:T(8,128)(2,1)S(1)}, u32[]{:S(2)}, u32[]{:S(2)}) %collective-permute-start.17) | collective-permute-done | bytes 917536 | tf_op jit(solution)/shard_map/ppermute | solution.py:160
  222.0 1.8 add.347.x_ref
  223.8 3.1 shard_map.55
  226.9 1.9 collective-permute-start.18
  228.8 2.1 fusion.32
  231.4 11.8 %collective-permute-done.18 = bf16[1024,512]{1,0:T(8,128)(2,1)S(1)} collective-permute-done((bf16[1024,512]{1,0:T(8,128)(2,1)}, bf16[1024,512]{1,0:T(8,128)(2,1)S(1)}, u32[]{:S(2)}, u32[]{:S(2)}) %collective-permute-start.18) | collective-permute-done | bytes 1048608 | tf_op jit(solution)/shard_map/ppermute | solution.py:25
  243.3 8.1 %shard_map.56 = bf16[512,512]{1,0:T(8,128)(2,1)S(1)} custom-call(s32[1]{0:T(128)} %bitcast.base_ref, f32[1024,512]{1,0:T(8,128)S(1)} %add.344.q_ref, f32[1,128]{1,0:T(1,128)S(1)} %bitcast.37, f32[1024,128]{1,0:T(8,128)S(1)} %copy-done, f32[1024,128]{1,0:T(8,128)S(1)} %copy-done.1, bf16[2048,512]{1,0:T(8,128)(2,1)S(1)} %pad_maximum_fusion.2.k_ref.v_ref, ...), custom_call_target="tpu_custom_call" | custom-call | flops 1342177280 | bytes 5242880 | tf_op jit(solution)/shard_map/pallas_call | solution.py:129
  251.4 2.3 collective-permute-start.19
  255.0 8.1 %shard_map.57 = bf16[512,512]{1,0:T(8,128)(2,1)S(1)} custom-call(s32[1]{0:T(128)} %bitcast.base_ref, f32[1024,512]{1,0:T(8,128)S(1)} %add.344.q_ref, f32[1,128]{1,0:T(1,128)S(1)} %bitcast.38, f32[1024,128]{1,0:T(8,128)S(1)} %copy-done, f32[1024,128]{1,0:T(8,128)S(1)} %copy-done.1, bf16[2048,512]{1,0:T(8,128)(2,1)S(1)} %pad_maximum_fusion.2.k_ref.v_ref, ...), custom_call_target="tpu_custom_call" | custom-call | flops 1342177280 | bytes 5242880 | tf_op jit(solution)/shard_map/pallas_call | solution.py:129
  263.1 4.6 %collective-permute-start.25 = (bf16[512,512]{1,0:T(8,128)(2,1)S(1)}, bf16[512,512]{1,0:T(8,128)(2,1)S(1)}, u32[]{:S(2)}, u32[]{:S(2)}) collective-permute-start(bf16[512,512]{1,0:T(8,128)(2,1)S(1)} %shard_map.57), channel_id=1, source_target_pairs={{0,1},{1,2},{2,3},{4,5},{5,6},{6,7},{8,9},{9,10},{10,11},{12,13},{... | collective-permute-start | bytes 1572872 | tf_op jit(solution)/shard_map/ppermute | solution.py:159
  271.0 3.3 %collective-permute-done.25 = bf16[512,512]{1,0:T(8,128)(2,1)S(1)} collective-permute-done((bf16[512,512]{1,0:T(8,128)(2,1)S(1)}, bf16[512,512]{1,0:T(8,128)(2,1)S(1)}, u32[]{:S(2)}, u32[]{:S(2)}) %collective-permute-start.25) | collective-permute-done | bytes 524320 | tf_op jit(solution)/shard_map/ppermute | solution.py:159
  274.4 1.6 collective-permute-start.27
  276.0 2.6 fusion.18
  278.6 2.3 fusion.16
  281.8 2.7 collective-permute-done.26
  289.3 6.5 %collective-permute-done.22 = bf16[512,512]{1,0:T(8,128)(2,1)} collective-permute-done((bf16[512,512]{1,0:T(8,128)(2,1)S(1)}, bf16[512,512]{1,0:T(8,128)(2,1)}, u32[]{:S(2)}, u32[]{:S(2)}) %collective-permute-start.22) | collective-permute-done | bytes 524320 | tf_op jit(solution)/shard_map/ppermute | solution.py:160
  297.8 9.1 %collective-permute-done.28 = bf16[512,512]{1,0:T(8,128)(2,1)S(1)} collective-permute-done((bf16[512,512]{1,0:T(8,128)(2,1)S(1)}, bf16[512,512]{1,0:T(8,128)(2,1)S(1)}, u32[]{:S(2)}, u32[]{:S(2)}) %collective-permute-start.28) | collective-permute-done | bytes 524320 | tf_op jit(solution)/shard_map/ppermute | solution.py:160
  308.2 2.0 convolution_add_fusion.4
  311.2 4.2 %collective-permute-done.24 = bf16[512,512]{1,0:T(8,128)(2,1)S(1)} collective-permute-done((bf16[512,512]{1,0:T(8,128)(2,1)}, bf16[512,512]{1,0:T(8,128)(2,1)S(1)}, u32[]{:S(2)}, u32[]{:S(2)}) %collective-permute-start.24) | collective-permute-done | bytes 524320 | tf_op jit(solution)/shard_map/ppermute | solution.py:160
  316.3 4.6 %collective-permute-done.30 = bf16[512,512]{1,0:T(8,128)(2,1)S(1)} collective-permute-done((bf16[512,512]{1,0:T(8,128)(2,1)S(1)}, bf16[512,512]{1,0:T(8,128)(2,1)S(1)}, u32[]{:S(2)}, u32[]{:S(2)}) %collective-permute-start.30) | collective-permute-done | bytes 524320 | tf_op jit(solution)/shard_map/ppermute | solution.py:160
  321.9 1.9 pad_maximum_fusion.1
  (86 shorter events, 42.9 us)
Async XLA Ops:
  6.5 81.8 %all-gather.3.cloned.1.call-start = ((), (), s32[]{:S(2)}) async-start(), calls=%async_computation | async-start | bytes 13762560 | tf_op jit(solution)/shard_map/all_gather | solution.py:218
  12.7 1.8 copy-start.4
  12.7 263.3 %all-gather.5.cloned.1.call-start = ((), (), s32[]{:S(2)}) async-start(), calls=%async_computation.1 | async-start | bytes 6881280 | tf_op jit(solution)/shard_map/all_gather | solution.py:210
  16.0 24.5 %collective-permute-start.2 = (bf16[1024,448]{0,1:T(8,128)(2,1)}, bf16[1024,448]{0,1:T(8,128)(2,1)}, u32[]{:S(2)}, u32[]{:S(2)}) collective-permute-start(bf16[1024,448]{0,1:T(8,128)(2,1)} %get-tuple-element.31), channel_id=1, source_target_pairs={{0,1},{1,2},{2,3},{4,5},{5,6},{6,7},{8,9},{9,10},{10,11},{12,13},{... | collective-permute-start | bytes 2752520 | tf_op jit(solution)/shard_map/ppermute | solution.py:159
  20.4 28.8 %collective-permute-start.3 = (bf16[1024,448]{0,1:T(8,128)(2,1)}, bf16[1024,448]{0,1:T(8,128)(2,1)}, u32[]{:S(2)}, u32[]{:S(2)}) collective-permute-start(bf16[1024,448]{0,1:T(8,128)(2,1)} %get-tuple-element.31), channel_id=1, source_target_pairs={{1,0},{2,1},{3,2},{5,4},{6,5},{7,6},{9,8},{10,9},{11,10},{13,12},{... | collective-permute-start | bytes 2752520 | tf_op jit(solution)/shard_map/ppermute | solution.py:160
  21.7 38.5 %collective-permute-start = (bf16[1024,448]{0,1:T(8,128)(2,1)}, bf16[1024,448]{0,1:T(8,128)(2,1)}, u32[]{:S(2)}, u32[]{:S(2)}) collective-permute-start(bf16[1024,448]{0,1:T(8,128)(2,1)} %get-tuple-element.30), channel_id=1, source_target_pairs={{0,1},{1,2},{2,3},{4,5},{5,6},{6,7},{8,9},{9,10},{10,11},{12,13},{... | collective-permute-start | bytes 2752520 | tf_op jit(solution)/shard_map/ppermute | solution.py:159
  27.2 38.4 %collective-permute-start.1 = (bf16[1024,448]{0,1:T(8,128)(2,1)}, bf16[1024,448]{0,1:T(8,128)(2,1)}, u32[]{:S(2)}, u32[]{:S(2)}) collective-permute-start(bf16[1024,448]{0,1:T(8,128)(2,1)} %get-tuple-element.30), channel_id=1, source_target_pairs={{1,0},{2,1},{3,2},{5,4},{6,5},{7,6},{9,8},{10,9},{11,10},{13,12},{... | collective-permute-start | bytes 2752520 | tf_op jit(solution)/shard_map/ppermute | solution.py:160
  28.5 56.7 %collective-permute-start.5 = (bf16[1024,448]{0,1:T(8,128)(2,1)}, bf16[1024,448]{0,1:T(8,128)(2,1)}, u32[]{:S(2)}, u32[]{:S(2)}) collective-permute-start(bf16[1024,448]{0,1:T(8,128)(2,1)} %get-tuple-element.29), channel_id=1, source_target_pairs={{1,0},{2,1},{3,2},{5,4},{6,5},{7,6},{9,8},{10,9},{11,10},{13,12},{... | collective-permute-start | bytes 2752520 | tf_op jit(solution)/shard_map/ppermute | solution.py:160
  40.6 46.0 %collective-permute-start.4 = (bf16[1024,448]{0,1:T(8,128)(2,1)}, bf16[1024,448]{0,1:T(8,128)(2,1)}, u32[]{:S(2)}, u32[]{:S(2)}) collective-permute-start(bf16[1024,448]{0,1:T(8,128)(2,1)} %get-tuple-element.29), channel_id=1, source_target_pairs={{0,1},{1,2},{2,3},{4,5},{5,6},{6,7},{8,9},{9,10},{10,11},{12,13},{... | collective-permute-start | bytes 2752520 | tf_op jit(solution)/shard_map/ppermute | solution.py:159
  49.3 88.3 %collective-permute-start.8 = (bf16[1024,448]{0,1:T(8,128)(2,1)}, bf16[1024,448]{0,1:T(8,128)(2,1)}, u32[]{:S(2)}, u32[]{:S(2)}) collective-permute-start(bf16[1024,448]{0,1:T(8,128)(2,1)} %collective-permute-done.2), channel_id=1, source_target_pairs={{1,2},{2,3},{5,6},{6,7},{9,10},{10,11},{13,14},{14,15},{17,18},{18... | collective-permute-start | bytes 2752520 | tf_op jit(solution)/shard_map/ppermute | solution.py:159
  60.2 81.5 %collective-permute-start.9 = (bf16[1024,448]{0,1:T(8,128)(2,1)}, bf16[1024,448]{0,1:T(8,128)(2,1)}, u32[]{:S(2)}, u32[]{:S(2)}) collective-permute-start(bf16[1024,448]{0,1:T(8,128)(2,1)} %collective-permute-done.3), channel_id=1, source_target_pairs={{1,0},{2,1},{5,4},{6,5},{9,8},{10,9},{13,12},{14,13},{17,16},{18,1... | collective-permute-start | bytes 2752520 | tf_op jit(solution)/shard_map/ppermute | solution.py:160
  65.6 73.3 %collective-permute-start.6 = (bf16[1024,448]{0,1:T(8,128)(2,1)}, bf16[1024,448]{0,1:T(8,128)(2,1)}, u32[]{:S(2)}, u32[]{:S(2)}) collective-permute-start(bf16[1024,448]{0,1:T(8,128)(2,1)} %collective-permute-done), channel_id=1, source_target_pairs={{1,2},{2,3},{5,6},{6,7},{9,10},{10,11},{13,14},{14,15},{17,18},{18... | collective-permute-start | bytes 2752520 | tf_op jit(solution)/shard_map/ppermute | solution.py:159
  85.2 55.2 %collective-permute-start.7 = (bf16[1024,448]{0,1:T(8,128)(2,1)}, bf16[1024,448]{0,1:T(8,128)(2,1)}, u32[]{:S(2)}, u32[]{:S(2)}) collective-permute-start(bf16[1024,448]{0,1:T(8,128)(2,1)} %collective-permute-done.1), channel_id=1, source_target_pairs={{1,0},{2,1},{5,4},{6,5},{9,8},{10,9},{13,12},{14,13},{17,16},{18,1... | collective-permute-start | bytes 2752520 | tf_op jit(solution)/shard_map/ppermute | solution.py:160
  86.5 67.2 %collective-permute-start.10 = (bf16[1024,448]{0,1:T(8,128)(2,1)}, bf16[1024,448]{0,1:T(8,128)(2,1)}, u32[]{:S(2)}, u32[]{:S(2)}) collective-permute-start(bf16[1024,448]{0,1:T(8,128)(2,1)} %collective-permute-done.4), channel_id=1, source_target_pairs={{1,2},{2,3},{5,6},{6,7},{9,10},{10,11},{13,14},{14,15},{17,18},{18... | collective-permute-start | bytes 2752520 | tf_op jit(solution)/shard_map/ppermute | solution.py:159
  88.3 12.3 %copy-start.5 = (bf16[5376,1024]{1,0:T(8,128)(2,1)S(1)}, bf16[5376,1024]{1,0:T(8,128)(2,1)}, u32[]{:S(2)}) copy-start(bf16[5376,1024]{1,0:T(8,128)(2,1)} %all-gather.3.cloned.1.call-done) | copy-start | bytes 33030148
  137.6 29.1 %collective-permute-start.11 = (bf16[1024,448]{0,1:T(8,128)(2,1)}, bf16[1024,448]{0,1:T(8,128)(2,1)S(1)}, u32[]{:S(2)}, u32[]{:S(2)}) collective-permute-start(bf16[1024,448]{0,1:T(8,128)(2,1)} %collective-permute-done.5), channel_id=1, source_target_pairs={{1,0},{2,1},{5,4},{6,5},{9,8},{10,9},{13,12},{14,13},{17,16},{18,1... | collective-permute-start | bytes 2752520 | tf_op jit(solution)/shard_map/ppermute | solution.py:160
  138.9 44.8 %collective-permute-start.12 = (bf16[1024,448]{0,1:T(8,128)(2,1)}, bf16[1024,448]{0,1:T(8,128)(2,1)}, u32[]{:S(2)}, u32[]{:S(2)}) collective-permute-start(bf16[1024,448]{0,1:T(8,128)(2,1)} %collective-permute-done.6), channel_id=1, source_target_pairs={{2,3},{6,7},{10,11},{14,15},{18,19},{22,23},{26,27},{30,31}} | collective-permute-start | bytes 2752520 | tf_op jit(solution)/shard_map/ppermute | solution.py:159
  140.5 46.0 %collective-permute-start.13 = (bf16[1024,448]{0,1:T(8,128)(2,1)}, bf16[1024,448]{0,1:T(8,128)(2,1)}, u32[]{:S(2)}, u32[]{:S(2)}) collective-permute-start(bf16[1024,448]{0,1:T(8,128)(2,1)} %collective-permute-done.7), channel_id=1, source_target_pairs={{1,0},{5,4},{9,8},{13,12},{17,16},{21,20},{25,24},{29,28}} | collective-permute-start | bytes 2752520 | tf_op jit(solution)/shard_map/ppermute | solution.py:160
  141.8 49.6 %collective-permute-start.14 = (bf16[1024,448]{0,1:T(8,128)(2,1)}, bf16[1024,448]{0,1:T(8,128)(2,1)}, u32[]{:S(2)}, u32[]{:S(2)}) collective-permute-start(bf16[1024,448]{0,1:T(8,128)(2,1)} %collective-permute-done.8), channel_id=1, source_target_pairs={{2,3},{6,7},{10,11},{14,15},{18,19},{22,23},{26,27},{30,31}} | collective-permute-start | bytes 2752520 | tf_op jit(solution)/shard_map/ppermute | solution.py:159
  153.7 52.4 %collective-permute-start.15 = (bf16[1024,448]{0,1:T(8,128)(2,1)}, bf16[1024,448]{0,1:T(8,128)(2,1)}, u32[]{:S(2)}, u32[]{:S(2)}) collective-permute-start(bf16[1024,448]{0,1:T(8,128)(2,1)} %collective-permute-done.9), channel_id=1, source_target_pairs={{1,0},{5,4},{9,8},{13,12},{17,16},{21,20},{25,24},{29,28}} | collective-permute-start | bytes 2752520 | tf_op jit(solution)/shard_map/ppermute | solution.py:160
  166.7 1.0 copy-start.9
  167.7 43.3 %collective-permute-start.16 = (bf16[1024,448]{0,1:T(8,128)(2,1)}, bf16[1024,448]{0,1:T(8,128)(2,1)S(1)}, u32[]{:S(2)}, u32[]{:S(2)}) collective-permute-start(bf16[1024,448]{0,1:T(8,128)(2,1)} %collective-permute-done.10), channel_id=1, source_target_pairs={{2,3},{6,7},{10,11},{14,15},{18,19},{22,23},{26,27},{30,31}} | collective-permute-start | bytes 2752520 | tf_op jit(solution)/shard_map/ppermute | solution.py:159
  176.6 7.1 %copy-start.10 = (bf16[1024,448]{0,1:T(8,128)(2,1)S(1)}, bf16[1024,448]{0,1:T(8,128)(2,1)}, u32[]{:S(2)}) copy-start(bf16[1024,448]{0,1:T(8,128)(2,1)} %copy-done.9) | copy-start | bytes 2752516
  183.7 37.5 %collective-permute-start.17 = (bf16[1024,448]{0,1:T(8,128)(2,1)S(1)}, bf16[1024,448]{0,1:T(8,128)(2,1)S(1)}, u32[]{:S(2)}, u32[]{:S(2)}) collective-permute-start(bf16[1024,448]{0,1:T(8,128)(2,1)S(1)} %copy-done.10), channel_id=1, source_target_pairs={{1,0},{5,4},{9,8},{13,12},{17,16},{21,20},{25,24},{29,28}} | collective-permute-start | bytes 2752520 | tf_op jit(solution)/shard_map/ppermute | solution.py:160
  211.0 12.8 %copy-start.7 = (bf16[1024,448]{0,1:T(8,128)(2,1)}, bf16[1024,448]{0,1:T(8,128)(2,1)S(1)}, u32[]{:S(2)}) copy-start(bf16[1024,448]{0,1:T(8,128)(2,1)S(1)} %collective-permute-done.16) | copy-start | bytes 2752516
  221.2 2.6 copy-start.8
  226.9 16.3 %collective-permute-start.18 = (bf16[1024,512]{1,0:T(8,128)(2,1)}, bf16[1024,512]{1,0:T(8,128)(2,1)S(1)}, u32[]{:S(2)}, u32[]{:S(2)}) collective-permute-start(bf16[1024,512]{1,0:T(8,128)(2,1)} %shard_map.55), channel_id=1, source_target_pairs={{0,4},{4,8},{8,12},{1,5},{5,9},{9,13},{2,6},{6,10},{10,14},{3,7},{... | collective-permute-start | bytes 3145736 | tf_op jit(solution)/shard_map/ppermute | solution.py:25
  230.8 12.3 %copy-start.6 = (bf16[1024,512]{1,0:T(8,128)(2,1)S(1)}, bf16[1024,512]{1,0:T(8,128)(2,1)}, u32[]{:S(2)}) copy-start(bf16[1024,512]{1,0:T(8,128)(2,1)} %shard_map.55) | copy-start | bytes 3145732
  231.3 12.0 %copy-start = (f32[1024,128]{1,0:T(8,128)S(1)}, f32[1024,128]{1,0:T(8,128)}, u32[]{:S(2)}) copy-start(f32[1024,128]{1,0:T(8,128)} %get-tuple-element.37.cos_ref) | copy-start | bytes 1572868
  231.4 12.0 %copy-start.1 = (f32[1024,128]{1,0:T(8,128)S(1)}, f32[1024,128]{1,0:T(8,128)}, u32[]{:S(2)}) copy-start(f32[1024,128]{1,0:T(8,128)} %get-tuple-element.38.sin_ref) | copy-start | bytes 1572868
  231.4 12.0 %copy-start.2 = (f32[128]{0:T(128)S(1)}, f32[128]{0:T(128)}, u32[]{:S(2)}) copy-start(f32[128]{0:T(128)} %param.8) | copy-start | bytes 1540
  251.4 17.6 %collective-permute-start.19 = (bf16[512,512]{1,0:T(8,128)(2,1)S(1)}, bf16[512,512]{1,0:T(8,128)(2,1)}, u32[]{:S(2)}, u32[]{:S(2)}) collective-permute-start(bf16[512,512]{1,0:T(8,128)(2,1)S(1)} %shard_map.56), channel_id=1, source_target_pairs={{0,1},{1,2},{2,3},{4,5},{5,6},{6,7},{8,9},{9,10},{10,11},{12,13},{... | collective-permute-start | bytes 1572872 | tf_op jit(solution)/shard_map/ppermute | solution.py:159
  253.7 16.0 %collective-permute-start.20 = (bf16[512,512]{1,0:T(8,128)(2,1)S(1)}, bf16[512,512]{1,0:T(8,128)(2,1)S(1)}, u32[]{:S(2)}, u32[]{:S(2)}) collective-permute-start(bf16[512,512]{1,0:T(8,128)(2,1)S(1)} %shard_map.56), channel_id=1, source_target_pairs={{1,0},{2,1},{3,2},{5,4},{6,5},{7,6},{9,8},{10,9},{11,10},{13,12},{... | collective-permute-start | bytes 1572872 | tf_op jit(solution)/shard_map/ppermute | solution.py:160
  263.1 11.2 %collective-permute-start.25 = (bf16[512,512]{1,0:T(8,128)(2,1)S(1)}, bf16[512,512]{1,0:T(8,128)(2,1)S(1)}, u32[]{:S(2)}, u32[]{:S(2)}) collective-permute-start(bf16[512,512]{1,0:T(8,128)(2,1)S(1)} %shard_map.57), channel_id=1, source_target_pairs={{0,1},{1,2},{2,3},{4,5},{5,6},{6,7},{8,9},{9,10},{10,11},{12,13},{... | collective-permute-start | bytes 1572872 | tf_op jit(solution)/shard_map/ppermute | solution.py:159
  267.7 16.8 %collective-permute-start.26 = (bf16[512,512]{1,0:T(8,128)(2,1)S(1)}, bf16[512,512]{1,0:T(8,128)(2,1)S(1)}, u32[]{:S(2)}, u32[]{:S(2)}) collective-permute-start(bf16[512,512]{1,0:T(8,128)(2,1)S(1)} %shard_map.57), channel_id=1, source_target_pairs={{1,0},{2,1},{3,2},{5,4},{6,5},{7,6},{9,8},{10,9},{11,10},{13,12},{... | collective-permute-start | bytes 1572872 | tf_op jit(solution)/shard_map/ppermute | solution.py:160
  269.0 19.5 %collective-permute-start.21 = (bf16[512,512]{1,0:T(8,128)(2,1)}, bf16[512,512]{1,0:T(8,128)(2,1)S(1)}, u32[]{:S(2)}, u32[]{:S(2)}) collective-permute-start(bf16[512,512]{1,0:T(8,128)(2,1)} %collective-permute-done.19), channel_id=1, source_target_pairs={{1,2},{2,3},{5,6},{6,7},{9,10},{10,11},{13,14},{14,15},{17,18},{18... | collective-permute-start | bytes 1572872 | tf_op jit(solution)/shard_map/ppermute | solution.py:159
  269.7 26.1 %collective-permute-start.22 = (bf16[512,512]{1,0:T(8,128)(2,1)S(1)}, bf16[512,512]{1,0:T(8,128)(2,1)}, u32[]{:S(2)}, u32[]{:S(2)}) collective-permute-start(bf16[512,512]{1,0:T(8,128)(2,1)S(1)} %collective-permute-done.20), channel_id=1, source_target_pairs={{1,0},{2,1},{5,4},{6,5},{9,8},{10,9},{13,12},{14,13},{17,16},{18,1... | collective-permute-start | bytes 1572872 | tf_op jit(solution)/shard_map/ppermute | solution.py:160
  274.4 22.7 %collective-permute-start.27 = (bf16[512,512]{1,0:T(8,128)(2,1)S(1)}, bf16[512,512]{1,0:T(8,128)(2,1)}, u32[]{:S(2)}, u32[]{:S(2)}) collective-permute-start(bf16[512,512]{1,0:T(8,128)(2,1)S(1)} %collective-permute-done.25), channel_id=1, source_target_pairs={{1,2},{2,3},{5,6},{6,7},{9,10},{10,11},{13,14},{14,15},{17,18},{18... | collective-permute-start | bytes 1572872 | tf_op jit(solution)/shard_map/ppermute | solution.py:159
  276.0 4.9 %copy-start.3 = (bf16[2048,1344]{0,1:T(8,128)(2,1)S(1)}, bf16[2048,1344]{0,1:T(8,128)(2,1)}, u32[]{:S(2)}) copy-start(bf16[2048,1344]{0,1:T(8,128)(2,1)} %all-gather.5.cloned.1.call-done) | copy-start | bytes 16515076
  284.5 22.5 %collective-permute-start.28 = (bf16[512,512]{1,0:T(8,128)(2,1)S(1)}, bf16[512,512]{1,0:T(8,128)(2,1)S(1)}, u32[]{:S(2)}, u32[]{:S(2)}) collective-permute-start(bf16[512,512]{1,0:T(8,128)(2,1)S(1)} %collective-permute-done.26), channel_id=1, source_target_pairs={{1,0},{2,1},{5,4},{6,5},{9,8},{10,9},{13,12},{14,13},{17,16},{18,1... | collective-permute-start | bytes 1572872 | tf_op jit(solution)/shard_map/ppermute | solution.py:160
  288.6 22.6 %collective-permute-start.23 = (bf16[512,512]{1,0:T(8,128)(2,1)S(1)}, bf16[512,512]{1,0:T(8,128)(2,1)S(1)}, u32[]{:S(2)}, u32[]{:S(2)}) collective-permute-start(bf16[512,512]{1,0:T(8,128)(2,1)S(1)} %collective-permute-done.21), channel_id=1, source_target_pairs={{2,3},{6,7},{10,11},{14,15},{18,19},{22,23},{26,27},{30,31}} | collective-permute-start | bytes 1572872 | tf_op jit(solution)/shard_map/ppermute | solution.py:159
  295.8 19.5 %collective-permute-start.24 = (bf16[512,512]{1,0:T(8,128)(2,1)}, bf16[512,512]{1,0:T(8,128)(2,1)S(1)}, u32[]{:S(2)}, u32[]{:S(2)}) collective-permute-start(bf16[512,512]{1,0:T(8,128)(2,1)} %collective-permute-done.22), channel_id=1, source_target_pairs={{1,0},{5,4},{9,8},{13,12},{17,16},{21,20},{25,24},{29,28}} | collective-permute-start | bytes 1572872 | tf_op jit(solution)/shard_map/ppermute | solution.py:160
  297.1 19.2 %collective-permute-start.29 = (bf16[512,512]{1,0:T(8,128)(2,1)}, bf16[512,512]{1,0:T(8,128)(2,1)S(1)}, u32[]{:S(2)}, u32[]{:S(2)}) collective-permute-start(bf16[512,512]{1,0:T(8,128)(2,1)} %collective-permute-done.27), channel_id=1, source_target_pairs={{2,3},{6,7},{10,11},{14,15},{18,19},{22,23},{26,27},{30,31}} | collective-permute-start | bytes 1572872 | tf_op jit(solution)/shard_map/ppermute | solution.py:159
  306.9 14.0 %collective-permute-start.30 = (bf16[512,512]{1,0:T(8,128)(2,1)S(1)}, bf16[512,512]{1,0:T(8,128)(2,1)S(1)}, u32[]{:S(2)}, u32[]{:S(2)}) collective-permute-start(bf16[512,512]{1,0:T(8,128)(2,1)S(1)} %collective-permute-done.28), channel_id=1, source_target_pairs={{1,0},{5,4},{9,8},{13,12},{17,16},{21,20},{25,24},{29,28}} | collective-permute-start | bytes 1572872 | tf_op jit(solution)/shard_map/ppermute | solution.py:160
Sparse Core Ops, SparseCore 0:
  12.8 73.2 all-gather.2
  87.7 41.9 all-gather.4
